TPU v7x, 32 devices: a whole 2x2x4 slice. The times are simulated.
32 devices in a mesh: groups: 2 (over y), hidden: 4 (over z), width: 4 (over x, core).
Axes of the slice: x: 2, y: 2, z: 4, core: 2. Of those that a mesh axis runs over, the one named last changes fastest.
Arguments:
- tokens: bfloat16 [64, 12288], P(('groups', 'hidden'), 'width'), parts along dimension 0, may hold values from -6 to 6
- w_in: bfloat16 [12288, 24576], P('width', 'hidden'), may hold values from -0.0546875 to 0.0546875
- w_out: bfloat16 [24576, 12288], P('hidden', 'width'), may hold values from -0.0546875 to 0.0546875
Outputs:
- result_state: bfloat16 [64, 12288], P(('groups', 'hidden'), 'width'), parts along dimension 0
There are 2 independent parts, one for each index of `groups`. A program takes and returns all parts, laid end to end along the dimension named above; an argument that names none is the same for every part. Nothing has to cross between parts.
All inputs are finite; a program needn't handle non-finite values.
Results may differ from a plain program's by a relative error of at most 0.018.
Values may be sent and summed in bfloat16 or wider, within the bound.
No kernel may reach another device: no remote copies, remote signals or barrier semaphores. Data moves between devices by JAX's collectives and lax.ppermute only.
A program may use at most 192 MiB of HBM per device.

v0:
```python
import jax
import jax.numpy as jnp
from jax import lax
from jax.sharding import PartitionSpec as P

STEPS = 2


def local(tokens, w_in, w_out):
    row_dev = tokens.shape[0]
    where = lax.axis_index("hidden")
    full = lax.all_gather(tokens, "hidden", axis=0, tiled=True)
    latest = tokens
    for step in range(STEPS):
        pre = jnp.dot(full, w_in, preferred_element_type=jnp.float32)
        summed = lax.psum(pre.astype(jnp.bfloat16), "width").astype(jnp.float32)
        activ = jax.nn.gelu(summed, approximate=True).astype(jnp.bfloat16)
        mine_sum = lax.psum_scatter(
            jnp.dot(activ, w_out, preferred_element_type=jnp.float32).astype(jnp.bfloat16),
            "hidden",
            scatter_dimension=0,
            tiled=True,
        ).astype(jnp.float32)
        mine_old = lax.dynamic_slice_in_dim(full, where * row_dev, row_dev, 0)
        latest = (mine_old.astype(jnp.float32) + mine_sum).astype(jnp.bfloat16)
        if step + 1 < STEPS:
            full = lax.all_gather(latest, "hidden", axis=0, tiled=True)
    return latest


def solution(mesh):
    placed = (P(("groups", "hidden"), "width"), P("width", "hidden"), P("hidden", "width"))
    return jax.shard_map(
        local,
        mesh=mesh,
        in_specs=placed,
        out_specs=P(("groups", "hidden"), "width"),
        check_vma=False,
    )
```

profile of v0, /device:TPU:0, one launch (start us, length us, event | category | flops | bytes accessed | tf_op | source)
XLA Modules:
  0.0 212.6 jit_solution(4902715175887616192)
XLA Ops:
  6.5 0.0 all-reduce.3.cloned.1.call-start
  6.5 15.7 %all_gather.6 = bf16[32,3072]{1,0:T(8,128)(2,1)S(1)} all-gather(bf16[8,3072]{1,0:T(8,128)(2,1)} %param.3), channel_id=1, replica_groups=mesh['groups'=2,'hidden'=4,'width'=4] {'hidden'}, dimensions={0}, use_global_device_ids=true | all-gather | bytes 245760 | tf_op jit(solution)/shard_map/all_gather | solution.py:12
  22.2 15.9 %convolution_convert_fusion.1 = bf16[32,6144]{1,0:T(8,128)(2,1)} fusion(bf16[32,3072]{1,0:T(8,128)(2,1)S(1)} %all_gather.6, bf16[3072,6144]{1,0:T(8,128)(2,1)} %param.4), kind=kOutput, calls=%fused_computation.1 | convolution fusion | flops 1208156160 | bytes 38338560 | tf_op jit(solution)/shard_map/dot_general | solution.py:15
  38.1 0.0 all-reduce.3.cloned.1.call-update
  38.1 0.0 reduce-scatter.3.cloned.1.call-start
  38.1 34.0 %all-reduce.3.cloned.1.call-done = bf16[32,6144]{1,0:T(8,128)(2,1)} async-done(((bf16[32,6144]{1,0:T(8,128)(2,1)}), bf16[32,6144]{1,0:T(8,128)(2,1)}) %all-reduce.3.cloned.1.call-update) | async-done | bytes 393232 | tf_op jit(solution)/shard_map/psum | solution.py:16
  72.1 15.9 %convolution_convert_fusion.3 = bf16[32,3072]{1,0:T(8,128)(2,1)} fusion(bf16[6144,3072]{1,0:T(8,128)(2,1)} %param.5, bf16[32,6144]{1,0:T(8,128)(2,1)} %all-reduce.3.cloned.1.call-done), kind=kOutput, calls=%fused_computation.3 | convolution fusion | flops 1210023936 | bytes 38338560 | tf_op jit(solution)/shard_map/dot_general | solution.py:19
  88.0 0.0 reduce-scatter.3.cloned.1.call-update
  88.0 0.0 all-reduce.5.cloned.1.call-start
  88.1 19.5 %reduce-scatter.3.cloned.1.call-done = bf16[8,3072]{1,0:T(8,128)(2,1)} async-done(((bf16[32,3072]{1,0:T(8,128)(2,1)}), bf16[8,3072]{1,0:T(8,128)(2,1)}) %reduce-scatter.3.cloned.1.call-update) | async-done | bytes 49168 | tf_op jit(solution)/shard_map/reduce_scatter | solution.py:18
  107.5 0.8 add_convert_fusion.1
  108.3 13.6 %all_gather.7 = bf16[32,3072]{1,0:T(8,128)(2,1)S(1)} all-gather(bf16[8,3072]{1,0:T(8,128)(2,1)S(1)} %add_convert_fusion.1), channel_id=1, replica_groups=mesh['groups'=2,'hidden'=4,'width'=4] {'hidden'}, dimensions={0}, use_global_device_ids=true | all-gather | bytes 245760 | tf_op jit(solution)/shard_map/all_gather | solution.py:27
  121.9 15.9 %convolution_convert_fusion = bf16[32,6144]{1,0:T(8,128)(2,1)} fusion(bf16[32,3072]{1,0:T(8,128)(2,1)S(1)} %all_gather.7, bf16[3072,6144]{1,0:T(8,128)(2,1)} %param.4), kind=kOutput, calls=%fused_computation | convolution fusion | flops 1208156160 | bytes 38338560 | tf_op jit(solution)/shard_map/dot_general | solution.py:15
  137.8 0.0 all-reduce.5.cloned.1.call-update
  137.8 0.0 reduce-scatter.5.cloned.1.call-start
  137.9 31.3 %all-reduce.5.cloned.1.call-done = bf16[32,6144]{1,0:T(8,128)(2,1)} async-done(((bf16[32,6144]{1,0:T(8,128)(2,1)}), bf16[32,6144]{1,0:T(8,128)(2,1)}) %all-reduce.5.cloned.1.call-update) | async-done | bytes 393232 | tf_op jit(solution)/shard_map/psum | solution.py:16
  169.2 15.9 %convolution_convert_fusion.2 = bf16[32,3072]{1,0:T(8,128)(2,1)} fusion(bf16[6144,3072]{1,0:T(8,128)(2,1)} %param.5, bf16[32,6144]{1,0:T(8,128)(2,1)} %all-reduce.5.cloned.1.call-done), kind=kOutput, calls=%fused_computation.2 | convolution fusion | flops 1210023936 | bytes 38338560 | tf_op jit(solution)/shard_map/dot_general | solution.py:19
  185.1 0.0 reduce-scatter.5.cloned.1.call-update
  185.1 19.5 %reduce-scatter.5.cloned.1.call-done = bf16[8,3072]{1,0:T(8,128)(2,1)} async-done(((bf16[32,3072]{1,0:T(8,128)(2,1)}), bf16[8,3072]{1,0:T(8,128)(2,1)}) %reduce-scatter.5.cloned.1.call-update) | async-done | bytes 49168 | tf_op jit(solution)/shard_map/reduce_scatter | solution.py:18
  204.6 1.4 add_convert_fusion
Async XLA Ops:
  6.5 65.6 %all-reduce.3.cloned.1.call-start = ((), (), s32[]{:S(2)}) async-start(), calls=%async_computation.2 | async-start | bytes 786432 | tf_op jit(solution)/shard_map/psum | solution.py:16
  38.1 69.4 %reduce-scatter.3.cloned.1.call-start = ((), (), s32[]{:S(2)}) async-start(), calls=%async_computation.3 | async-start | bytes 245760 | tf_op jit(solution)/shard_map/reduce_scatter | solution.py:18
  88.0 81.2 %all-reduce.5.cloned.1.call-start = ((), (), s32[]{:S(2)}) async-start(), calls=%async_computation.4 | async-start | bytes 786432 | tf_op jit(solution)/shard_map/psum | solution.py:16
  137.8 66.8 %reduce-scatter.5.cloned.1.call-start = ((), (), s32[]{:S(2)}) async-start(), calls=%async_computation.5 | async-start | bytes 245760 | tf_op jit(solution)/shard_map/reduce_scatter | solution.py:18
Sparse Core Ops, SparseCore 0:
  38.2 33.8 all-reduce.2
  88.1 19.3 reduce-scatter.2
  137.9 31.2 all-reduce.4
  185.2 19.3 reduce-scatter.4
where the time goes:
time: 213 us
  waiting for transfers between devices  104 us (49%)
  matrix products  63.5 us (30%)
  blocking collectives  29.2 us (14%)
  between operations  13.1 us (6%)
  other arithmetic  2.24 us (1%)
    psum x2, waiting for transfers between devices, local(): summed = lax.psum(pre.astype(jnp.bfloat16), 'width').astype(jnp.float32)  65.3 us
    reduce_scatter x2, waiting for transfers between devices, local(): lax.psum_scatter(jnp.dot(activ, w_out, preferred_element_type=jnp.float32...  39 us
    dot_general x2, matrix products, local(): jnp.dot(activ, w_out, preferred_element_type=jnp.float32)  31.8 us
    dot_general x2, matrix products, local(): pre = jnp.dot(full, w_in, preferred_element_type=jnp.float32)  31.7 us
    all_gather x1, blocking collectives, local(): full = lax.all_gather(tokens, 'hidden', axis=0, tiled=True)  15.7 us
    all_gather x1, blocking collectives, local(): full = lax.all_gather(latest, 'hidden', axis=0, tiled=True)  13.6 us
  transfers between devices with their start and end apart: 4, of which 4 were waited for; matrix products, arithmetic and copies ran while one was open for 0% of the time, Pallas kernels for 0%

commit v1 on v0

v1 whole, which is shorter than its diff:
```python
import jax
import jax.numpy as jnp
from jax import lax
from jax.experimental import pallas as pl
from jax.experimental.pallas import tpu as pltpu
from jax.sharding import PartitionSpec as P

STEPS = 2
PIECES = 2
COLS = 4
bf16, f32 = jnp.bfloat16, jnp.float32


def plain(tokens, w_in, w_out):
    row_dev = tokens.shape[0]
    where = lax.axis_index("hidden")
    full = lax.all_gather(tokens, "hidden", axis=0, tiled=True)
    latest = tokens
    for step in range(STEPS):
        pre = jnp.dot(full, w_in, preferred_element_type=f32)
        summed = lax.psum(pre.astype(bf16), "width").astype(f32)
        activ = jax.nn.gelu(summed, approximate=True).astype(bf16)
        mine_sum = lax.psum_scatter(
            jnp.dot(activ, w_out, preferred_element_type=f32).astype(bf16),
            "hidden",
            scatter_dimension=0,
            tiled=True,
        ).astype(f32)
        mine_old = lax.dynamic_slice_in_dim(full, where * row_dev, row_dev, 0)
        latest = (mine_old.astype(f32) + mine_sum).astype(bf16)
        if step + 1 < STEPS:
            full = lax.all_gather(latest, "hidden", axis=0, tiled=True)
    return latest


def swap(x, axis, n, mask):
    return lax.ppermute(x, axis, [(i, i ^ mask) for i in range(n)])


def stage(products, loads, name, behind=()):
    arrays = []
    for array, _, _ in loads:
        if not any(array is a for a in arrays):
            arrays.append(array)
    flat = [r for pair in products for r in pair]
    n_p, n_a, n_l = len(flat), len(arrays), len(loads)
    which = [next(i for i, a in enumerate(arrays) if a is array) for array, _, _ in loads]

    def kernel(*refs):
        given, hbm = refs[:n_p], refs[n_p : n_p + n_a]
        out = refs[n_p + n_a + len(behind) :]
        result = out[0] if products else None
        out = out[1:] if products else out
        held, sems = out[:n_l], out[n_l:]
        core = lax.rem(lax.axis_index("width"), 2)
        copies = []
        for i, (array, rows, cols) in enumerate(loads):
            index = []
            for (size, start, per), full in zip((rows, cols), array.shape):
                if per:
                    half = core if per > 0 else 1 - core
                    start = pl.multiple_of(half * (full // 2) + start, 128)
                index.append(pl.ds(start, size))
            copies.append(pltpu.make_async_copy(hbm[which[i]].at[tuple(index)], held[i], sems[0].at[i]))
        for copy in copies:
            copy.start()
        if products:
            total = None
            for i in range(0, n_p, 2):
                part = jnp.dot(given[i][...], given[i + 1][...], preferred_element_type=f32)
                total = part if total is None else total + part
            result[...] = total.astype(result.dtype)
        for copy in copies:
            copy.wait()

    shapes = [pltpu.VMEM((r[0], c[0]), a.dtype) for a, r, c in loads]
    if products:
        shapes = [jax.ShapeDtypeStruct((flat[0].shape[0], flat[1].shape[1]), bf16)] + shapes
    vmem = pl.BlockSpec(memory_space=pltpu.VMEM)
    got = pl.pallas_call(
        kernel,
        out_shape=shapes,
        in_specs=[vmem] * n_p + [pl.BlockSpec(memory_space=pltpu.HBM)] * n_a + [pl.BlockSpec(memory_space=pl.ANY)] * len(behind),
        out_specs=[vmem] * len(shapes),
        scratch_shapes=[pltpu.SemaphoreType.DMA((n_l,))] if loads else [],
        compiler_params=pltpu.CompilerParams(vmem_limit_bytes=3 * 2**20),
        cost_estimate=pl.CostEstimate(
            flops=sum(2 * flat[i].shape[0] * flat[i + 1].size for i in range(0, n_p, 2)),
            bytes_accessed=sum(2 * r[0] * c[0] for _, r, c in loads),
            transcendentals=0,
        ),
        name=name,
    )(*flat, *[pltpu.with_memory_space_constraint(a, pltpu.HBM) for a in arrays], *behind)
    return (got[0], list(got[1:])) if products else (None, list(got))


def gather(block, nz):
    return jnp.concatenate([block] + [swap(block, "hidden", nz, k) for k in range(1, nz)], 0)


def tuned(nz, nw, tokens, w_in, w_out):
    rows, d = tokens.shape
    f = w_in.shape[1]
    piece, cols = f // 2 // PIECES, d // COLS

    def up(j, per):
        return (w_in, (d, 0, 0), (piece, j * piece, per))

    def down(n):
        return [(w_out, (f // 2, 0, per), (cols, n * cols, 0)) for per in (1, -1)]

    def after(sent, kept):
        chip = (kept.astype(f32) + swap(sent, "width", nw, 1).astype(f32)).astype(bf16)
        total = chip.astype(f32) + swap(chip, "width", nw, 2).astype(f32)
        return jax.nn.gelu(total, approximate=True).astype(bf16)

    def scattered(part, old):
        total = part[:rows].astype(f32)
        for k in range(1, nz):
            total = total + swap(part[k * rows : (k + 1) * rows], "hidden", nz, k).astype(f32)
        return (old.astype(f32) + total).astype(bf16)

    x = gather(tokens, nz)
    old = [tokens[:, n * cols : (n + 1) * cols] for n in range(COLS)]

    _, (t0, m0) = stage([], [up(0, -1), up(0, 1)], "load_up")
    p_t0, (t1,) = stage([(x, t0)], [up(1, -1)], "up_t0")
    p_m0, (m1,) = stage([(x, m0)], [up(1, 1)], "up_m0", [p_t0])
    p_t1, wo0 = stage([(x, t1)], down(0), "up_t1", [p_m0])
    p_m1, wo1 = stage([(x, m1)], down(1), "up_m1", [p_t1])
    a0 = after(p_t0, p_m0)
    a1 = after(p_t1, p_m1)
    _, wo2 = stage([], down(2), "load_down", [p_m1])
    mine = jnp.concatenate([a0, a1], 1)
    other = jnp.concatenate([swap(a0, "width", nw, 1), swap(a1, "width", nw, 1)], 1)
    q0, _ = stage([(mine, wo0[0]), (other, wo0[1])], [], "down_0", [wo2[0]])
    q1, wo3 = stage([(mine, wo1[0]), (other, wo1[1])], down(3), "down_1", [q0])
    q2, (t0,) = stage([(mine, wo2[0]), (other, wo2[1])], [up(0, -1)], "down_2", [q1])
    q3, _ = stage([(mine, wo3[0]), (other, wo3[1])], [], "down_3", [q2])
    old = [scattered(q, o) for q, o in zip((q0, q1, q2, q3), old)]
    x = jnp.concatenate([gather(o, nz) for o in old], 1)

    p_t0, _ = stage([(x, t0)], [], "up_t0")
    p_m0, _ = stage([(x, m0)], [], "up_m0", [p_t0])
    p_t1, _ = stage([(x, t1)], [], "up_t1", [p_m0])
    p_m1, _ = stage([(x, m1)], [], "up_m1", [p_t1])
    a0 = after(p_t0, p_m0)
    a1 = after(p_t1, p_m1)
    _, wo01 = stage([], down(0) + down(1), "load_down", [p_m1])
    wo0, wo1 = wo01[:2], wo01[2:]
    mine = jnp.concatenate([a0, a1], 1)
    other = jnp.concatenate([swap(a0, "width", nw, 1), swap(a1, "width", nw, 1)], 1)
    new, last = [], wo01[0]
    for n, wo in ((2, wo2), (3, wo3), (0, wo0), (1, wo1)):
        last, _ = stage([(mine, wo[0]), (other, wo[1])], [], f"down_{n}", [last])
        new.append((n, scattered(last, old[n])))
    return jnp.concatenate([v for _, v in sorted(new, key=lambda item: item[0])], 1)


def solution(mesh):
    placed = (P(("groups", "hidden"), "width"), P("width", "hidden"), P("hidden", "width"))
    nz, nw = mesh.shape["hidden"], mesh.shape["width"]

    def local(tokens, w_in, w_out):
        fits = nz == 4 and nw == 4 and w_in.shape[1] % (256 * PIECES) == 0
        return tuned(nz, nw, tokens, w_in, w_out) if fits else plain(tokens, w_in, w_out)

    return jax.shard_map(
        local,
        mesh=mesh,
        in_specs=placed,
        out_specs=P(("groups", "hidden"), "width"),
        check_vma=False,
    )
```

time: 213 us -> 165 us (0.77)
  waiting for transfers between devices: 104 us -> 19 us
  Pallas kernels: 0 us -> 69.3 us
  starting transfers between devices: 0.13 us -> 64.4 us
  matrix products: 63.5 us -> 0 us
  blocking collectives: 29.2 us -> 0 us
  between operations: 13.1 us -> 0.55 us
  local copies, waits for them, and re-layouts: 0 us -> 10.4 us
    pallas_call x0 -> x19, Pallas kernels: none -> 69.3 us  [stage(): pl.pallas_call(kernel, out_shape=shapes, in_specs=[vmem] * n_p + [pl.Bloc...]
    psum x2 -> x0, waiting for transfers between devices: 65.3 us -> none  [local(): summed = lax.psum(pre.astype(jnp.bfloat16), 'width').astype(jnp.float32)]
    ppermute x0 -> x51, starting transfers between devices: none -> 64.4 us  [swap(): return lax.ppermute(x, axis, [(i, i ^ mask) for i in range(n)])]
    dot_general x4 -> x0, matrix products: 63.5 us -> none  [the longest x2 31.8 us: local(): jnp.dot(activ, w_out, preferred_element_type=jnp.float32)]
    reduce_scatter x2 -> x0, waiting for transfers between devices: 39 us -> none  [local(): lax.psum_scatter(jnp.dot(activ, w_out, preferred_element_type=jnp.float32...]
    all_gather x2 -> x0, blocking collectives: 29.2 us -> none  [the longest x1 15.7 us: local(): full = lax.all_gather(tokens, 'hidden', axis=0, tiled=True)]
    ppermute x0 -> x51, waiting for transfers between devices: none -> 19 us  [swap(): return lax.ppermute(x, axis, [(i, i ^ mask) for i in range(n)])]
    unnamed x0 -> x29, local copies, waits for them, and re-layouts: none -> 10.3 us
  transfers between devices with their start and end apart: 4 -> 51, of which waited for: 4 -> 12; matrix products, arithmetic and copies ran while one was open for 0% -> 1% of each run, Pallas kernels for 0% -> 21%
where the time goes in v1:
time: 165 us
  Pallas kernels  69.3 us (42%)
  starting transfers between devices  64.4 us (39%)
  waiting for transfers between devices  19 us (12%)
  local copies, waits for them, and re-layouts  10.4 us (6%)
    pallas_call x19, Pallas kernels, stage(): pl.pallas_call(kernel, out_shape=shapes, in_specs=[vmem] * n_p + [pl.Bloc...  69.3 us
    ppermute x51, starting transfers between devices, swap(): return lax.ppermute(x, axis, [(i, i ^ mask) for i in range(n)])  64.4 us
    ppermute x51, waiting for transfers between devices, swap(): return lax.ppermute(x, axis, [(i, i ^ mask) for i in range(n)])  19 us
    unnamed x29, local copies, waits for them, and re-layouts  10.3 us
  transfers between devices with their start and end apart: 51, of which 12 were waited for; matrix products, arithmetic and copies ran while one was open for 1% of the time, Pallas kernels for 21%

profile of v1, /device:TPU:0, one launch (start us, length us, event | category | flops | bytes accessed | tf_op | source)
XLA Modules:
  0.0 164.8 jit_solution(11958099100281352284)
XLA Ops:
  0.0 3.0 %collective-permute-start = (bf16[8,3072]{1,0:T(8,128)(2,1)}, bf16[8,3072]{1,0:T(8,128)(2,1)S(1)}, u32[]{:S(2)}, u32[]{:S(2)}) collective-permute-start(bf16[8,3072]{1,0:T(8,128)(2,1)} %param.3), channel_id=1, source_target_pairs={{0,4},{4,0},{8,12},{12,8},{1,5},{5,1},{9,13},{13,9},{2,6},{6,2},{1... | collective-permute-start | bytes 147464 | tf_op jit(solution)/shard_map/ppermute | solution.py:37
  3.0 2.6 %collective-permute-start.1 = (bf16[8,3072]{1,0:T(8,128)(2,1)}, bf16[8,3072]{1,0:T(8,128)(2,1)S(1)}, u32[]{:S(2)}, u32[]{:S(2)}) collective-permute-start(bf16[8,3072]{1,0:T(8,128)(2,1)} %param.3), channel_id=1, source_target_pairs={{0,8},{4,12},{8,0},{12,4},{1,9},{5,13},{9,1},{13,5},{2,10},{6,14},... | collective-permute-start | bytes 147464 | tf_op jit(solution)/shard_map/ppermute | solution.py:37
  6.5 6.5 %load_up.1 = (bf16[3072,1536]{1,0:T(8,128)(2,1)S(1)}, bf16[3072,1536]{1,0:T(8,128)(2,1)S(1)}) custom-call(bf16[3072,6144]{1,0:T(8,128)(2,1)} %refs_4_.3), custom_call_target="tpu_custom_call" | custom-call | bytes 18874368 | tf_op jit(solution)/shard_map/load_up/pallas_call | solution.py:80
  13.0 5.3 %up_t0.2 = (bf16[32,1536]{1,0:T(8,128)(2,1)S(1)}, bf16[3072,1536]{1,0:T(8,128)(2,1)S(1)}) custom-call(bf16[32,3072]{1,0:T(8,128)(2,1)S(1)} %constant_dynamic-update-slice_fusion.refs_0_, bf16[3072,1536]{1,0:T(8,128)(2,1)S(1)} %get-tuple-element.29.refs_1_, bf16[3072,6144]{1,0:T(8,128)(2,1)} %refs_4_.3), custom_call_target="tpu_custom_call" | custom-call | flops 301989888 | bytes 9437184 | tf_op jit(solution)/shard_map/up_t0/pallas_call | solution.py:80
  18.3 5.3 %up_m0.2 = (bf16[32,1536]{1,0:T(8,128)(2,1)S(1)}, bf16[3072,1536]{1,0:T(8,128)(2,1)S(1)}) custom-call(bf16[32,3072]{1,0:T(8,128)(2,1)S(1)} %constant_dynamic-update-slice_fusion.refs_0_, bf16[3072,1536]{1,0:T(8,128)(2,1)S(1)} %get-tuple-element.28.refs_1_, bf16[3072,6144]{1,0:T(8,128)(2,1)} %refs_4_.3, bf16[32,1536]{1,0:T(8,128)(2,1)S(1)} %get-tuple-element.30.refs_3_), custom_call_target="tpu_custom_call" | custom-call | flops 301989888 | bytes 9437184 | tf_op jit(solution)/shard_map/up_m0/pallas_call | solution.py:80
  23.6 5.4 %up_t1.2 = (bf16[32,1536]{1,0:T(8,128)(2,1)S(1)}, bf16[3072,768]{1,0:T(8,128)(2,1)S(1)}, bf16[3072,768]{1,0:T(8,128)(2,1)S(1)}) custom-call(bf16[32,3072]{1,0:T(8,128)(2,1)S(1)} %constant_dynamic-update-slice_fusion.refs_0_, bf16[3072,1536]{1,0:T(8,128)(2,1)S(1)} %get-tuple-element.33.refs_1_, bf16[6144,3072]{1,0:T(8,128)(2,1)} %refs_0_.5, ...), custom_call_target="tpu_custom_call" | custom-call | flops 301989888 | bytes 9437184 | tf_op jit(solution)/shard_map/up_t1/pallas_call | solution.py:80
  29.6 5.4 %up_m1.2 = (bf16[32,1536]{1,0:T(8,128)(2,1)S(1)}, bf16[3072,768]{1,0:T(8,128)(2,1)S(1)}, bf16[3072,768]{1,0:T(8,128)(2,1)S(1)}) custom-call(bf16[32,3072]{1,0:T(8,128)(2,1)S(1)} %constant_dynamic-update-slice_fusion.refs_0_, bf16[3072,1536]{1,0:T(8,128)(2,1)S(1)} %get-tuple-element.32.refs_1_, bf16[6144,3072]{1,0:T(8,128)(2,1)} %refs_0_.5, ...), custom_call_target="tpu_custom_call" | custom-call | flops 301989888 | bytes 9437184 | tf_op jit(solution)/shard_map/up_m1/pallas_call | solution.py:80
  35.0 7.1 %load_down.2 = (bf16[3072,768]{1,0:T(8,128)(2,1)S(1)}, bf16[3072,768]{1,0:T(8,128)(2,1)S(1)}) custom-call(bf16[6144,3072]{1,0:T(8,128)(2,1)} %refs_0_.5, bf16[32,1536]{1,0:T(8,128)(2,1)S(1)} %get-tuple-element.35.refs_1_), custom_call_target="tpu_custom_call" | custom-call | bytes 9437184 | tf_op jit(solution)/shard_map/load_down/pallas_call | solution.py:80
  42.2 1.7 %collective-permute-start.6 = (bf16[32,1536]{1,0:T(8,128)(2,1)S(1)}, bf16[32,1536]{1,0:T(8,128)(2,1)S(1)}, u32[]{:S(2)}, u32[]{:S(2)}) collective-permute-start(bf16[32,1536]{1,0:T(8,128)(2,1)S(1)} %add_convert_fusion.2), channel_id=1, source_target_pairs={{0,2},{1,3},{2,0},{3,1},{4,6},{5,7},{6,4},{7,5},{8,10},{9,11},{10,... | collective-permute-start | bytes 294920 | tf_op jit(solution)/shard_map/ppermute | solution.py:37
  44.3 3.3 %collective-permute-done.6 = bf16[32,1536]{1,0:T(8,128)(2,1)S(1)} collective-permute-done((bf16[32,1536]{1,0:T(8,128)(2,1)S(1)}, bf16[32,1536]{1,0:T(8,128)(2,1)S(1)}, u32[]{:S(2)}, u32[]{:S(2)}) %collective-permute-start.6) | collective-permute-done | bytes 98336 | tf_op jit(solution)/shard_map/ppermute | solution.py:37
  50.6 2.5 %copy-done.6 = bf16[3072,768]{1,0:T(8,128)(2,1)S(1)} copy-done((bf16[3072,768]{1,0:T(8,128)(2,1)S(1)}, bf16[3072,768]{1,0:T(8,128)(2,1)}, u32[]{:S(2)}) %copy-start.6) | copy-done | bytes 4718616
  53.1 1.7 %down_0.2.refs_5_ = bf16[32,768]{1,0:T(8,128)(2,1)S(1)} custom-call(bf16[32,3072]{1,0:T(8,128)(2,1)S(1)} %pad_maximum_fusion.refs_0_, bf16[3072,768]{1,0:T(8,128)(2,1)S(1)} %get-tuple-element.36.refs_1_, bf16[32,3072]{1,0:T(8,128)(2,1)S(1)} %constant_dynamic-update-slice_fusion.4.refs_2_, bf16[3072,768]{1,0:T(8,128)(2,1)S(1)} %copy-done.6, ...), custom_call_target="tpu_custom_call" | custom-call | flops 301989888 | tf_op jit(solution)/shard_map/down_0/pallas_call | solution.py:80
  54.8 2.3 %copy-done.4 = bf16[3072,768]{1,0:T(8,128)(2,1)S(1)} copy-done((bf16[3072,768]{1,0:T(8,128)(2,1)S(1)}, bf16[3072,768]{1,0:T(8,128)(2,1)}, u32[]{:S(2)}) %copy-start.4) | copy-done | bytes 4718616
  57.2 5.4 %down_1.2 = (bf16[32,768]{1,0:T(8,128)(2,1)S(1)}, bf16[3072,768]{1,0:T(8,128)(2,1)S(1)}, bf16[3072,768]{1,0:T(8,128)(2,1)S(1)}) custom-call(bf16[32,3072]{1,0:T(8,128)(2,1)S(1)} %pad_maximum_fusion.refs_0_, bf16[3072,768]{1,0:T(8,128)(2,1)S(1)} %bitcast.3, bf16[32,3072]{1,0:T(8,128)(2,1)S(1)} %constant_dynamic-update-slice_fusion.4.refs_2_, ...), custom_call_target="tpu_custom_call" | custom-call | flops 301989888 | bytes 9437184 | tf_op jit(solution)/shard_map/down_1/pallas_call | solution.py:80
  62.6 2.2 %copy-done = bf16[3072,768]{1,0:T(8,128)(2,1)} copy-done((bf16[3072,768]{1,0:T(8,128)(2,1)}, bf16[3072,768]{1,0:T(8,128)(2,1)S(1)}, u32[]{:S(2)}) %copy-start) | copy-done | bytes 4718616
  64.8 5.3 %down_2.2 = (bf16[32,768]{1,0:T(8,128)(2,1)S(1)}, bf16[3072,1536]{1,0:T(8,128)(2,1)S(1)}) custom-call(bf16[32,3072]{1,0:T(8,128)(2,1)S(1)} %pad_maximum_fusion.refs_0_, bf16[3072,768]{1,0:T(8,128)(2,1)S(1)} %get-tuple-element.38.refs_4_.refs_1_, bf16[32,3072]{1,0:T(8,128)(2,1)S(1)} %constant_dynamic-update-slice_fusion.4.refs_2_, ...), custom_call_target="tpu_custom_call" | custom-call | flops 301989888 | bytes 9437184 | tf_op jit(solution)/shard_map/down_2/pallas_call | solution.py:80
  71.0 3.5 %collective-permute-start.22 = (bf16[8,768]{1,0:T(8,128)(2,1)S(1)}, bf16[8,768]{1,0:T(8,128)(2,1)S(1)}, u32[]{:S(2)}, u32[]{:S(2)}) collective-permute-start(bf16[8,768]{1,0:T(8,128)(2,1)S(1)} %get-tuple-element.74), channel_id=1, source_target_pairs={{0,8},{4,12},{8,0},{12,4},{1,9},{5,13},{9,1},{13,5},{2,10},{6,14},... | collective-permute-start | bytes 36872 | tf_op jit(solution)/shard_map/ppermute | solution.py:37
  74.5 2.3 %copy-done.1 = bf16[3072,768]{1,0:T(8,128)(2,1)S(1)} copy-done((bf16[3072,768]{1,0:T(8,128)(2,1)S(1)}, bf16[3072,768]{1,0:T(8,128)(2,1)}, u32[]{:S(2)}) %copy-start.1) | copy-done | bytes 4718616
  76.9 1.7 %down_3.2 = bf16[32,768]{1,0:T(8,128)(2,1)S(1)} custom-call(bf16[32,3072]{1,0:T(8,128)(2,1)S(1)} %pad_maximum_fusion.refs_0_, bf16[3072,768]{1,0:T(8,128)(2,1)S(1)} %get-tuple-element.44.refs_1_, bf16[32,3072]{1,0:T(8,128)(2,1)S(1)} %constant_dynamic-update-slice_fusion.4.refs_2_, bf16[3072,768]{1,0:T(8,128)(2,1)S(1)} %copy-done.1, ...), custom_call_target="tpu_custom_call" | custom-call | flops 301989888 | tf_op jit(solution)/shard_map/down_3/pallas_call | solution.py:80
  79.2 3.8 %collective-permute-start.28 = (bf16[8,768]{1,0:T(8,128)(2,1)S(1)}, bf16[8,768]{1,0:T(8,128)(2,1)S(1)}, u32[]{:S(2)}, u32[]{:S(2)}) collective-permute-start(bf16[8,768]{1,0:T(8,128)(2,1)S(1)} %get-tuple-element.77), channel_id=1, source_target_pairs={{0,8},{4,12},{8,0},{12,4},{1,9},{5,13},{9,1},{13,5},{2,10},{6,14},... | collective-permute-start | bytes 36872 | tf_op jit(solution)/shard_map/ppermute | solution.py:37
  83.6 3.8 %collective-permute-start.16 = (bf16[8,768]{1,0:T(8,128)(2,1)S(1)}, bf16[8,768]{1,0:T(8,128)(2,1)S(1)}, u32[]{:S(2)}, u32[]{:S(2)}) collective-permute-start(bf16[8,768]{1,0:T(8,128)(2,1)S(1)} %get-tuple-element.71), channel_id=1, source_target_pairs={{0,8},{4,12},{8,0},{12,4},{1,9},{5,13},{9,1},{13,5},{2,10},{6,14},... | collective-permute-start | bytes 36872 | tf_op jit(solution)/shard_map/ppermute | solution.py:37
  89.0 2.4 %collective-permute-start.11 = (bf16[8,768]{1,0:T(8,128)(2,1)S(1)}, bf16[8,768]{1,0:T(8,128)(2,1)S(1)}, u32[]{:S(2)}, u32[]{:S(2)}) collective-permute-start(bf16[8,768]{1,0:T(8,128)(2,1)S(1)} %get-tuple-element.67), channel_id=1, source_target_pairs={{0,12},{4,8},{8,4},{12,0},{1,13},{5,9},{9,5},{13,1},{2,14},{6,10},... | collective-permute-start | bytes 36872 | tf_op jit(solution)/shard_map/ppermute | solution.py:37
  91.9 1.5 collective-permute-start.24
  93.4 2.0 %collective-permute-start.25 = (bf16[8,768]{1,0:T(8,128)(2,1)S(1)}, bf16[8,768]{1,0:T(8,128)(2,1)S(1)}, u32[]{:S(2)}, u32[]{:S(2)}) collective-permute-start(bf16[8,768]{1,0:T(8,128)(2,1)S(1)} %add_convert_fusion.9), channel_id=1, source_target_pairs={{0,8},{4,12},{8,0},{12,4},{1,9},{5,13},{9,1},{13,5},{2,10},{6,14},... | collective-permute-start | bytes 36872 | tf_op jit(solution)/shard_map/ppermute | solution.py:37
  97.0 2.9 %collective-permute-start.13 = (bf16[8,768]{1,0:T(8,128)(2,1)S(1)}, bf16[8,768]{1,0:T(8,128)(2,1)S(1)}, u32[]{:S(2)}, u32[]{:S(2)}) collective-permute-start(bf16[8,768]{1,0:T(8,128)(2,1)S(1)} %get-tuple-element.63), channel_id=1, source_target_pairs={{0,8},{4,12},{8,0},{12,4},{1,9},{5,13},{9,1},{13,5},{2,10},{6,14},... | collective-permute-start | bytes 36872 | tf_op jit(solution)/shard_map/ppermute | solution.py:37
  100.9 3.4 %collective-permute-start.19 = (bf16[8,768]{1,0:T(8,128)(2,1)S(1)}, bf16[8,768]{1,0:T(8,128)(2,1)S(1)}, u32[]{:S(2)}, u32[]{:S(2)}) collective-permute-start(bf16[8,768]{1,0:T(8,128)(2,1)S(1)} %get-tuple-element.64), channel_id=1, source_target_pairs={{0,8},{4,12},{8,0},{12,4},{1,9},{5,13},{9,1},{13,5},{2,10},{6,14},... | collective-permute-start | bytes 36872 | tf_op jit(solution)/shard_map/ppermute | solution.py:37
  105.4 3.3 %collective-permute-start.31 = (bf16[8,768]{1,0:T(8,128)(2,1)S(1)}, bf16[8,768]{1,0:T(8,128)(2,1)S(1)}, u32[]{:S(2)}, u32[]{:S(2)}) collective-permute-start(bf16[8,768]{1,0:T(8,128)(2,1)S(1)} %get-tuple-element.65), channel_id=1, source_target_pairs={{0,8},{4,12},{8,0},{12,4},{1,9},{5,13},{9,1},{13,5},{2,10},{6,14},... | collective-permute-start | bytes 36872 | tf_op jit(solution)/shard_map/ppermute | solution.py:37
  110.4 3.8 %collective-permute-done.32 = bf16[8,768]{1,0:T(8,128)(2,1)S(1)} collective-permute-done((bf16[8,768]{1,0:T(8,128)(2,1)S(1)}, bf16[8,768]{1,0:T(8,128)(2,1)S(1)}, u32[]{:S(2)}, u32[]{:S(2)}) %collective-permute-start.32) | collective-permute-done | bytes 12320 | tf_op jit(solution)/shard_map/ppermute | solution.py:37
  114.2 1.7 %up_t0.3.refs_2_ = bf16[32,1536]{1,0:T(8,128)(2,1)S(1)} custom-call(bf16[32,3072]{1,0:T(8,128)(2,1)S(1)} %maximum_maximum_fusion.refs_0_, bf16[3072,1536]{1,0:T(8,128)(2,1)S(1)} %get-tuple-element.46.refs_1_), custom_call_target="tpu_custom_call" | custom-call | flops 301989888 | tf_op jit(solution)/shard_map/up_t0/pallas_call | solution.py:80
  115.9 1.7 %up_m0.3.refs_2_ = bf16[32,1536]{1,0:T(8,128)(2,1)S(1)} custom-call(bf16[32,3072]{1,0:T(8,128)(2,1)S(1)} %maximum_maximum_fusion.refs_0_, bf16[3072,1536]{1,0:T(8,128)(2,1)S(1)} %get-tuple-element.28.refs_1_, bf16[32,1536]{1,0:T(8,128)(2,1)S(1)} %up_t0.3.refs_2_), custom_call_target="tpu_custom_call" | custom-call | flops 301989888 | tf_op jit(solution)/shard_map/up_m0/pallas_call | solution.py:80
  117.6 1.9 %up_t1.3.refs_2_ = bf16[32,1536]{1,0:T(8,128)(2,1)S(1)} custom-call(bf16[32,3072]{1,0:T(8,128)(2,1)S(1)} %maximum_maximum_fusion.refs_0_, bf16[3072,1536]{1,0:T(8,128)(2,1)S(1)} %get-tuple-element.33.refs_1_, bf16[32,1536]{1,0:T(8,128)(2,1)S(1)} %up_m0.3.refs_2_), custom_call_target="tpu_custom_call" | custom-call | flops 301989888 | tf_op jit(solution)/shard_map/up_t1/pallas_call | solution.py:80
  120.0 1.7 %up_m1.3.refs_1_ = bf16[32,1536]{1,0:T(8,128)(2,1)S(1)} custom-call(bf16[32,3072]{1,0:T(8,128)(2,1)S(1)} %maximum_maximum_fusion.refs_0_, bf16[3072,1536]{1,0:T(8,128)(2,1)S(1)} %get-tuple-element.32.refs_1_, bf16[32,1536]{1,0:T(8,128)(2,1)S(1)} %up_t1.3.refs_2_), custom_call_target="tpu_custom_call" | custom-call | flops 301989888 | tf_op jit(solution)/shard_map/up_m1/pallas_call | solution.py:80
  121.7 6.6 %load_down.3 = (bf16[3072,768]{1,0:T(8,128)(2,1)S(1)}, bf16[3072,768]{1,0:T(8,128)(2,1)S(1)}, bf16[3072,768]{1,0:T(8,128)(2,1)S(1)}, bf16[3072,768]{1,0:T(8,128)(2,1)S(1)}) custom-call(bf16[6144,3072]{1,0:T(8,128)(2,1)} %refs_0_.5, bf16[32,1536]{1,0:T(8,128)(2,1)S(1)} %up_m1.3.refs_1_), custom_call_target="tpu_custom_call" | custom-call | bytes 18874368 | tf_op jit(solution)/shard_map/load_down/pallas_call | solution.py:80
  128.4 1.6 collective-permute-start.34
  130.5 3.4 %collective-permute-done.34 = bf16[32,1536]{1,0:T(8,128)(2,1)S(1)} collective-permute-done((bf16[32,1536]{1,0:T(8,128)(2,1)S(1)}, bf16[32,1536]{1,0:T(8,128)(2,1)S(1)}, u32[]{:S(2)}, u32[]{:S(2)}) %collective-permute-start.34) | collective-permute-done | bytes 98336 | tf_op jit(solution)/shard_map/ppermute | solution.py:37
  136.7 1.7 %down_2.3.refs_4_ = bf16[32,768]{1,0:T(8,128)(2,1)S(1)} custom-call(bf16[32,3072]{1,0:T(8,128)(2,1)S(1)} %pad_maximum_fusion.1.refs_0_, bf16[3072,768]{1,0:T(8,128)(2,1)S(1)} %get-tuple-element.38.refs_4_.refs_1_, bf16[32,3072]{1,0:T(8,128)(2,1)S(1)} %constant_dynamic-update-slice_fusion.6.refs_2_, bf16[3072,768]{1,0:T(8,128)(2,1)S(1)} %get-tuple-element.42.refs_3_, ...), custom_call_target="tpu_custom_call" | custom-call | flops 301989888 | tf_op jit(solution)/shard_map/down_2/pallas_call | solution.py:80
  138.5 1.7 %down_3.3.refs_4_ = bf16[32,768]{1,0:T(8,128)(2,1)S(1)} custom-call(bf16[32,3072]{1,0:T(8,128)(2,1)S(1)} %pad_maximum_fusion.1.refs_0_, bf16[3072,768]{1,0:T(8,128)(2,1)S(1)} %get-tuple-element.44.refs_1_, bf16[32,3072]{1,0:T(8,128)(2,1)S(1)} %constant_dynamic-update-slice_fusion.6.refs_2_, bf16[3072,768]{1,0:T(8,128)(2,1)S(1)} %bitcast.1, ...), custom_call_target="tpu_custom_call" | custom-call | flops 301989888 | tf_op jit(solution)/shard_map/down_3/pallas_call | solution.py:80
  140.2 1.7 %down_0.3.refs_4_ = bf16[32,768]{1,0:T(8,128)(2,1)S(1)} custom-call(bf16[32,3072]{1,0:T(8,128)(2,1)S(1)} %pad_maximum_fusion.1.refs_0_, bf16[3072,768]{1,0:T(8,128)(2,1)S(1)} %get-tuple-element.47.refs_4_.refs_1_, bf16[32,3072]{1,0:T(8,128)(2,1)S(1)} %constant_dynamic-update-slice_fusion.6.refs_2_, bf16[3072,768]{1,0:T(8,128)(2,1)S(1)} %get-tuple-element.48.refs_3_, ...), custom_call_target="tpu_custom_call" | custom-call | flops 301989888 | tf_op jit(solution)/shard_map/down_0/pallas_call | solution.py:80
  142.0 1.5 collective-permute-start.40
  143.5 2.9 %collective-permute-start.41 = (bf16[8,768]{1,0:T(8,128)(2,1)S(1)}, bf16[8,768]{1,0:T(8,128)(2,1)S(1)}, u32[]{:S(2)}, u32[]{:S(2)}) collective-permute-start(bf16[8,768]{1,0:T(8,128)(2,1)S(1)} %get-tuple-element.52), channel_id=1, source_target_pairs={{0,12},{4,8},{8,4},{12,0},{1,13},{5,9},{9,5},{13,1},{2,14},{6,10},... | collective-permute-start | bytes 36872 | tf_op jit(solution)/shard_map/ppermute | solution.py:37
  146.4 1.7 %down_1.3 = bf16[32,768]{1,0:T(8,128)(2,1)S(1)} custom-call(bf16[32,3072]{1,0:T(8,128)(2,1)S(1)} %pad_maximum_fusion.1.refs_0_, bf16[3072,768]{1,0:T(8,128)(2,1)S(1)} %get-tuple-element.49.refs_1_, bf16[32,3072]{1,0:T(8,128)(2,1)S(1)} %constant_dynamic-update-slice_fusion.6.refs_2_, bf16[3072,768]{1,0:T(8,128)(2,1)S(1)} %get-tuple-element.50.refs_3_, ...), custom_call_target="tpu_custom_call" | custom-call | flops 301989888 | tf_op jit(solution)/shard_map/down_1/pallas_call | solution.py:80
  148.2 1.5 collective-permute-start.43
  149.7 2.9 %collective-permute-start.44 = (bf16[8,768]{1,0:T(8,128)(2,1)S(1)}, bf16[8,768]{1,0:T(8,128)(2,1)S(1)}, u32[]{:S(2)}, u32[]{:S(2)}) collective-permute-start(bf16[8,768]{1,0:T(8,128)(2,1)S(1)} %get-tuple-element.55), channel_id=1, source_target_pairs={{0,12},{4,8},{8,4},{12,0},{1,13},{5,9},{9,5},{13,1},{2,14},{6,10},... | collective-permute-start | bytes 36872 | tf_op jit(solution)/shard_map/ppermute | solution.py:37
  152.6 1.5 collective-permute-start.46
  154.1 2.9 %collective-permute-start.47 = (bf16[8,768]{1,0:T(8,128)(2,1)S(1)}, bf16[8,768]{1,0:T(8,128)(2,1)S(1)}, u32[]{:S(2)}, u32[]{:S(2)}) collective-permute-start(bf16[8,768]{1,0:T(8,128)(2,1)S(1)} %get-tuple-element.58), channel_id=1, source_target_pairs={{0,12},{4,8},{8,4},{12,0},{1,13},{5,9},{9,5},{13,1},{2,14},{6,10},... | collective-permute-start | bytes 36872 | tf_op jit(solution)/shard_map/ppermute | solution.py:37
  157.1 1.5 collective-permute-start.49
  158.6 2.9 %collective-permute-start.50 = (bf16[8,768]{1,0:T(8,128)(2,1)S(1)}, bf16[8,768]{1,0:T(8,128)(2,1)S(1)}, u32[]{:S(2)}, u32[]{:S(2)}) collective-permute-start(bf16[8,768]{1,0:T(8,128)(2,1)S(1)} %get-tuple-element.61), channel_id=1, source_target_pairs={{0,12},{4,8},{8,4},{12,0},{1,13},{5,9},{9,5},{13,1},{2,14},{6,10},... | collective-permute-start | bytes 36872 | tf_op jit(solution)/shard_map/ppermute | solution.py:37
  161.7 2.5 %collective-permute-done.50 = bf16[8,768]{1,0:T(8,128)(2,1)S(1)} collective-permute-done((bf16[8,768]{1,0:T(8,128)(2,1)S(1)}, bf16[8,768]{1,0:T(8,128)(2,1)S(1)}, u32[]{:S(2)}, u32[]{:S(2)}) %collective-permute-start.50) | collective-permute-done | bytes 12320 | tf_op jit(solution)/shard_map/ppermute | solution.py:37
  (133 shorter events, 19.6 us)
Async XLA Ops:
  0.0 13.0 %collective-permute-start = (bf16[8,3072]{1,0:T(8,128)(2,1)}, bf16[8,3072]{1,0:T(8,128)(2,1)S(1)}, u32[]{:S(2)}, u32[]{:S(2)}) collective-permute-start(bf16[8,3072]{1,0:T(8,128)(2,1)} %param.3), channel_id=1, source_target_pairs={{0,4},{4,0},{8,12},{12,8},{1,5},{5,1},{9,13},{13,9},{2,6},{6,2},{1... | collective-permute-start | bytes 147464 | tf_op jit(solution)/shard_map/ppermute | solution.py:37
  3.0 10.0 %collective-permute-start.1 = (bf16[8,3072]{1,0:T(8,128)(2,1)}, bf16[8,3072]{1,0:T(8,128)(2,1)S(1)}, u32[]{:S(2)}, u32[]{:S(2)}) collective-permute-start(bf16[8,3072]{1,0:T(8,128)(2,1)} %param.3), channel_id=1, source_target_pairs={{0,8},{4,12},{8,0},{12,4},{1,9},{5,13},{9,1},{13,5},{2,10},{6,14},... | collective-permute-start | bytes 147464 | tf_op jit(solution)/shard_map/ppermute | solution.py:37
  5.6 7.4 %collective-permute-start.2 = (bf16[8,3072]{1,0:T(8,128)(2,1)}, bf16[8,3072]{1,0:T(8,128)(2,1)S(1)}, u32[]{:S(2)}, u32[]{:S(2)}) collective-permute-start(bf16[8,3072]{1,0:T(8,128)(2,1)} %param.3), channel_id=1, source_target_pairs={{0,12},{4,8},{8,4},{12,0},{1,13},{5,9},{9,5},{13,1},{2,14},{6,10},... | collective-permute-start | bytes 147464 | tf_op jit(solution)/shard_map/ppermute | solution.py:37
  29.0 13.1 %collective-permute-start.5 = (bf16[32,1536]{1,0:T(8,128)(2,1)S(1)}, bf16[32,1536]{1,0:T(8,128)(2,1)S(1)}, u32[]{:S(2)}, u32[]{:S(2)}) collective-permute-start(bf16[32,1536]{1,0:T(8,128)(2,1)S(1)} %get-tuple-element.34.refs_3_), channel_id=1, source_target_pairs={{0,1},{1,0},{2,3},{3,2},{4,5},{5,4},{6,7},{7,6},{8,9},{9,8},{10,11... | collective-permute-start | bytes 294920 | tf_op jit(solution)/shard_map/ppermute | solution.py:37
  29.1 14.8 %collective-permute-start.3 = (bf16[32,1536]{1,0:T(8,128)(2,1)S(1)}, bf16[32,1536]{1,0:T(8,128)(2,1)S(1)}, u32[]{:S(2)}, u32[]{:S(2)}) collective-permute-start(bf16[32,1536]{1,0:T(8,128)(2,1)S(1)} %get-tuple-element.30.refs_3_), channel_id=1, source_target_pairs={{0,1},{1,0},{2,3},{3,2},{4,5},{5,4},{6,7},{7,6},{8,9},{9,8},{10,11... | collective-permute-start | bytes 294920 | tf_op jit(solution)/shard_map/ppermute | solution.py:37
  42.2 5.5 %collective-permute-start.6 = (bf16[32,1536]{1,0:T(8,128)(2,1)S(1)}, bf16[32,1536]{1,0:T(8,128)(2,1)S(1)}, u32[]{:S(2)}, u32[]{:S(2)}) collective-permute-start(bf16[32,1536]{1,0:T(8,128)(2,1)S(1)} %add_convert_fusion.2), channel_id=1, source_target_pairs={{0,2},{1,3},{2,0},{3,1},{4,6},{5,7},{6,4},{7,5},{8,10},{9,11},{10,... | collective-permute-start | bytes 294920 | tf_op jit(solution)/shard_map/ppermute | solution.py:37
  43.9 5.2 %collective-permute-start.4 = (bf16[32,1536]{1,0:T(8,128)(2,1)S(1)}, bf16[32,1536]{1,0:T(8,128)(2,1)S(1)}, u32[]{:S(2)}, u32[]{:S(2)}) collective-permute-start(bf16[32,1536]{1,0:T(8,128)(2,1)S(1)} %add_convert_fusion.3), channel_id=1, source_target_pairs={{0,2},{1,3},{2,0},{3,1},{4,6},{5,7},{6,4},{7,5},{8,10},{9,11},{10,... | collective-permute-start | bytes 294920 | tf_op jit(solution)/shard_map/ppermute | solution.py:37
  47.8 2.8 %collective-permute-start.8 = (bf16[32,1536]{1,0:T(8,128)(2,1)S(1)}, bf16[32,1536]{1,0:T(8,128)(2,1)S(1)}, u32[]{:S(2)}, u32[]{:S(2)}) collective-permute-start(bf16[32,1536]{1,0:T(8,128)(2,1)S(1)} %fusion.15), channel_id=1, source_target_pairs={{0,1},{1,0},{2,3},{3,2},{4,5},{5,4},{6,7},{7,6},{8,9},{9,8},{10,11... | collective-permute-start | bytes 294920 | tf_op jit(solution)/shard_map/ppermute | solution.py:37
  70.1 12.9 %collective-permute-start.21 = (bf16[8,768]{1,0:T(8,128)(2,1)S(1)}, bf16[8,768]{1,0:T(8,128)(2,1)S(1)}, u32[]{:S(2)}, u32[]{:S(2)}) collective-permute-start(bf16[8,768]{1,0:T(8,128)(2,1)S(1)} %get-tuple-element.72), channel_id=1, source_target_pairs={{0,4},{4,0},{8,12},{12,8},{1,5},{5,1},{9,13},{13,9},{2,6},{6,2},{1... | collective-permute-start | bytes 36872 | tf_op jit(solution)/shard_map/ppermute | solution.py:37
  71.0 12.1 %collective-permute-start.22 = (bf16[8,768]{1,0:T(8,128)(2,1)S(1)}, bf16[8,768]{1,0:T(8,128)(2,1)S(1)}, u32[]{:S(2)}, u32[]{:S(2)}) collective-permute-start(bf16[8,768]{1,0:T(8,128)(2,1)S(1)} %get-tuple-element.74), channel_id=1, source_target_pairs={{0,8},{4,12},{8,0},{12,4},{1,9},{5,13},{9,1},{13,5},{2,10},{6,14},... | collective-permute-start | bytes 36872 | tf_op jit(solution)/shard_map/ppermute | solution.py:37
  74.5 9.1 %collective-permute-start.23 = (bf16[8,768]{1,0:T(8,128)(2,1)S(1)}, bf16[8,768]{1,0:T(8,128)(2,1)S(1)}, u32[]{:S(2)}, u32[]{:S(2)}) collective-permute-start(bf16[8,768]{1,0:T(8,128)(2,1)S(1)} %get-tuple-element.73), channel_id=1, source_target_pairs={{0,12},{4,8},{8,4},{12,0},{1,13},{5,9},{9,5},{13,1},{2,14},{6,10},... | collective-permute-start | bytes 36872 | tf_op jit(solution)/shard_map/ppermute | solution.py:37
  78.6 8.8 %collective-permute-start.27 = (bf16[8,768]{1,0:T(8,128)(2,1)S(1)}, bf16[8,768]{1,0:T(8,128)(2,1)S(1)}, u32[]{:S(2)}, u32[]{:S(2)}) collective-permute-start(bf16[8,768]{1,0:T(8,128)(2,1)S(1)} %get-tuple-element.75), channel_id=1, source_target_pairs={{0,4},{4,0},{8,12},{12,8},{1,5},{5,1},{9,13},{13,9},{2,6},{6,2},{1... | collective-permute-start | bytes 36872 | tf_op jit(solution)/shard_map/ppermute | solution.py:37
  79.2 8.3 %collective-permute-start.28 = (bf16[8,768]{1,0:T(8,128)(2,1)S(1)}, bf16[8,768]{1,0:T(8,128)(2,1)S(1)}, u32[]{:S(2)}, u32[]{:S(2)}) collective-permute-start(bf16[8,768]{1,0:T(8,128)(2,1)S(1)} %get-tuple-element.77), channel_id=1, source_target_pairs={{0,8},{4,12},{8,0},{12,4},{1,9},{5,13},{9,1},{13,5},{2,10},{6,14},... | collective-permute-start | bytes 36872 | tf_op jit(solution)/shard_map/ppermute | solution.py:37
  83.0 6.0 %collective-permute-start.29 = (bf16[8,768]{1,0:T(8,128)(2,1)S(1)}, bf16[8,768]{1,0:T(8,128)(2,1)S(1)}, u32[]{:S(2)}, u32[]{:S(2)}) collective-permute-start(bf16[8,768]{1,0:T(8,128)(2,1)S(1)} %get-tuple-element.76), channel_id=1, source_target_pairs={{0,12},{4,8},{8,4},{12,0},{1,13},{5,9},{9,5},{13,1},{2,14},{6,10},... | collective-permute-start | bytes 36872 | tf_op jit(solution)/shard_map/ppermute | solution.py:37
  83.1 8.3 %collective-permute-start.15 = (bf16[8,768]{1,0:T(8,128)(2,1)S(1)}, bf16[8,768]{1,0:T(8,128)(2,1)S(1)}, u32[]{:S(2)}, u32[]{:S(2)}) collective-permute-start(bf16[8,768]{1,0:T(8,128)(2,1)S(1)} %get-tuple-element.69), channel_id=1, source_target_pairs={{0,4},{4,0},{8,12},{12,8},{1,5},{5,1},{9,13},{13,9},{2,6},{6,2},{1... | collective-permute-start | bytes 36872 | tf_op jit(solution)/shard_map/ppermute | solution.py:37
  83.6 8.3 %collective-permute-start.16 = (bf16[8,768]{1,0:T(8,128)(2,1)S(1)}, bf16[8,768]{1,0:T(8,128)(2,1)S(1)}, u32[]{:S(2)}, u32[]{:S(2)}) collective-permute-start(bf16[8,768]{1,0:T(8,128)(2,1)S(1)} %get-tuple-element.71), channel_id=1, source_target_pairs={{0,8},{4,12},{8,0},{12,4},{1,9},{5,13},{9,1},{13,5},{2,10},{6,14},... | collective-permute-start | bytes 36872 | tf_op jit(solution)/shard_map/ppermute | solution.py:37
  87.4 6.0 %collective-permute-start.17 = (bf16[8,768]{1,0:T(8,128)(2,1)S(1)}, bf16[8,768]{1,0:T(8,128)(2,1)S(1)}, u32[]{:S(2)}, u32[]{:S(2)}) collective-permute-start(bf16[8,768]{1,0:T(8,128)(2,1)S(1)} %get-tuple-element.70), channel_id=1, source_target_pairs={{0,12},{4,8},{8,4},{12,0},{1,13},{5,9},{9,5},{13,1},{2,14},{6,10},... | collective-permute-start | bytes 36872 | tf_op jit(solution)/shard_map/ppermute | solution.py:37
  87.5 7.9 %collective-permute-start.10 = (bf16[8,768]{1,0:T(8,128)(2,1)S(1)}, bf16[8,768]{1,0:T(8,128)(2,1)S(1)}, u32[]{:S(2)}, u32[]{:S(2)}) collective-permute-start(bf16[8,768]{1,0:T(8,128)(2,1)S(1)} %get-tuple-element.68), channel_id=1, source_target_pairs={{0,8},{4,12},{8,0},{12,4},{1,9},{5,13},{9,1},{13,5},{2,10},{6,14},... | collective-permute-start | bytes 36872 | tf_op jit(solution)/shard_map/ppermute | solution.py:37
  89.0 7.4 %collective-permute-start.11 = (bf16[8,768]{1,0:T(8,128)(2,1)S(1)}, bf16[8,768]{1,0:T(8,128)(2,1)S(1)}, u32[]{:S(2)}, u32[]{:S(2)}) collective-permute-start(bf16[8,768]{1,0:T(8,128)(2,1)S(1)} %get-tuple-element.67), channel_id=1, source_target_pairs={{0,12},{4,8},{8,4},{12,0},{1,13},{5,9},{9,5},{13,1},{2,14},{6,10},... | collective-permute-start | bytes 36872 | tf_op jit(solution)/shard_map/ppermute | solution.py:37
  91.3 5.1 %collective-permute-start.9 = (bf16[8,768]{1,0:T(8,128)(2,1)S(1)}, bf16[8,768]{1,0:T(8,128)(2,1)S(1)}, u32[]{:S(2)}, u32[]{:S(2)}) collective-permute-start(bf16[8,768]{1,0:T(8,128)(2,1)S(1)} %get-tuple-element.66), channel_id=1, source_target_pairs={{0,4},{4,0},{8,12},{12,8},{1,5},{5,1},{9,13},{13,9},{2,6},{6,2},{1... | collective-permute-start | bytes 36872 | tf_op jit(solution)/shard_map/ppermute | solution.py:37
  91.9 8.0 %collective-permute-start.24 = (bf16[8,768]{1,0:T(8,128)(2,1)S(1)}, bf16[8,768]{1,0:T(8,128)(2,1)S(1)}, u32[]{:S(2)}, u32[]{:S(2)}) collective-permute-start(bf16[8,768]{1,0:T(8,128)(2,1)S(1)} %add_convert_fusion.9), channel_id=1, source_target_pairs={{0,4},{4,0},{8,12},{12,8},{1,5},{5,1},{9,13},{13,9},{2,6},{6,2},{1... | collective-permute-start | bytes 36872 | tf_op jit(solution)/shard_map/ppermute | solution.py:37
  93.4 7.4 %collective-permute-start.25 = (bf16[8,768]{1,0:T(8,128)(2,1)S(1)}, bf16[8,768]{1,0:T(8,128)(2,1)S(1)}, u32[]{:S(2)}, u32[]{:S(2)}) collective-permute-start(bf16[8,768]{1,0:T(8,128)(2,1)S(1)} %add_convert_fusion.9), channel_id=1, source_target_pairs={{0,8},{4,12},{8,0},{12,4},{1,9},{5,13},{9,1},{13,5},{2,10},{6,14},... | collective-permute-start | bytes 36872 | tf_op jit(solution)/shard_map/ppermute | solution.py:37
  95.4 5.5 %collective-permute-start.26 = (bf16[8,768]{1,0:T(8,128)(2,1)S(1)}, bf16[8,768]{1,0:T(8,128)(2,1)S(1)}, u32[]{:S(2)}, u32[]{:S(2)}) collective-permute-start(bf16[8,768]{1,0:T(8,128)(2,1)S(1)} %add_convert_fusion.9), channel_id=1, source_target_pairs={{0,12},{4,8},{8,4},{12,0},{1,13},{5,9},{9,5},{13,1},{2,14},{6,10},... | collective-permute-start | bytes 36872 | tf_op jit(solution)/shard_map/ppermute | solution.py:37
  96.4 7.9 %collective-permute-start.12 = (bf16[8,768]{1,0:T(8,128)(2,1)S(1)}, bf16[8,768]{1,0:T(8,128)(2,1)S(1)}, u32[]{:S(2)}, u32[]{:S(2)}) collective-permute-start(bf16[8,768]{1,0:T(8,128)(2,1)S(1)} %get-tuple-element.63), channel_id=1, source_target_pairs={{0,4},{4,0},{8,12},{12,8},{1,5},{5,1},{9,13},{13,9},{2,6},{6,2},{1... | collective-permute-start | bytes 36872 | tf_op jit(solution)/shard_map/ppermute | solution.py:37
  97.0 8.2 %collective-permute-start.13 = (bf16[8,768]{1,0:T(8,128)(2,1)S(1)}, bf16[8,768]{1,0:T(8,128)(2,1)S(1)}, u32[]{:S(2)}, u32[]{:S(2)}) collective-permute-start(bf16[8,768]{1,0:T(8,128)(2,1)S(1)} %get-tuple-element.63), channel_id=1, source_target_pairs={{0,8},{4,12},{8,0},{12,4},{1,9},{5,13},{9,1},{13,5},{2,10},{6,14},... | collective-permute-start | bytes 36872 | tf_op jit(solution)/shard_map/ppermute | solution.py:37
  99.9 5.5 %collective-permute-start.14 = (bf16[8,768]{1,0:T(8,128)(2,1)S(1)}, bf16[8,768]{1,0:T(8,128)(2,1)S(1)}, u32[]{:S(2)}, u32[]{:S(2)}) collective-permute-start(bf16[8,768]{1,0:T(8,128)(2,1)S(1)} %get-tuple-element.63), channel_id=1, source_target_pairs={{0,12},{4,8},{8,4},{12,0},{1,13},{5,9},{9,5},{13,1},{2,14},{6,10},... | collective-permute-start | bytes 36872 | tf_op jit(solution)/shard_map/ppermute | solution.py:37
  100.9 7.8 %collective-permute-start.18 = (bf16[8,768]{1,0:T(8,128)(2,1)S(1)}, bf16[8,768]{1,0:T(8,128)(2,1)S(1)}, u32[]{:S(2)}, u32[]{:S(2)}) collective-permute-start(bf16[8,768]{1,0:T(8,128)(2,1)S(1)} %get-tuple-element.64), channel_id=1, source_target_pairs={{0,4},{4,0},{8,12},{12,8},{1,5},{5,1},{9,13},{13,9},{2,6},{6,2},{1... | collective-permute-start | bytes 36872 | tf_op jit(solution)/shard_map/ppermute | solution.py:37
  100.9 8.8 %collective-permute-start.19 = (bf16[8,768]{1,0:T(8,128)(2,1)S(1)}, bf16[8,768]{1,0:T(8,128)(2,1)S(1)}, u32[]{:S(2)}, u32[]{:S(2)}) collective-permute-start(bf16[8,768]{1,0:T(8,128)(2,1)S(1)} %get-tuple-element.64), channel_id=1, source_target_pairs={{0,8},{4,12},{8,0},{12,4},{1,9},{5,13},{9,1},{13,5},{2,10},{6,14},... | collective-permute-start | bytes 36872 | tf_op jit(solution)/shard_map/ppermute | solution.py:37
  104.3 5.5 %collective-permute-start.20 = (bf16[8,768]{1,0:T(8,128)(2,1)S(1)}, bf16[8,768]{1,0:T(8,128)(2,1)S(1)}, u32[]{:S(2)}, u32[]{:S(2)}) collective-permute-start(bf16[8,768]{1,0:T(8,128)(2,1)S(1)} %get-tuple-element.64), channel_id=1, source_target_pairs={{0,12},{4,8},{8,4},{12,0},{1,13},{5,9},{9,5},{13,1},{2,14},{6,10},... | collective-permute-start | bytes 36872 | tf_op jit(solution)/shard_map/ppermute | solution.py:37
  105.3 4.5 %collective-permute-start.30 = (bf16[8,768]{1,0:T(8,128)(2,1)S(1)}, bf16[8,768]{1,0:T(8,128)(2,1)S(1)}, u32[]{:S(2)}, u32[]{:S(2)}) collective-permute-start(bf16[8,768]{1,0:T(8,128)(2,1)S(1)} %get-tuple-element.65), channel_id=1, source_target_pairs={{0,4},{4,0},{8,12},{12,8},{1,5},{5,1},{9,13},{13,9},{2,6},{6,2},{1... | collective-permute-start | bytes 36872 | tf_op jit(solution)/shard_map/ppermute | solution.py:37
  105.4 5.0 %collective-permute-start.31 = (bf16[8,768]{1,0:T(8,128)(2,1)S(1)}, bf16[8,768]{1,0:T(8,128)(2,1)S(1)}, u32[]{:S(2)}, u32[]{:S(2)}) collective-permute-start(bf16[8,768]{1,0:T(8,128)(2,1)S(1)} %get-tuple-element.65), channel_id=1, source_target_pairs={{0,8},{4,12},{8,0},{12,4},{1,9},{5,13},{9,1},{13,5},{2,10},{6,14},... | collective-permute-start | bytes 36872 | tf_op jit(solution)/shard_map/ppermute | solution.py:37
  108.7 5.5 %collective-permute-start.32 = (bf16[8,768]{1,0:T(8,128)(2,1)S(1)}, bf16[8,768]{1,0:T(8,128)(2,1)S(1)}, u32[]{:S(2)}, u32[]{:S(2)}) collective-permute-start(bf16[8,768]{1,0:T(8,128)(2,1)S(1)} %get-tuple-element.65), channel_id=1, source_target_pairs={{0,12},{4,8},{8,4},{12,0},{1,13},{5,9},{9,5},{13,1},{2,14},{6,10},... | collective-permute-start | bytes 36872 | tf_op jit(solution)/shard_map/ppermute | solution.py:37
  115.9 12.4 %collective-permute-start.33 = (bf16[32,1536]{1,0:T(8,128)(2,1)S(1)}, bf16[32,1536]{1,0:T(8,128)(2,1)S(1)}, u32[]{:S(2)}, u32[]{:S(2)}) collective-permute-start(bf16[32,1536]{1,0:T(8,128)(2,1)S(1)} %up_t0.3.refs_2_), channel_id=1, source_target_pairs={{0,1},{1,0},{2,3},{3,2},{4,5},{5,4},{6,7},{7,6},{8,9},{9,8},{10,11... | collective-permute-start | bytes 294920 | tf_op jit(solution)/shard_map/ppermute | solution.py:37
  119.5 10.4 %collective-permute-start.35 = (bf16[32,1536]{1,0:T(8,128)(2,1)S(1)}, bf16[32,1536]{1,0:T(8,128)(2,1)S(1)}, u32[]{:S(2)}, u32[]{:S(2)}) collective-permute-start(bf16[32,1536]{1,0:T(8,128)(2,1)S(1)} %up_t1.3.refs_2_), channel_id=1, source_target_pairs={{0,1},{1,0},{2,3},{3,2},{4,5},{5,4},{6,7},{7,6},{8,9},{9,8},{10,11... | collective-permute-start | bytes 294920 | tf_op jit(solution)/shard_map/ppermute | solution.py:37
  128.4 5.6 %collective-permute-start.34 = (bf16[32,1536]{1,0:T(8,128)(2,1)S(1)}, bf16[32,1536]{1,0:T(8,128)(2,1)S(1)}, u32[]{:S(2)}, u32[]{:S(2)}) collective-permute-start(bf16[32,1536]{1,0:T(8,128)(2,1)S(1)} %add_convert_fusion.1), channel_id=1, source_target_pairs={{0,2},{1,3},{2,0},{3,1},{4,6},{5,7},{6,4},{7,5},{8,10},{9,11},{10,... | collective-permute-start | bytes 294920 | tf_op jit(solution)/shard_map/ppermute | solution.py:37
  130.0 5.3 %collective-permute-start.36 = (bf16[32,1536]{1,0:T(8,128)(2,1)S(1)}, bf16[32,1536]{1,0:T(8,128)(2,1)S(1)}, u32[]{:S(2)}, u32[]{:S(2)}) collective-permute-start(bf16[32,1536]{1,0:T(8,128)(2,1)S(1)} %add_convert_fusion), channel_id=1, source_target_pairs={{0,2},{1,3},{2,0},{3,1},{4,6},{5,7},{6,4},{7,5},{8,10},{9,11},{10,... | collective-permute-start | bytes 294920 | tf_op jit(solution)/shard_map/ppermute | solution.py:37
  141.9 7.8 %collective-permute-start.39 = (bf16[8,768]{1,0:T(8,128)(2,1)S(1)}, bf16[8,768]{1,0:T(8,128)(2,1)S(1)}, u32[]{:S(2)}, u32[]{:S(2)}) collective-permute-start(bf16[8,768]{1,0:T(8,128)(2,1)S(1)} %get-tuple-element.51), channel_id=1, source_target_pairs={{0,4},{4,0},{8,12},{12,8},{1,5},{5,1},{9,13},{13,9},{2,6},{6,2},{1... | collective-permute-start | bytes 36872 | tf_op jit(solution)/shard_map/ppermute | solution.py:37
  142.0 10.6 %collective-permute-start.40 = (bf16[8,768]{1,0:T(8,128)(2,1)S(1)}, bf16[8,768]{1,0:T(8,128)(2,1)S(1)}, u32[]{:S(2)}, u32[]{:S(2)}) collective-permute-start(bf16[8,768]{1,0:T(8,128)(2,1)S(1)} %get-tuple-element.53), channel_id=1, source_target_pairs={{0,8},{4,12},{8,0},{12,4},{1,9},{5,13},{9,1},{13,5},{2,10},{6,14},... | collective-permute-start | bytes 36872 | tf_op jit(solution)/shard_map/ppermute | solution.py:37
  143.5 9.1 %collective-permute-start.41 = (bf16[8,768]{1,0:T(8,128)(2,1)S(1)}, bf16[8,768]{1,0:T(8,128)(2,1)S(1)}, u32[]{:S(2)}, u32[]{:S(2)}) collective-permute-start(bf16[8,768]{1,0:T(8,128)(2,1)S(1)} %get-tuple-element.52), channel_id=1, source_target_pairs={{0,12},{4,8},{8,4},{12,0},{1,13},{5,9},{9,5},{13,1},{2,14},{6,10},... | collective-permute-start | bytes 36872 | tf_op jit(solution)/shard_map/ppermute | solution.py:37
  148.1 6.0 %collective-permute-start.42 = (bf16[8,768]{1,0:T(8,128)(2,1)S(1)}, bf16[8,768]{1,0:T(8,128)(2,1)S(1)}, u32[]{:S(2)}, u32[]{:S(2)}) collective-permute-start(bf16[8,768]{1,0:T(8,128)(2,1)S(1)} %get-tuple-element.54), channel_id=1, source_target_pairs={{0,4},{4,0},{8,12},{12,8},{1,5},{5,1},{9,13},{13,9},{2,6},{6,2},{1... | collective-permute-start | bytes 36872 | tf_op jit(solution)/shard_map/ppermute | solution.py:37
  148.2 8.9 %collective-permute-start.43 = (bf16[8,768]{1,0:T(8,128)(2,1)S(1)}, bf16[8,768]{1,0:T(8,128)(2,1)S(1)}, u32[]{:S(2)}, u32[]{:S(2)}) collective-permute-start(bf16[8,768]{1,0:T(8,128)(2,1)S(1)} %get-tuple-element.56), channel_id=1, source_target_pairs={{0,8},{4,12},{8,0},{12,4},{1,9},{5,13},{9,1},{13,5},{2,10},{6,14},... | collective-permute-start | bytes 36872 | tf_op jit(solution)/shard_map/ppermute | solution.py:37
  149.7 7.4 %collective-permute-start.44 = (bf16[8,768]{1,0:T(8,128)(2,1)S(1)}, bf16[8,768]{1,0:T(8,128)(2,1)S(1)}, u32[]{:S(2)}, u32[]{:S(2)}) collective-permute-start(bf16[8,768]{1,0:T(8,128)(2,1)S(1)} %get-tuple-element.55), channel_id=1, source_target_pairs={{0,12},{4,8},{8,4},{12,0},{1,13},{5,9},{9,5},{13,1},{2,14},{6,10},... | collective-permute-start | bytes 36872 | tf_op jit(solution)/shard_map/ppermute | solution.py:37
  152.6 6.0 %collective-permute-start.45 = (bf16[8,768]{1,0:T(8,128)(2,1)S(1)}, bf16[8,768]{1,0:T(8,128)(2,1)S(1)}, u32[]{:S(2)}, u32[]{:S(2)}) collective-permute-start(bf16[8,768]{1,0:T(8,128)(2,1)S(1)} %get-tuple-element.57), channel_id=1, source_target_pairs={{0,4},{4,0},{8,12},{12,8},{1,5},{5,1},{9,13},{13,9},{2,6},{6,2},{1... | collective-permute-start | bytes 36872 | tf_op jit(solution)/shard_map/ppermute | solution.py:37
  152.6 9.0 %collective-permute-start.46 = (bf16[8,768]{1,0:T(8,128)(2,1)S(1)}, bf16[8,768]{1,0:T(8,128)(2,1)S(1)}, u32[]{:S(2)}, u32[]{:S(2)}) collective-permute-start(bf16[8,768]{1,0:T(8,128)(2,1)S(1)} %get-tuple-element.59), channel_id=1, source_target_pairs={{0,8},{4,12},{8,0},{12,4},{1,9},{5,13},{9,1},{13,5},{2,10},{6,14},... | collective-permute-start | bytes 36872 | tf_op jit(solution)/shard_map/ppermute | solution.py:37
  154.1 7.4 %collective-permute-start.47 = (bf16[8,768]{1,0:T(8,128)(2,1)S(1)}, bf16[8,768]{1,0:T(8,128)(2,1)S(1)}, u32[]{:S(2)}, u32[]{:S(2)}) collective-permute-start(bf16[8,768]{1,0:T(8,128)(2,1)S(1)} %get-tuple-element.58), channel_id=1, source_target_pairs={{0,12},{4,8},{8,4},{12,0},{1,13},{5,9},{9,5},{13,1},{2,14},{6,10},... | collective-permute-start | bytes 36872 | tf_op jit(solution)/shard_map/ppermute | solution.py:37
  157.1 4.5 %collective-permute-start.48 = (bf16[8,768]{1,0:T(8,128)(2,1)S(1)}, bf16[8,768]{1,0:T(8,128)(2,1)S(1)}, u32[]{:S(2)}, u32[]{:S(2)}) collective-permute-start(bf16[8,768]{1,0:T(8,128)(2,1)S(1)} %get-tuple-element.60), channel_id=1, source_target_pairs={{0,4},{4,0},{8,12},{12,8},{1,5},{5,1},{9,13},{13,9},{2,6},{6,2},{1... | collective-permute-start | bytes 36872 | tf_op jit(solution)/shard_map/ppermute | solution.py:37
  157.1 4.7 %collective-permute-start.49 = (bf16[8,768]{1,0:T(8,128)(2,1)S(1)}, bf16[8,768]{1,0:T(8,128)(2,1)S(1)}, u32[]{:S(2)}, u32[]{:S(2)}) collective-permute-start(bf16[8,768]{1,0:T(8,128)(2,1)S(1)} %get-tuple-element.62), channel_id=1, source_target_pairs={{0,8},{4,12},{8,0},{12,4},{1,9},{5,13},{9,1},{13,5},{2,10},{6,14},... | collective-permute-start | bytes 36872 | tf_op jit(solution)/shard_map/ppermute | solution.py:37
  158.6 5.6 %collective-permute-start.50 = (bf16[8,768]{1,0:T(8,128)(2,1)S(1)}, bf16[8,768]{1,0:T(8,128)(2,1)S(1)}, u32[]{:S(2)}, u32[]{:S(2)}) collective-permute-start(bf16[8,768]{1,0:T(8,128)(2,1)S(1)} %get-tuple-element.61), channel_id=1, source_target_pairs={{0,12},{4,8},{8,4},{12,0},{1,13},{5,9},{9,5},{13,1},{2,14},{6,10},... | collective-permute-start | bytes 36872 | tf_op jit(solution)/shard_map/ppermute | solution.py:37
  (15 other events, 64.9 us)

commit v2 on v0

v2 whole, which is shorter than its diff:
```python
import jax
import jax.numpy as jnp
from jax import lax
from jax.experimental import pallas as pl
from jax.experimental.pallas import tpu as pltpu
from jax.sharding import PartitionSpec as P

STEPS = 2
PIECES = 2
BLOCKS = 2
bf16, f32 = jnp.bfloat16, jnp.float32


def plain(tokens, w_in, w_out):
    row_dev = tokens.shape[0]
    where = lax.axis_index("hidden")
    full = lax.all_gather(tokens, "hidden", axis=0, tiled=True)
    latest = tokens
    for step in range(STEPS):
        pre = jnp.dot(full, w_in, preferred_element_type=f32)
        summed = lax.psum(pre.astype(bf16), "width").astype(f32)
        activ = jax.nn.gelu(summed, approximate=True).astype(bf16)
        mine_sum = lax.psum_scatter(
            jnp.dot(activ, w_out, preferred_element_type=f32).astype(bf16),
            "hidden",
            scatter_dimension=0,
            tiled=True,
        ).astype(f32)
        mine_old = lax.dynamic_slice_in_dim(full, where * row_dev, row_dev, 0)
        latest = (mine_old.astype(f32) + mine_sum).astype(bf16)
        if step + 1 < STEPS:
            full = lax.all_gather(latest, "hidden", axis=0, tiled=True)
    return latest


def swap(x, axis, n, mask):
    return lax.ppermute(x, axis, [(i, i ^ mask) for i in range(n)])


def stage(products, loads, name, behind=(), add=None, dtype=bf16):
    arrays = []
    for array, _, _ in loads:
        if not any(array is a for a in arrays):
            arrays.append(array)
    given = [a for x, w in products for a in (x, *w)] + ([] if add is None else [add])
    n_g, n_a, n_l = len(given), len(arrays), BLOCKS * len(loads)
    which = [next(i for i, a in enumerate(arrays) if a is array) for array, _, _ in loads]
    width = w_width = 0
    if products:
        w_width = products[0][1][0].shape[1]
        width = BLOCKS * w_width

    def kernel(*refs):
        refs_in, hbm = refs[:n_g], refs[n_g : n_g + n_a]
        out = refs[n_g + n_a + len(behind) :]
        result = out[0] if products else None
        out = out[1:] if products else out
        held, sems = out[:n_l], out[n_l:]
        core = lax.rem(lax.axis_index("width"), 2)
        copies = []
        for i, (array, rows, cols) in enumerate(loads):
            size = cols[0] // BLOCKS
            for b in range(BLOCKS):
                index = []
                for (extent, start, per), full in zip((rows, (size, cols[1] + b * size, cols[2])), array.shape):
                    if per:
                        half = core if per > 0 else 1 - core
                        start = pl.multiple_of(half * (full // 2) + start, 128)
                    index.append(pl.ds(start, extent))
                slot = i * BLOCKS + b
                copies.append(pltpu.make_async_copy(hbm[which[i]].at[tuple(index)], held[slot], sems[0].at[slot]))
        for copy in copies:
            copy.start()
        if products:

            @pl.when(core < 2)
            def _():
                for b in range(BLOCKS):
                    columns = slice(b * w_width, (b + 1) * w_width)
                    total = None if add is None else refs_in[-1][:, columns]
                    for p in range(len(products)):
                        x, w = refs_in[p * (1 + BLOCKS)], refs_in[p * (1 + BLOCKS) + 1 + b]
                        part = jnp.dot(x[...], w[...], preferred_element_type=f32)
                        total = part if total is None else total + part
                    result[:, columns] = total.astype(result.dtype)

        for copy in copies:
            copy.wait()

    shapes = [pltpu.VMEM((r[0], c[0] // BLOCKS), a.dtype) for a, r, c in loads for _ in range(BLOCKS)]
    if products:
        shapes = [jax.ShapeDtypeStruct((given[0].shape[0], width), dtype)] + shapes
    vmem, hbm, anywhere = (pl.BlockSpec(memory_space=m) for m in (pltpu.VMEM, pltpu.HBM, pl.ANY))
    got = pl.pallas_call(
        kernel,
        out_shape=shapes,
        in_specs=[vmem] * n_g + [hbm] * n_a + [anywhere] * len(behind),
        out_specs=[vmem] * len(shapes),
        scratch_shapes=[pltpu.SemaphoreType.DMA((n_l,))] if loads else [],
        compiler_params=pltpu.CompilerParams(vmem_limit_bytes=2 * 2**20),
        cost_estimate=pl.CostEstimate(flops=1000, bytes_accessed=1000, transcendentals=0),
        name=name,
    )(*given, *[pltpu.with_memory_space_constraint(a, pltpu.HBM) for a in arrays], *behind)
    result, blocks = (got[0], got[1:]) if products else (None, got)
    return result, [list(blocks[i * BLOCKS : (i + 1) * BLOCKS]) for i in range(len(loads))]


def gather(block, nz):
    return jnp.concatenate([block] + [swap(block, "hidden", nz, k) for k in range(1, nz)], 0)


def tuned(nz, nw, tokens, w_in, w_out):
    rows, d = tokens.shape
    f = w_in.shape[1]
    piece = f // 2 // PIECES

    def up(j, per):
        return (w_in, (d, 0, 0), (piece, j * piece, per))

    def down(j, per):
        return (w_out, (piece, j * piece, per), (d, 0, 0))

    def chip_sum(sent, kept):
        return (kept.astype(f32) + swap(sent, "width", nw, 1).astype(f32)).astype(bf16)

    def activation(chip):
        total = chip.astype(f32) + swap(chip, "width", nw, 2).astype(f32)
        return jax.nn.gelu(total, approximate=True).astype(bf16)

    def scattered(part, old):
        total = part[:rows].astype(f32)
        for k in range(nz - 1, 0, -1):
            total = total + swap(part[k * rows : (k + 1) * rows], "hidden", nz, k).astype(f32)
        return (old.astype(f32) + total).astype(bf16)

    state = tokens
    x = gather(state, nz)
    _, (t0,) = stage([], [up(0, -1)], "load_t0")
    s_t0, (m0,) = stage([(x, t0)], [up(0, 1)], "up_t0")
    s_m0, (t1,) = stage([(x, m0)], [up(1, -1)], "up_m0", [s_t0])
    c0 = chip_sum(s_t0, s_m0)
    s_t1, (m1,) = stage([(x, t1)], [up(1, 1)], "up_t1", [c0])
    s_m1, (d_m0, d_m1) = stage([(x, m1)], [down(0, 1), down(1, 1)], "up_m1", [s_t1])
    for step in range(STEPS):
        c1 = chip_sum(s_t1, s_m1)
        mine0 = activation(c0)
        q, (d_t0, d_t1) = stage([(mine0, d_m0)], [down(0, -1), down(1, -1)], "down_m0", [c1], None, f32)
        other0 = swap(mine0, "width", nw, 1)
        mine1 = activation(c1)
        q, _ = stage([(other0, d_t0), (mine1, d_m1)], [], "down_t0_m1", [], q, f32)
        other1 = swap(mine1, "width", nw, 1)
        q, _ = stage([(other1, d_t1)], [], "down_t1", [], q)
        if step + 1 < STEPS:
            _, (t0,) = stage([], [up(0, -1)], "load_t0", [q])
        state = scattered(q, state)
        if step + 1 < STEPS:
            _, (m0,) = stage([], [up(0, 1)], "load_m0", [state])
            x = gather(state, nz)
            s_t0, (t1,) = stage([(x, t0)], [up(1, -1)], "up_t0", [m0[0]])
            s_m0, (d_m0,) = stage([(x, m0)], [down(0, 1)], "up_m0", [s_t0])
            c0 = chip_sum(s_t0, s_m0)
            s_t1, (d_m1,) = stage([(x, t1)], [down(1, 1)], "up_t1", [c0])
            s_m1, _ = stage([(x, m1)], [], "up_m1", [s_t1])
    return state


def solution(mesh):
    placed = (P(("groups", "hidden"), "width"), P("width", "hidden"), P("hidden", "width"))
    nz, nw = mesh.shape["hidden"], mesh.shape["width"]

    def local(tokens, w_in, w_out):
        fits = nz == 4 and nw == 4 and w_in.shape[1] % (256 * PIECES) == 0
        return tuned(nz, nw, tokens, w_in, w_out) if fits else plain(tokens, w_in, w_out)

    return jax.shard_map(
        local,
        mesh=mesh,
        in_specs=placed,
        out_specs=P(("groups", "hidden"), "width"),
        check_vma=False,
    )
```

time: 213 us -> 109 us (0.51)
  waiting for transfers between devices: 104 us -> 16.4 us
  Pallas kernels: 0 us -> 65.6 us
  matrix products: 63.5 us -> 0 us
  blocking collectives: 29.2 us -> 0 us
  starting transfers between devices: 0.13 us -> 24.7 us
  between operations: 13.1 us -> 0.41 us
    pallas_call x0 -> x17, Pallas kernels: none -> 65.6 us  [stage(): pl.pallas_call(kernel, out_shape=shapes, in_specs=[vmem] * n_g + [hbm] *...]
    psum x2 -> x0, waiting for transfers between devices: 65.3 us -> none  [local(): summed = lax.psum(pre.astype(jnp.bfloat16), 'width').astype(jnp.float32)]
    dot_general x4 -> x0, matrix products: 63.5 us -> none  [the longest x2 31.8 us: local(): jnp.dot(activ, w_out, preferred_element_type=jnp.float32)]
    reduce_scatter x2 -> x0, waiting for transfers between devices: 39 us -> none  [local(): lax.psum_scatter(jnp.dot(activ, w_out, preferred_element_type=jnp.float32...]
    all_gather x2 -> x0, blocking collectives: 29.2 us -> none  [the longest x1 15.7 us: local(): full = lax.all_gather(tokens, 'hidden', axis=0, tiled=True)]
    ppermute x0 -> x24, starting transfers between devices: none -> 24.7 us  [swap(): return lax.ppermute(x, axis, [(i, i ^ mask) for i in range(n)])]
    ppermute x0 -> x24, waiting for transfers between devices: none -> 16.4 us  [swap(): return lax.ppermute(x, axis, [(i, i ^ mask) for i in range(n)])]
  transfers between devices with their start and end apart: 4 -> 24, of which waited for: 4 -> 9; matrix products, arithmetic and copies ran while one was open for 0% -> 1% of each run, Pallas kernels for 0% -> 43%
where the time goes in v2:
time: 109 us
  Pallas kernels  65.6 us (60%)
  starting transfers between devices  24.7 us (23%)
  waiting for transfers between devices  16.4 us (15%)
  other arithmetic  1.18 us (1%)
    pallas_call x17, Pallas kernels, stage(): pl.pallas_call(kernel, out_shape=shapes, in_specs=[vmem] * n_g + [hbm] *...  65.6 us
    ppermute x24, starting transfers between devices, swap(): return lax.ppermute(x, axis, [(i, i ^ mask) for i in range(n)])  24.7 us
    ppermute x24, waiting for transfers between devices, swap(): return lax.ppermute(x, axis, [(i, i ^ mask) for i in range(n)])  16.4 us
  transfers between devices with their start and end apart: 24, of which 9 were waited for; matrix products, arithmetic and copies ran while one was open for 1% of the time, Pallas kernels for 43%

profile of v2, /device:TPU:0, one launch (start us, length us, event | category | flops | bytes accessed | tf_op | source)
XLA Modules:
  0.0 109.3 jit_solution(7977733163663376495)
XLA Ops:
  0.0 3.0 %collective-permute-start = (bf16[8,3072]{1,0:T(8,128)(2,1)}, bf16[8,3072]{1,0:T(8,128)(2,1)S(1)}, u32[]{:S(2)}, u32[]{:S(2)}) collective-permute-start(bf16[8,3072]{1,0:T(8,128)(2,1)} %param.3), channel_id=1, source_target_pairs={{0,4},{4,0},{8,12},{12,8},{1,5},{5,1},{9,13},{13,9},{2,6},{6,2},{1... | collective-permute-start | bytes 147464 | tf_op jit(solution)/shard_map/ppermute | solution.py:37
  3.0 2.6 %collective-permute-start.1 = (bf16[8,3072]{1,0:T(8,128)(2,1)}, bf16[8,3072]{1,0:T(8,128)(2,1)S(1)}, u32[]{:S(2)}, u32[]{:S(2)}) collective-permute-start(bf16[8,3072]{1,0:T(8,128)(2,1)} %param.3), channel_id=1, source_target_pairs={{0,8},{4,12},{8,0},{12,4},{1,9},{5,13},{9,1},{13,5},{2,10},{6,14},... | collective-permute-start | bytes 147464 | tf_op jit(solution)/shard_map/ppermute | solution.py:37
  5.6 0.9 constant_dynamic-update-slice_fusion.3
  6.5 3.8 %load_t0.2 = (bf16[3072,768]{1,0:T(8,128)(2,1)S(1)}, bf16[3072,768]{1,0:T(8,128)(2,1)S(1)}) custom-call(bf16[3072,6144]{1,0:T(8,128)(2,1)} %refs_3_.14), custom_call_target="tpu_custom_call" | custom-call | flops 1000 | bytes 1000 | tf_op jit(solution)/shard_map/load_t0/pallas_call | solution.py:94
  10.3 1.4 %collective-permute-done.2 = bf16[8,3072]{1,0:T(8,128)(2,1)S(1)} collective-permute-done((bf16[8,3072]{1,0:T(8,128)(2,1)}, bf16[8,3072]{1,0:T(8,128)(2,1)S(1)}, u32[]{:S(2)}, u32[]{:S(2)}) %collective-permute-start.2) | collective-permute-done | bytes 49184 | tf_op jit(solution)/shard_map/ppermute | solution.py:37
  11.7 3.8 %up_t0.2 = (bf16[32,1536]{1,0:T(8,128)(2,1)S(1)}, bf16[3072,768]{1,0:T(8,128)(2,1)S(1)}, bf16[3072,768]{1,0:T(8,128)(2,1)S(1)}) custom-call(bf16[32,3072]{1,0:T(8,128)(2,1)S(1)} %constant_dynamic-update-slice_fusion.refs_0_, bf16[3072,768]{1,0:T(8,128)(2,1)S(1)} %get-tuple-element.44.refs_1_, bf16[3072,768]{1,0:T(8,128)(2,1)S(1)} %get-tuple-element.45.refs_2_, ...), custom_call_target="tpu_custom_call" | custom-call | flops 1000 | bytes 1000 | tf_op jit(solution)/shard_map/up_t0/pallas_call | solution.py:94
  15.5 0.1 collective-permute-start.3
  15.6 3.8 %up_m0.2 = (bf16[32,1536]{1,0:T(8,128)(2,1)S(1)}, bf16[3072,768]{1,0:T(8,128)(2,1)S(1)}, bf16[3072,768]{1,0:T(8,128)(2,1)S(1)}) custom-call(bf16[32,3072]{1,0:T(8,128)(2,1)S(1)} %constant_dynamic-update-slice_fusion.refs_0_, bf16[3072,768]{1,0:T(8,128)(2,1)S(1)} %get-tuple-element.46.refs_1_, bf16[3072,768]{1,0:T(8,128)(2,1)S(1)} %get-tuple-element.47.refs_2_, ...), custom_call_target="tpu_custom_call" | custom-call | flops 1000 | bytes 1000 | tf_op jit(solution)/shard_map/up_m0/pallas_call | solution.py:94
  19.5 3.8 %up_t1.2 = (bf16[32,1536]{1,0:T(8,128)(2,1)S(1)}, bf16[3072,768]{1,0:T(8,128)(2,1)S(1)}, bf16[3072,768]{1,0:T(8,128)(2,1)S(1)}) custom-call(bf16[32,3072]{1,0:T(8,128)(2,1)S(1)} %constant_dynamic-update-slice_fusion.refs_0_, bf16[3072,768]{1,0:T(8,128)(2,1)S(1)} %get-tuple-element.49.refs_1_, bf16[3072,768]{1,0:T(8,128)(2,1)S(1)} %get-tuple-element.50.refs_2_, ...), custom_call_target="tpu_custom_call" | custom-call | flops 1000 | bytes 1000 | tf_op jit(solution)/shard_map/up_t1/pallas_call | solution.py:94
  23.3 0.6 collective-permute-start.4
  23.9 1.5 %collective-permute-start.7 = (bf16[32,1536]{1,0:T(8,128)(2,1)S(1)}, bf16[32,1536]{1,0:T(8,128)(2,1)S(1)}, u32[]{:S(2)}, u32[]{:S(2)}) collective-permute-start(bf16[32,1536]{1,0:T(8,128)(2,1)S(1)} %add_convert_fusion.3.refs_4_), channel_id=1, source_target_pairs={{0,2},{1,3},{2,0},{3,1},{4,6},{5,7},{6,4},{7,5},{8,10},{9,11},{10,... | collective-permute-start | bytes 294920 | tf_op jit(solution)/shard_map/ppermute | solution.py:37
  25.4 6.5 %up_m1.2 = (bf16[32,1536]{1,0:T(8,128)(2,1)S(1)}, bf16[1536,1536]{1,0:T(8,128)(2,1)S(1)}, bf16[1536,1536]{1,0:T(8,128)(2,1)S(1)}, bf16[1536,1536]{1,0:T(8,128)(2,1)S(1)}, bf16[1536,1536]{1,0:T(8,128)(2,1)S(1)}) custom-call(bf16[32,3072]{1,0:T(8,128)(2,1)S(1)} %constant_dynamic-update-slice_fusion.refs_0_, bf16[3072,768]{1,0:T(8,128)(2,1)S(1)} %get-tuple-element.52.refs_1_, ...), custom_call_target="tpu_custom_call" | custom-call | flops 1000 | bytes 1000 | tf_op jit(solution)/shard_map/up_m1/pallas_call | solution.py:94
  31.9 0.6 collective-permute-start.5
  32.5 0.1 fusion.15.refs_0_
  32.7 3.9 %collective-permute-done.5 = bf16[32,1536]{1,0:T(8,128)(2,1)S(1)} collective-permute-done((bf16[32,1536]{1,0:T(8,128)(2,1)S(1)}, bf16[32,1536]{1,0:T(8,128)(2,1)S(1)}, u32[]{:S(2)}, u32[]{:S(2)}) %collective-permute-start.5) | collective-permute-done | bytes 98336 | tf_op jit(solution)/shard_map/ppermute | solution.py:37
  36.6 0.1 fusion.7.refs_3_
  36.8 6.5 %down_m0.2 = (f32[32,3072]{1,0:T(8,128)S(1)}, bf16[1536,1536]{1,0:T(8,128)(2,1)S(1)}, bf16[1536,1536]{1,0:T(8,128)(2,1)S(1)}, bf16[1536,1536]{1,0:T(8,128)(2,1)S(1)}, bf16[1536,1536]{1,0:T(8,128)(2,1)S(1)}) custom-call(bf16[32,1536]{1,0:T(8,128)(2,1)S(1)} %fusion.15.refs_0_, bf16[1536,1536]{1,0:T(8,128)(2,1)S(1)} %get-tuple-element.56.refs_1_, ...), custom_call_target="tpu_custom_call" | custom-call | flops 1000 | bytes 1000 | tf_op jit(solution)/shard_map/down_m0/pallas_call | solution.py:94
  43.3 3.3 %down_t0_m1.2.refs_3_ = f32[32,3072]{1,0:T(8,128)S(1)} custom-call(bf16[32,1536]{1,0:T(8,128)(2,1)S(1)} %collective-permute-done.8.refs_0_, bf16[1536,1536]{1,0:T(8,128)(2,1)S(1)} %get-tuple-element.60.refs_1_, bf16[1536,1536]{1,0:T(8,128)(2,1)S(1)} %get-tuple-element.61.refs_2_, bf16[32,1536]{1,0:T(8,128)(2,1)S(1)} %fusion.7.refs_3_, ...), custom_call_target="tpu_custom_call" | custom-call | flops 1000 | bytes 1000 | tf_op jit(solution)/shard_map/down_t0_m1/pallas_call | solution.py:94
  46.7 1.7 %down_t1.2.refs_1_ = bf16[32,3072]{1,0:T(8,128)(2,1)S(1)} custom-call(bf16[32,1536]{1,0:T(8,128)(2,1)S(1)} %collective-permute-done.6.refs_0_, bf16[1536,1536]{1,0:T(8,128)(2,1)S(1)} %get-tuple-element.58.refs_1_, bf16[1536,1536]{1,0:T(8,128)(2,1)S(1)} %get-tuple-element.59.refs_2_, f32[32,3072]{1,0:T(8,128)S(1)} %down_t0_m1.2.refs_3_), custom_call_target="tpu_custom_call" | custom-call | flops 1000 | bytes 1000 | tf_op jit(solution)/shard_map/down_t1/pallas_call | solution.py:94
  48.4 0.6 collective-permute-start.10
  49.0 2.5 %collective-permute-start.11 = (bf16[8,3072]{1,0:T(8,128)(2,1)S(1)}, bf16[8,3072]{1,0:T(8,128)(2,1)S(1)}, u32[]{:S(2)}, u32[]{:S(2)}) collective-permute-start(bf16[8,3072]{1,0:T(8,128)(2,1)S(1)} %get-tuple-element.87), channel_id=1, source_target_pairs={{0,4},{4,0},{8,12},{12,8},{1,5},{5,1},{9,13},{13,9},{2,6},{6,2},{1... | collective-permute-start | bytes 147464 | tf_op jit(solution)/shard_map/ppermute | solution.py:37
  51.5 1.4 %collective-permute-start.9 = (bf16[8,3072]{1,0:T(8,128)(2,1)S(1)}, bf16[8,3072]{1,0:T(8,128)(2,1)S(1)}, u32[]{:S(2)}, u32[]{:S(2)}) collective-permute-start(bf16[8,3072]{1,0:T(8,128)(2,1)S(1)} %get-tuple-element.86), channel_id=1, source_target_pairs={{0,12},{4,8},{8,4},{12,0},{1,13},{5,9},{9,5},{13,1},{2,14},{6,10},... | collective-permute-start | bytes 147464 | tf_op jit(solution)/shard_map/ppermute | solution.py:37
  52.8 1.6 %collective-permute-done.10 = bf16[8,3072]{1,0:T(8,128)(2,1)S(1)} collective-permute-done((bf16[8,3072]{1,0:T(8,128)(2,1)S(1)}, bf16[8,3072]{1,0:T(8,128)(2,1)S(1)}, u32[]{:S(2)}, u32[]{:S(2)}) %collective-permute-start.10) | collective-permute-done | bytes 49184 | tf_op jit(solution)/shard_map/ppermute | solution.py:37
  54.5 0.2 collective-permute-done.11
  54.6 2.7 %collective-permute-done.9 = bf16[8,3072]{1,0:T(8,128)(2,1)S(1)} collective-permute-done((bf16[8,3072]{1,0:T(8,128)(2,1)S(1)}, bf16[8,3072]{1,0:T(8,128)(2,1)S(1)}, u32[]{:S(2)}, u32[]{:S(2)}) %collective-permute-start.9) | collective-permute-done | bytes 49184 | tf_op jit(solution)/shard_map/ppermute | solution.py:37
  57.5 1.9 %collective-permute-start.13 = (bf16[8,3072]{1,0:T(8,128)(2,1)S(1)}, bf16[8,3072]{1,0:T(8,128)(2,1)S(1)}, u32[]{:S(2)}, u32[]{:S(2)}) collective-permute-start(bf16[8,3072]{1,0:T(8,128)(2,1)S(1)} %add_convert_fusion.5.refs_1_), channel_id=1, source_target_pairs={{0,8},{4,12},{8,0},{12,4},{1,9},{5,13},{9,1},{13,5},{2,10},{6,14},... | collective-permute-start | bytes 147464 | tf_op jit(solution)/shard_map/ppermute | solution.py:37
  59.4 2.4 %collective-permute-start.14 = (bf16[8,3072]{1,0:T(8,128)(2,1)S(1)}, bf16[8,3072]{1,0:T(8,128)(2,1)S(1)}, u32[]{:S(2)}, u32[]{:S(2)}) collective-permute-start(bf16[8,3072]{1,0:T(8,128)(2,1)S(1)} %add_convert_fusion.5.refs_1_), channel_id=1, source_target_pairs={{0,12},{4,8},{8,4},{12,0},{1,13},{5,9},{9,5},{13,1},{2,14},{6,10},... | collective-permute-start | bytes 147464 | tf_op jit(solution)/shard_map/ppermute | solution.py:37
  61.9 3.8 %load_t0.3 = (bf16[3072,768]{1,0:T(8,128)(2,1)S(1)}, bf16[3072,768]{1,0:T(8,128)(2,1)S(1)}) custom-call(bf16[3072,6144]{1,0:T(8,128)(2,1)} %refs_3_.14, bf16[32,3072]{1,0:T(8,128)(2,1)S(1)} %down_t1.2.refs_1_), custom_call_target="tpu_custom_call" | custom-call | flops 1000 | bytes 1000 | tf_op jit(solution)/shard_map/load_t0/pallas_call | solution.py:94
  65.7 3.8 %load_m0.1 = (bf16[3072,768]{1,0:T(8,128)(2,1)S(1)}, bf16[3072,768]{1,0:T(8,128)(2,1)S(1)}) custom-call(bf16[3072,6144]{1,0:T(8,128)(2,1)} %refs_3_.14, bf16[8,3072]{1,0:T(8,128)(2,1)S(1)} %add_convert_fusion.5.refs_1_), custom_call_target="tpu_custom_call" | custom-call | flops 1000 | bytes 1000 | tf_op jit(solution)/shard_map/load_m0/pallas_call | solution.py:94
  69.5 3.8 %up_t0.3 = (bf16[32,1536]{1,0:T(8,128)(2,1)S(1)}, bf16[3072,768]{1,0:T(8,128)(2,1)S(1)}, bf16[3072,768]{1,0:T(8,128)(2,1)S(1)}) custom-call(bf16[32,3072]{1,0:T(8,128)(2,1)S(1)} %pad_maximum_fusion.refs_0_, bf16[3072,768]{1,0:T(8,128)(2,1)S(1)} %get-tuple-element.65.refs_1_, bf16[3072,768]{1,0:T(8,128)(2,1)S(1)} %get-tuple-element.66.refs_2_, ...), custom_call_target="tpu_custom_call" | custom-call | flops 1000 | bytes 1000 | tf_op jit(solution)/shard_map/up_t0/pallas_call | solution.py:94
  73.5 3.8 %up_m0.3 = (bf16[32,1536]{1,0:T(8,128)(2,1)S(1)}, bf16[1536,1536]{1,0:T(8,128)(2,1)S(1)}, bf16[1536,1536]{1,0:T(8,128)(2,1)S(1)}) custom-call(bf16[32,3072]{1,0:T(8,128)(2,1)S(1)} %pad_maximum_fusion.refs_0_, bf16[3072,768]{1,0:T(8,128)(2,1)S(1)} %get-tuple-element.67.refs_4_.refs_1_, bf16[3072,768]{1,0:T(8,128)(2,1)S(1)} %get-tuple-element.70.refs_2_, ...), custom_call_target="tpu_custom_call" | custom-call | flops 1000 | bytes 1000 | tf_op jit(solution)/shard_map/up_m0/pallas_call | solution.py:94
  77.3 3.8 %up_t1.3 = (bf16[32,1536]{1,0:T(8,128)(2,1)S(1)}, bf16[1536,1536]{1,0:T(8,128)(2,1)S(1)}, bf16[1536,1536]{1,0:T(8,128)(2,1)S(1)}) custom-call(bf16[32,3072]{1,0:T(8,128)(2,1)S(1)} %pad_maximum_fusion.refs_0_, bf16[3072,768]{1,0:T(8,128)(2,1)S(1)} %get-tuple-element.68.refs_1_, bf16[3072,768]{1,0:T(8,128)(2,1)S(1)} %get-tuple-element.69.refs_2_, ...), custom_call_target="tpu_custom_call" | custom-call | flops 1000 | bytes 1000 | tf_op jit(solution)/shard_map/up_t1/pallas_call | solution.py:94
  81.1 0.6 collective-permute-start.16
  81.7 0.5 collective-permute-start.19
  82.2 1.7 %up_m1.3 = bf16[32,1536]{1,0:T(8,128)(2,1)S(1)} custom-call(bf16[32,3072]{1,0:T(8,128)(2,1)S(1)} %pad_maximum_fusion.refs_0_, bf16[3072,768]{1,0:T(8,128)(2,1)S(1)} %get-tuple-element.52.refs_1_, bf16[3072,768]{1,0:T(8,128)(2,1)S(1)} %get-tuple-element.53.refs_2_, bf16[32,1536]{1,0:T(8,128)(2,1)S(1)} %get-tuple-element.73.refs_3_), custom_call_target="tpu_custom_call" | custom-call | flops 1000 | bytes 1000 | tf_op jit(solution)/shard_map/up_m1/pallas_call | solution.py:94
  84.0 1.6 %collective-permute-start.17 = (bf16[32,1536]{1,0:T(8,128)(2,1)S(1)}, bf16[32,1536]{1,0:T(8,128)(2,1)S(1)}, u32[]{:S(2)}, u32[]{:S(2)}) collective-permute-start(bf16[32,1536]{1,0:T(8,128)(2,1)S(1)} %add_convert_fusion.refs_4_), channel_id=1, source_target_pairs={{0,2},{1,3},{2,0},{3,1},{4,6},{5,7},{6,4},{7,5},{8,10},{9,11},{10,... | collective-permute-start | bytes 294920 | tf_op jit(solution)/shard_map/ppermute | solution.py:37
  85.6 0.9 collective-permute-done.19
  86.5 0.1 fusion.31.refs_0_
  86.6 2.0 %collective-permute-done.17 = bf16[32,1536]{1,0:T(8,128)(2,1)S(1)} collective-permute-done((bf16[32,1536]{1,0:T(8,128)(2,1)S(1)}, bf16[32,1536]{1,0:T(8,128)(2,1)S(1)}, u32[]{:S(2)}, u32[]{:S(2)}) %collective-permute-start.17) | collective-permute-done | bytes 98336 | tf_op jit(solution)/shard_map/ppermute | solution.py:37
  88.7 0.1 fusion.23.refs_3_
  88.9 6.6 %down_m0.3 = (f32[32,3072]{1,0:T(8,128)S(1)}, bf16[1536,1536]{1,0:T(8,128)(2,1)S(1)}, bf16[1536,1536]{1,0:T(8,128)(2,1)S(1)}, bf16[1536,1536]{1,0:T(8,128)(2,1)S(1)}, bf16[1536,1536]{1,0:T(8,128)(2,1)S(1)}) custom-call(bf16[32,1536]{1,0:T(8,128)(2,1)S(1)} %fusion.31.refs_0_, bf16[1536,1536]{1,0:T(8,128)(2,1)S(1)} %get-tuple-element.74.refs_1_, ...), custom_call_target="tpu_custom_call" | custom-call | flops 1000 | bytes 1000 | tf_op jit(solution)/shard_map/down_m0/pallas_call | solution.py:94
  95.5 3.3 %down_t0_m1.3.refs_3_ = f32[32,3072]{1,0:T(8,128)S(1)} custom-call(bf16[32,1536]{1,0:T(8,128)(2,1)S(1)} %collective-permute-done.20.refs_0_, bf16[1536,1536]{1,0:T(8,128)(2,1)S(1)} %get-tuple-element.78.refs_1_, bf16[1536,1536]{1,0:T(8,128)(2,1)S(1)} %get-tuple-element.79.refs_2_, bf16[32,1536]{1,0:T(8,128)(2,1)S(1)} %fusion.23.refs_3_, ...), custom_call_target="tpu_custom_call" | custom-call | flops 1000 | bytes 1000 | tf_op jit(solution)/shard_map/down_t0_m1/pallas_call | solution.py:94
  98.8 1.7 %down_t1.3 = bf16[32,3072]{1,0:T(8,128)(2,1)S(1)} custom-call(bf16[32,1536]{1,0:T(8,128)(2,1)S(1)} %collective-permute-done.18.refs_0_, bf16[1536,1536]{1,0:T(8,128)(2,1)S(1)} %get-tuple-element.76.refs_1_, bf16[1536,1536]{1,0:T(8,128)(2,1)S(1)} %get-tuple-element.77.refs_2_, f32[32,3072]{1,0:T(8,128)S(1)} %down_t0_m1.3.refs_3_), custom_call_target="tpu_custom_call" | custom-call | flops 1000 | bytes 1000 | tf_op jit(solution)/shard_map/down_t1/pallas_call | solution.py:94
  100.5 1.4 %collective-permute-start.21 = (bf16[8,3072]{1,0:T(8,128)(2,1)S(1)}, bf16[8,3072]{1,0:T(8,128)(2,1)S(1)}, u32[]{:S(2)}, u32[]{:S(2)}) collective-permute-start(bf16[8,3072]{1,0:T(8,128)(2,1)S(1)} %get-tuple-element.83), channel_id=1, source_target_pairs={{0,12},{4,8},{8,4},{12,0},{1,13},{5,9},{9,5},{13,1},{2,14},{6,10},... | collective-permute-start | bytes 147464 | tf_op jit(solution)/shard_map/ppermute | solution.py:37
  102.0 3.0 %collective-permute-start.23 = (bf16[8,3072]{1,0:T(8,128)(2,1)S(1)}, bf16[8,3072]{1,0:T(8,128)(2,1)S(1)}, u32[]{:S(2)}, u32[]{:S(2)}) collective-permute-start(bf16[8,3072]{1,0:T(8,128)(2,1)S(1)} %get-tuple-element.84), channel_id=1, source_target_pairs={{0,4},{4,0},{8,12},{12,8},{1,5},{5,1},{9,13},{13,9},{2,6},{6,2},{1... | collective-permute-start | bytes 147464 | tf_op jit(solution)/shard_map/ppermute | solution.py:37
  105.0 2.0 %collective-permute-done.21 = bf16[8,3072]{1,0:T(8,128)(2,1)S(1)} collective-permute-done((bf16[8,3072]{1,0:T(8,128)(2,1)S(1)}, bf16[8,3072]{1,0:T(8,128)(2,1)S(1)}, u32[]{:S(2)}, u32[]{:S(2)}) %collective-permute-start.21) | collective-permute-done | bytes 49184 | tf_op jit(solution)/shard_map/ppermute | solution.py:37
  107.0 1.6 %collective-permute-done.22 = bf16[8,3072]{1,0:T(8,128)(2,1)S(1)} collective-permute-done((bf16[8,3072]{1,0:T(8,128)(2,1)S(1)}, bf16[8,3072]{1,0:T(8,128)(2,1)S(1)}, u32[]{:S(2)}, u32[]{:S(2)}) %collective-permute-start.22) | collective-permute-done | bytes 49184 | tf_op jit(solution)/shard_map/ppermute | solution.py:37
  108.6 0.7 add_convert_fusion.4
  (43 shorter events, 0.7 us)
Async XLA Ops:
  0.0 10.3 %collective-permute-start = (bf16[8,3072]{1,0:T(8,128)(2,1)}, bf16[8,3072]{1,0:T(8,128)(2,1)S(1)}, u32[]{:S(2)}, u32[]{:S(2)}) collective-permute-start(bf16[8,3072]{1,0:T(8,128)(2,1)} %param.3), channel_id=1, source_target_pairs={{0,4},{4,0},{8,12},{12,8},{1,5},{5,1},{9,13},{13,9},{2,6},{6,2},{1... | collective-permute-start | bytes 147464 | tf_op jit(solution)/shard_map/ppermute | solution.py:37
  3.0 7.3 %collective-permute-start.1 = (bf16[8,3072]{1,0:T(8,128)(2,1)}, bf16[8,3072]{1,0:T(8,128)(2,1)S(1)}, u32[]{:S(2)}, u32[]{:S(2)}) collective-permute-start(bf16[8,3072]{1,0:T(8,128)(2,1)} %param.3), channel_id=1, source_target_pairs={{0,8},{4,12},{8,0},{12,4},{1,9},{5,13},{9,1},{13,5},{2,10},{6,14},... | collective-permute-start | bytes 147464 | tf_op jit(solution)/shard_map/ppermute | solution.py:37
  5.6 6.1 %collective-permute-start.2 = (bf16[8,3072]{1,0:T(8,128)(2,1)}, bf16[8,3072]{1,0:T(8,128)(2,1)S(1)}, u32[]{:S(2)}, u32[]{:S(2)}) collective-permute-start(bf16[8,3072]{1,0:T(8,128)(2,1)} %param.3), channel_id=1, source_target_pairs={{0,12},{4,8},{8,4},{12,0},{1,13},{5,9},{9,5},{13,1},{2,14},{6,10},... | collective-permute-start | bytes 147464 | tf_op jit(solution)/shard_map/ppermute | solution.py:37
  15.5 3.9 %collective-permute-start.3 = (bf16[32,1536]{1,0:T(8,128)(2,1)S(1)}, bf16[32,1536]{1,0:T(8,128)(2,1)S(1)}, u32[]{:S(2)}, u32[]{:S(2)}) collective-permute-start(bf16[32,1536]{1,0:T(8,128)(2,1)S(1)} %get-tuple-element.48.refs_4_), channel_id=1, source_target_pairs={{0,1},{1,0},{2,3},{3,2},{4,5},{5,4},{6,7},{7,6},{8,9},{9,8},{10,11... | collective-permute-start | bytes 294920 | tf_op jit(solution)/shard_map/ppermute | solution.py:37
  23.3 8.6 %collective-permute-start.4 = (bf16[32,1536]{1,0:T(8,128)(2,1)S(1)}, bf16[32,1536]{1,0:T(8,128)(2,1)S(1)}, u32[]{:S(2)}, u32[]{:S(2)}) collective-permute-start(bf16[32,1536]{1,0:T(8,128)(2,1)S(1)} %get-tuple-element.54.refs_4_), channel_id=1, source_target_pairs={{0,1},{1,0},{2,3},{3,2},{4,5},{5,4},{6,7},{7,6},{8,9},{9,8},{10,11... | collective-permute-start | bytes 294920 | tf_op jit(solution)/shard_map/ppermute | solution.py:37
  23.9 8.7 %collective-permute-start.7 = (bf16[32,1536]{1,0:T(8,128)(2,1)S(1)}, bf16[32,1536]{1,0:T(8,128)(2,1)S(1)}, u32[]{:S(2)}, u32[]{:S(2)}) collective-permute-start(bf16[32,1536]{1,0:T(8,128)(2,1)S(1)} %add_convert_fusion.3.refs_4_), channel_id=1, source_target_pairs={{0,2},{1,3},{2,0},{3,1},{4,6},{5,7},{6,4},{7,5},{8,10},{9,11},{10,... | collective-permute-start | bytes 294920 | tf_op jit(solution)/shard_map/ppermute | solution.py:37
  31.9 4.7 %collective-permute-start.5 = (bf16[32,1536]{1,0:T(8,128)(2,1)S(1)}, bf16[32,1536]{1,0:T(8,128)(2,1)S(1)}, u32[]{:S(2)}, u32[]{:S(2)}) collective-permute-start(bf16[32,1536]{1,0:T(8,128)(2,1)S(1)} %add_convert_fusion.2.refs_4_), channel_id=1, source_target_pairs={{0,2},{1,3},{2,0},{3,1},{4,6},{5,7},{6,4},{7,5},{8,10},{9,11},{10,... | collective-permute-start | bytes 294920 | tf_op jit(solution)/shard_map/ppermute | solution.py:37
  32.6 10.7 %collective-permute-start.8 = (bf16[32,1536]{1,0:T(8,128)(2,1)S(1)}, bf16[32,1536]{1,0:T(8,128)(2,1)S(1)}, u32[]{:S(2)}, u32[]{:S(2)}) collective-permute-start(bf16[32,1536]{1,0:T(8,128)(2,1)S(1)} %fusion.15.refs_0_), channel_id=1, source_target_pairs={{0,1},{1,0},{2,3},{3,2},{4,5},{5,4},{6,7},{7,6},{8,9},{9,8},{10,11... | collective-permute-start | bytes 294920 | tf_op jit(solution)/shard_map/ppermute | solution.py:37
  36.7 9.9 %collective-permute-start.6 = (bf16[32,1536]{1,0:T(8,128)(2,1)S(1)}, bf16[32,1536]{1,0:T(8,128)(2,1)S(1)}, u32[]{:S(2)}, u32[]{:S(2)}) collective-permute-start(bf16[32,1536]{1,0:T(8,128)(2,1)S(1)} %fusion.7.refs_3_), channel_id=1, source_target_pairs={{0,1},{1,0},{2,3},{3,2},{4,5},{5,4},{6,7},{7,6},{8,9},{9,8},{10,11... | collective-permute-start | bytes 294920 | tf_op jit(solution)/shard_map/ppermute | solution.py:37
  46.6 10.7 %copy-start.1 = (bf16[8,3072]{1,0:T(8,128)(2,1)S(1)}, bf16[8,3072]{1,0:T(8,128)(2,1)}, u32[]{:S(2)}) copy-start(bf16[8,3072]{1,0:T(8,128)(2,1)} %param.3) | copy-start | bytes 147460
  48.4 6.1 %collective-permute-start.10 = (bf16[8,3072]{1,0:T(8,128)(2,1)S(1)}, bf16[8,3072]{1,0:T(8,128)(2,1)S(1)}, u32[]{:S(2)}, u32[]{:S(2)}) collective-permute-start(bf16[8,3072]{1,0:T(8,128)(2,1)S(1)} %get-tuple-element.88), channel_id=1, source_target_pairs={{0,8},{4,12},{8,0},{12,4},{1,9},{5,13},{9,1},{13,5},{2,10},{6,14},... | collective-permute-start | bytes 147464 | tf_op jit(solution)/shard_map/ppermute | solution.py:37
  49.0 5.6 %collective-permute-start.11 = (bf16[8,3072]{1,0:T(8,128)(2,1)S(1)}, bf16[8,3072]{1,0:T(8,128)(2,1)S(1)}, u32[]{:S(2)}, u32[]{:S(2)}) collective-permute-start(bf16[8,3072]{1,0:T(8,128)(2,1)S(1)} %get-tuple-element.87), channel_id=1, source_target_pairs={{0,4},{4,0},{8,12},{12,8},{1,5},{5,1},{9,13},{13,9},{2,6},{6,2},{1... | collective-permute-start | bytes 147464 | tf_op jit(solution)/shard_map/ppermute | solution.py:37
  51.5 5.9 %collective-permute-start.9 = (bf16[8,3072]{1,0:T(8,128)(2,1)S(1)}, bf16[8,3072]{1,0:T(8,128)(2,1)S(1)}, u32[]{:S(2)}, u32[]{:S(2)}) collective-permute-start(bf16[8,3072]{1,0:T(8,128)(2,1)S(1)} %get-tuple-element.86), channel_id=1, source_target_pairs={{0,12},{4,8},{8,4},{12,0},{1,13},{5,9},{9,5},{13,1},{2,14},{6,10},... | collective-permute-start | bytes 147464 | tf_op jit(solution)/shard_map/ppermute | solution.py:37
  57.4 12.1 %collective-permute-start.12 = (bf16[8,3072]{1,0:T(8,128)(2,1)S(1)}, bf16[8,3072]{1,0:T(8,128)(2,1)S(1)}, u32[]{:S(2)}, u32[]{:S(2)}) collective-permute-start(bf16[8,3072]{1,0:T(8,128)(2,1)S(1)} %add_convert_fusion.5.refs_1_), channel_id=1, source_target_pairs={{0,4},{4,0},{8,12},{12,8},{1,5},{5,1},{9,13},{13,9},{2,6},{6,2},{1... | collective-permute-start | bytes 147464 | tf_op jit(solution)/shard_map/ppermute | solution.py:37
  57.5 12.0 %collective-permute-start.13 = (bf16[8,3072]{1,0:T(8,128)(2,1)S(1)}, bf16[8,3072]{1,0:T(8,128)(2,1)S(1)}, u32[]{:S(2)}, u32[]{:S(2)}) collective-permute-start(bf16[8,3072]{1,0:T(8,128)(2,1)S(1)} %add_convert_fusion.5.refs_1_), channel_id=1, source_target_pairs={{0,8},{4,12},{8,0},{12,4},{1,9},{5,13},{9,1},{13,5},{2,10},{6,14},... | collective-permute-start | bytes 147464 | tf_op jit(solution)/shard_map/ppermute | solution.py:37
  59.4 10.1 %collective-permute-start.14 = (bf16[8,3072]{1,0:T(8,128)(2,1)S(1)}, bf16[8,3072]{1,0:T(8,128)(2,1)S(1)}, u32[]{:S(2)}, u32[]{:S(2)}) collective-permute-start(bf16[8,3072]{1,0:T(8,128)(2,1)S(1)} %add_convert_fusion.5.refs_1_), channel_id=1, source_target_pairs={{0,12},{4,8},{8,4},{12,0},{1,13},{5,9},{9,5},{13,1},{2,14},{6,10},... | collective-permute-start | bytes 147464 | tf_op jit(solution)/shard_map/ppermute | solution.py:37
  73.4 3.9 %collective-permute-start.15 = (bf16[32,1536]{1,0:T(8,128)(2,1)S(1)}, bf16[32,1536]{1,0:T(8,128)(2,1)S(1)}, u32[]{:S(2)}, u32[]{:S(2)}) collective-permute-start(bf16[32,1536]{1,0:T(8,128)(2,1)S(1)} %get-tuple-element.71.refs_4_), channel_id=1, source_target_pairs={{0,1},{1,0},{2,3},{3,2},{4,5},{5,4},{6,7},{7,6},{8,9},{9,8},{10,11... | collective-permute-start | bytes 294920 | tf_op jit(solution)/shard_map/ppermute | solution.py:37
  81.1 2.8 %copy-start = (bf16[1536,1536]{1,0:T(8,128)(2,1)}, bf16[1536,1536]{1,0:T(8,128)(2,1)S(1)}, u32[]{:S(2)}) copy-start(bf16[1536,1536]{1,0:T(8,128)(2,1)S(1)} %get-tuple-element.81.refs_5_) | copy-start | bytes 14155780
  81.1 2.8 %collective-permute-start.16 = (bf16[32,1536]{1,0:T(8,128)(2,1)S(1)}, bf16[32,1536]{1,0:T(8,128)(2,1)S(1)}, u32[]{:S(2)}, u32[]{:S(2)}) collective-permute-start(bf16[32,1536]{1,0:T(8,128)(2,1)S(1)} %get-tuple-element.73.refs_3_), channel_id=1, source_target_pairs={{0,1},{1,0},{2,3},{3,2},{4,5},{5,4},{6,7},{7,6},{8,9},{9,8},{10,11... | collective-permute-start | bytes 294920 | tf_op jit(solution)/shard_map/ppermute | solution.py:37
  81.7 4.8 %collective-permute-start.19 = (bf16[32,1536]{1,0:T(8,128)(2,1)S(1)}, bf16[32,1536]{1,0:T(8,128)(2,1)S(1)}, u32[]{:S(2)}, u32[]{:S(2)}) collective-permute-start(bf16[32,1536]{1,0:T(8,128)(2,1)S(1)} %add_convert_fusion.1.refs_4_), channel_id=1, source_target_pairs={{0,2},{1,3},{2,0},{3,1},{4,6},{5,7},{6,4},{7,5},{8,10},{9,11},{10,... | collective-permute-start | bytes 294920 | tf_op jit(solution)/shard_map/ppermute | solution.py:37
  84.0 4.7 %collective-permute-start.17 = (bf16[32,1536]{1,0:T(8,128)(2,1)S(1)}, bf16[32,1536]{1,0:T(8,128)(2,1)S(1)}, u32[]{:S(2)}, u32[]{:S(2)}) collective-permute-start(bf16[32,1536]{1,0:T(8,128)(2,1)S(1)} %add_convert_fusion.refs_4_), channel_id=1, source_target_pairs={{0,2},{1,3},{2,0},{3,1},{4,6},{5,7},{6,4},{7,5},{8,10},{9,11},{10,... | collective-permute-start | bytes 294920 | tf_op jit(solution)/shard_map/ppermute | solution.py:37
  86.5 9.0 %slice-start = ((s8[4718592]{0:T(1024)(128)(4,1)}), s8[4194304]{0:T(1024)(128)(4,1)S(1)}, s32[]{:S(2)}) async-start(s8[4718592]{0:T(1024)(128)(4,1)} %bitcast), calls=%async_computation | async-start | bytes 8388608
  86.6 8.9 %collective-permute-start.20 = (bf16[32,1536]{1,0:T(8,128)(2,1)S(1)}, bf16[32,1536]{1,0:T(8,128)(2,1)S(1)}, u32[]{:S(2)}, u32[]{:S(2)}) collective-permute-start(bf16[32,1536]{1,0:T(8,128)(2,1)S(1)} %fusion.31.refs_0_), channel_id=1, source_target_pairs={{0,1},{1,0},{2,3},{3,2},{4,5},{5,4},{6,7},{7,6},{8,9},{9,8},{10,11... | collective-permute-start | bytes 294920 | tf_op jit(solution)/shard_map/ppermute | solution.py:37
  88.8 10.0 %collective-permute-start.18 = (bf16[32,1536]{1,0:T(8,128)(2,1)S(1)}, bf16[32,1536]{1,0:T(8,128)(2,1)S(1)}, u32[]{:S(2)}, u32[]{:S(2)}) collective-permute-start(bf16[32,1536]{1,0:T(8,128)(2,1)S(1)} %fusion.23.refs_3_), channel_id=1, source_target_pairs={{0,1},{1,0},{2,3},{3,2},{4,5},{5,4},{6,7},{7,6},{8,9},{9,8},{10,11... | collective-permute-start | bytes 294920 | tf_op jit(solution)/shard_map/ppermute | solution.py:37
  88.9 6.6 %slice-start.1 = ((s8[4718592]{0:T(1024)(128)(4,1)}), s8[524288]{0:T(1024)(128)(4,1)S(1)}, s32[]{:S(2)}) async-start(s8[4718592]{0:T(1024)(128)(4,1)} %bitcast), calls=%async_computation.1 | async-start | bytes 1048576
  100.5 6.5 %collective-permute-start.21 = (bf16[8,3072]{1,0:T(8,128)(2,1)S(1)}, bf16[8,3072]{1,0:T(8,128)(2,1)S(1)}, u32[]{:S(2)}, u32[]{:S(2)}) collective-permute-start(bf16[8,3072]{1,0:T(8,128)(2,1)S(1)} %get-tuple-element.83), channel_id=1, source_target_pairs={{0,12},{4,8},{8,4},{12,0},{1,13},{5,9},{9,5},{13,1},{2,14},{6,10},... | collective-permute-start | bytes 147464 | tf_op jit(solution)/shard_map/ppermute | solution.py:37
  102.0 6.7 %collective-permute-start.22 = (bf16[8,3072]{1,0:T(8,128)(2,1)S(1)}, bf16[8,3072]{1,0:T(8,128)(2,1)S(1)}, u32[]{:S(2)}, u32[]{:S(2)}) collective-permute-start(bf16[8,3072]{1,0:T(8,128)(2,1)S(1)} %get-tuple-element.85), channel_id=1, source_target_pairs={{0,8},{4,12},{8,0},{12,4},{1,9},{5,13},{9,1},{13,5},{2,10},{6,14},... | collective-permute-start | bytes 147464 | tf_op jit(solution)/shard_map/ppermute | solution.py:37
  102.0 6.7 %collective-permute-start.23 = (bf16[8,3072]{1,0:T(8,128)(2,1)S(1)}, bf16[8,3072]{1,0:T(8,128)(2,1)S(1)}, u32[]{:S(2)}, u32[]{:S(2)}) collective-permute-start(bf16[8,3072]{1,0:T(8,128)(2,1)S(1)} %get-tuple-element.84), channel_id=1, source_target_pairs={{0,4},{4,0},{8,12},{12,8},{1,5},{5,1},{9,13},{13,9},{2,6},{6,2},{1... | collective-permute-start | bytes 147464 | tf_op jit(solution)/shard_map/ppermute | solution.py:37

commit v3 on v0

v3 whole, which is shorter than its diff:
```python
import jax
import jax.numpy as jnp
from jax import lax
from jax.experimental import pallas as pl
from jax.experimental.pallas import tpu as pltpu
from jax.sharding import PartitionSpec as P

STEPS = 2
BLOCKS = 8
EARLY = 4
bf16, f32 = jnp.bfloat16, jnp.float32


def plain(tokens, w_in, w_out):
    row_dev = tokens.shape[0]
    where = lax.axis_index("hidden")
    full = lax.all_gather(tokens, "hidden", axis=0, tiled=True)
    latest = tokens
    for step in range(STEPS):
        pre = jnp.dot(full, w_in, preferred_element_type=f32)
        summed = lax.psum(pre.astype(bf16), "width").astype(f32)
        activ = jax.nn.gelu(summed, approximate=True).astype(bf16)
        mine_sum = lax.psum_scatter(
            jnp.dot(activ, w_out, preferred_element_type=f32).astype(bf16),
            "hidden",
            scatter_dimension=0,
            tiled=True,
        ).astype(f32)
        mine_old = lax.dynamic_slice_in_dim(full, where * row_dev, row_dev, 0)
        latest = (mine_old.astype(f32) + mine_sum).astype(bf16)
        if step + 1 < STEPS:
            full = lax.all_gather(latest, "hidden", axis=0, tiled=True)
    return latest


def swap(x, axis, n, mask):
    return lax.ppermute(x, axis, [(i, i ^ mask) for i in range(n)])


def stage(products, loads, name, behind=(), add=None, dtype=bf16, carry=None, over=()):
    given = [a for x, w in products for a in (x, *w)] + [a for a in (add, carry) if a is not None]
    copied = [(array, dim, per, b) for array, dim, per, first, last in loads for b in range(first, last)]
    n_g, n_a, n_l = len(given), len(loads), len(copied)
    n_b = len(products[0][1]) if products else 0
    wide = products[0][1][0].shape[1] if products else 0
    source = [i for i, (_, _, _, first, last) in enumerate(loads) for _ in range(first, last)]

    def size(array, dim):
        rows, cols = (n // 2 if k == dim else n for k, n in enumerate(array.shape))
        return rows, cols // BLOCKS

    def kernel(*refs):
        refs_in, hbm = refs[:n_g], refs[n_g : n_g + n_a]
        out = list(refs[n_g + n_a + len(behind) + len(over) :])
        result = out.pop(0) if products else None
        carried = out.pop(0) if carry is not None else None
        held, sems = out[:n_l], out[n_l:]
        core = lax.rem(lax.axis_index("width"), 2)
        copies = []
        for i, (array, dim, per, b) in enumerate(copied):
            rows, cols = size(array, dim)
            half = core if per > 0 else 1 - core
            top, left = (half * rows, b * cols) if dim == 0 else (0, half * (cols * BLOCKS) + b * cols)
            index = (pl.ds(pl.multiple_of(top, 128), rows), pl.ds(pl.multiple_of(left, 128), cols))
            copies.append(pltpu.make_async_copy(hbm[source[i]].at[index], held[i], sems[0].at[i]))
        for copy in copies:
            copy.start()
        if carry is not None:
            carried[...] = refs_in[-1][...]
        if products:

            @pl.when(core < 2)
            def _():
                for b in range(n_b):
                    columns = slice(b * wide, (b + 1) * wide)
                    total = None if add is None else refs_in[len(products) * (1 + n_b)][:, columns]
                    for p in range(len(products)):
                        x, w = refs_in[p * (1 + n_b)], refs_in[p * (1 + n_b) + 1 + b]
                        part = jnp.dot(x[...], w[...], preferred_element_type=f32)
                        total = part if total is None else total + part
                    result[:, columns] = total.astype(result.dtype)

        for copy in copies:
            copy.wait()

    shapes = [pltpu.VMEM(size(array, dim), array.dtype) for array, dim, _, _ in copied]
    if carry is not None:
        shapes = [jax.ShapeDtypeStruct(carry.shape, carry.dtype)] + shapes
    if products:
        shapes = [jax.ShapeDtypeStruct((given[0].shape[0], n_b * wide), dtype)] + shapes
    vmem, hbm, anywhere = (pl.BlockSpec(memory_space=m) for m in (pltpu.VMEM, pltpu.HBM, pl.ANY))
    got = pl.pallas_call(
        kernel,
        out_shape=shapes,
        in_specs=[vmem] * n_g + [hbm] * n_a + [anywhere] * len(behind) + [vmem] * len(over),
        out_specs=[vmem] * len(shapes),
        input_output_aliases={n_g + n_a + len(behind) + i: len(shapes) - n_l + i for i in range(len(over))},
        scratch_shapes=[pltpu.SemaphoreType.DMA((n_l,))] if loads else [],
        compiler_params=pltpu.CompilerParams(vmem_limit_bytes=2 * 2**20),
        cost_estimate=pl.CostEstimate(flops=1000, bytes_accessed=1000, transcendentals=0),
        name=name,
    )(*given, *[pltpu.with_memory_space_constraint(load[0], pltpu.HBM) for load in loads], *behind, *over)
    got = list(got)
    lead = [got.pop(0) for there in (products, carry is not None) if there]
    return *lead, got


def gather(block, nz):
    return jnp.concatenate([block] + [swap(block, "hidden", nz, k) for k in range(1, nz)], 0)


def tuned(nz, nw, tokens, w_in, w_out):
    rows, d = tokens.shape
    def load(array, dim, per, first=0, last=BLOCKS):
        return (array, dim, per, first, last)

    def scattered(part, old, total):
        for k in range(nz - 1, 0, -1):
            total = total + swap(part[k * rows : (k + 1) * rows], "hidden", nz, k).astype(f32)
        return (old.astype(f32) + total).astype(bf16)

    state = tokens
    x = gather(state, nz)
    (other_in,) = stage([], [load(w_in, 1, -1)], "load_other_in")
    for step in range(STEPS):
        first, last = step == 0, step + 1 == STEPS
        sent, got = stage([(x, other_in)], [load(w_in, 1, 1)] if first else [], "up_other")
        mine_in = got if first else mine_in
        kept, got = stage([(x, mine_in)], [load(w_out, 0, 1)] if first else [], "up_mine", [sent])
        mine_out = got if first else mine_out
        chip = (kept.astype(f32) + swap(sent, "width", nw, 1).astype(f32)).astype(bf16)
        across = swap(chip, "width", nw, 2)
        chip, other_out = stage([], [load(w_out, 0, -1)], "load_other_out", carry=chip, over=other_in)
        total = chip.astype(f32) + across.astype(f32)
        mine = jax.nn.gelu(total, approximate=True).astype(bf16)
        other = swap(mine, "width", nw, 1)
        part, _ = stage([(mine, mine_out)], [], "down_mine", [], None, f32)
        part, _ = stage([(other, other_out)], [], "down_other", [], part)
        if last:
            state = scattered(part, state, part[:rows].astype(f32))
        else:
            half = [load(w_in, 1, -1, 0, EARLY)], [load(w_in, 1, -1, EARLY, BLOCKS)]
            old, got = stage([], half[0], "load_other_in", [part], carry=state, over=other_out[:EARLY])
            state = scattered(part, old, part[:rows].astype(f32))
            other_in = got + stage([], half[1], "load_other_in", [state], over=other_out[EARLY:])[0]
            x = gather(state, nz)
    return state


def solution(mesh):
    placed = (P(("groups", "hidden"), "width"), P("width", "hidden"), P("hidden", "width"))
    nz, nw = mesh.shape["hidden"], mesh.shape["width"]

    def local(tokens, w_in, w_out):
        d = tokens.shape[1]
        fits = nz == 4 and nw == 4 and w_in.shape[1] == 2 * d and d % (128 * BLOCKS) == 0
        return tuned(nz, nw, tokens, w_in, w_out) if fits else plain(tokens, w_in, w_out)

    return jax.shard_map(
        local,
        mesh=mesh,
        in_specs=placed,
        out_specs=P(("groups", "hidden"), "width"),
        check_vma=False,
    )
```

time: 213 us -> 92.6 us (0.43)
  waiting for transfers between devices: 104 us -> 4.8 us
  matrix products: 63.5 us -> 0 us
  Pallas kernels: 0 us -> 62 us
  blocking collectives: 29.2 us -> 0 us
  starting transfers between devices: 0.13 us -> 21.7 us
  between operations: 13.1 us -> 0.51 us
  local copies, waits for them, and re-layouts: 0 us -> 2.21 us
    psum x2 -> x0, waiting for transfers between devices: 65.3 us -> none  [local(): summed = lax.psum(pre.astype(jnp.bfloat16), 'width').astype(jnp.float32)]
    dot_general x4 -> x0, matrix products: 63.5 us -> none  [the longest x2 31.8 us: local(): jnp.dot(activ, w_out, preferred_element_type=jnp.float32)]
    pallas_call x0 -> x13, Pallas kernels: none -> 62 us  [stage(): pl.pallas_call(kernel, out_shape=shapes, in_specs=[vmem] * n_g + [hbm] *...]
    reduce_scatter x2 -> x0, waiting for transfers between devices: 39 us -> none  [local(): lax.psum_scatter(jnp.dot(activ, w_out, preferred_element_type=jnp.float32...]
    all_gather x2 -> x0, blocking collectives: 29.2 us -> none  [the longest x1 15.7 us: local(): full = lax.all_gather(tokens, 'hidden', axis=0, tiled=True)]
    ppermute x0 -> x18, starting transfers between devices: none -> 21.7 us  [swap(): return lax.ppermute(x, axis, [(i, i ^ mask) for i in range(n)])]
    ppermute x0 -> x18, waiting for transfers between devices: none -> 4.8 us  [swap(): return lax.ppermute(x, axis, [(i, i ^ mask) for i in range(n)])]
    unnamed x0 -> x29, local copies, waits for them, and re-layouts: none -> 2.18 us
  transfers between devices with their start and end apart: 4 -> 18, of which waited for: 4 -> 5; matrix products, arithmetic and copies ran while one was open for 0% -> 1% of each run, Pallas kernels for 0% -> 50%
where the time goes in v3:
time: 92.6 us; the launch traced here: 92.4 us
  Pallas kernels  62 us (67%)
  starting transfers between devices  21.7 us (23%)
  waiting for transfers between devices  4.8 us (5%)
  local copies, waits for them, and re-layouts  2.21 us (2%)
  other arithmetic  1.15 us (1%)
    pallas_call x13, Pallas kernels, stage(): pl.pallas_call(kernel, out_shape=shapes, in_specs=[vmem] * n_g + [hbm] *...  62 us
    ppermute x18, starting transfers between devices, swap(): return lax.ppermute(x, axis, [(i, i ^ mask) for i in range(n)])  21.7 us
    ppermute x18, waiting for transfers between devices, swap(): return lax.ppermute(x, axis, [(i, i ^ mask) for i in range(n)])  4.8 us
    unnamed x29, local copies, waits for them, and re-layouts  2.18 us
  transfers between devices with their start and end apart: 18, of which 5 were waited for; matrix products, arithmetic and copies ran while one was open for 1% of the time, Pallas kernels for 50%

profile of v3, /device:TPU:0, one launch (start us, length us, event | category | flops | bytes accessed | tf_op | source)
XLA Modules:
  0.0 92.4 jit_solution(11341715073703885486)
XLA Ops:
  0.0 5.0 %collective-permute-start.2 = (bf16[8,3072]{1,0:T(8,128)(2,1)}, bf16[8,3072]{1,0:T(8,128)(2,1)S(1)}, u32[]{:S(2)}, u32[]{:S(2)}) collective-permute-start(bf16[8,3072]{1,0:T(8,128)(2,1)} %refs_0_.4), channel_id=1, source_target_pairs={{0,12},{4,8},{8,4},{12,0},{1,13},{5,9},{9,5},{13,1},{2,14},{6,10},... | collective-permute-start | bytes 147464 | tf_op jit(solution)/shard_map/ppermute | solution.py:37
  5.1 0.6 collective-permute-start
  5.6 0.8 constant_dynamic-update-slice_fusion.3
  6.5 6.6 %load_other_in.3 = (bf16[3072,384]{1,0:T(8,128)(2,1)S(1)}, bf16[3072,384]{1,0:T(8,128)(2,1)S(1)}, bf16[3072,384]{1,0:T(8,128)(2,1)S(1)}, bf16[3072,384]{1,0:T(8,...) custom-call(bf16[3072,6144]{1,0:T(8,128)(2,1)} %refs_0_.5), custom_call_target="tpu_custom_call" | custom-call | flops 1000 | bytes 1000 | tf_op jit(solution)/shard_map/load_other_in/pallas_call | solution.py:92
  13.1 0.0 collective-permute-done.1
  13.2 6.7 %up_other.2 = (bf16[32,3072]{1,0:T(8,128)(2,1)S(1)}, bf16[3072,384]{1,0:T(8,128)(2,1)S(1)}, bf16[3072,384]{1,0:T(8,128)(2,1)S(1)}, bf16[3072,384]{1,0:T(8,128)(2...) custom-call(bf16[32,3072]{1,0:T(8,128)(2,1)S(1)} %constant_dynamic-u, ...), custom_call_target="tpu_custom_call" | custom-call | flops 1000 | bytes 1000 | tf_op jit(solution)/shard_map/up_other/pallas_call | solution.py:92
  19.9 0.1 collective-permute-start.3
  20.0 10.6 %up_mine.2 = (bf16[32,3072]{1,0:T(8,128)(2,1)S(1)}, bf16[3072,384]{1,0:T(8,128)(2,1)S(1)}, bf16[3072,384]{1,0:T(8,128)(2,1)S(1)}, bf16[3072,384]{1,0:T(8,128)(2,...) custom-call(bf16[32,3072]{1,0:T(8,128)(2,1)S(1)} %constant_dynamic-u, ...), custom_call_target="tpu_custom_call" | custom-call | flops 1000 | bytes 1000 | tf_op jit(solution)/shard_map/up_mine/pallas_call | solution.py:92
  30.6 0.0 collective-permute-done.3
  30.7 1.8 %collective-permute-start.4 = (bf16[32,3072]{1,0:T(8,128)(2,1)S(1)}, bf16[32,3072]{1,0:T(8,128)(2,1)S(1)}, u32[]{:S(2)}, u32[]{:S(2)}) collective-permute-start(bf16[32,3072]{1,0:T(8,128)(2,1)S(1)} %add_convert_fusion.1.refs_0_), channel_id=1, source_target_pairs={{0,2},{1,3},{2,0},{3,1},{4,6},{5,7},{6,4},{7,5},{8,10},{9,11},{10,... | collective-permute-start | bytes 589832 | tf_op jit(solution)/shard_map/ppermute | solution.py:37
  32.4 6.6 %load_other_out.2 = (bf16[32,3072]{1,0:T(8,128)(2,1)S(1)}, bf16[3072,384]{1,0:T(8,128)(2,1)S(1)}, bf16[3072,384]{1,0:T(8,128)(2,1)S(1)}, bf16[3072,384]{1,0:T(8,...) custom-call(bf16[32,3072]{1,0:T(8,128)(2,1)S(1)} %add_convert_fusion, ...), custom_call_target="tpu_custom_call", output_to_operand_aliasing={{1}: (2, {}), {2}: (3, {}), {3}: (4, {}), {4}: (5, {}), {5}... | custom-call | flops 1000 | bytes 1000 | tf_op jit(solution)/shard_map/load_other_out/pallas_call | solution.py:92
  39.1 0.0 collective-permute-done.4
  39.1 0.2 fusion.7.refs_0_
  39.3 0.1 collective-permute-start.5
  39.4 2.8 %down_mine.2.refs_9_ = f32[32,3072]{1,0:T(8,128)S(1)} custom-call(bf16[32,3072]{1,0:T(8,128)(2,1)S(1)} %fusion.7.refs_0_, bf16[3072,384]{1,0:T(8,128)(2,1)S(1)} %get-tuple-element.85.refs_1_, bf16[3072,384]{1,0:T(8,128)(2,1)S(1)} %get-tuple-element.86.refs_2_, bf16[3072,384]{1,0:T(8,128)(2,1)S(1)} %get-tuple-element.87.refs_3_, ...), custom_call_target="tpu_custom_call" | custom-call | flops 1000 | bytes 1000 | tf_op jit(solution)/shard_map/down_mine/pallas_call | solution.py:92
  42.2 0.0 collective-permute-done.5.refs_0_
  42.2 0.0 copy-start.12
  42.2 2.8 %down_other.2.refs_2_ = bf16[32,3072]{1,0:T(8,128)(2,1)S(1)} custom-call(bf16[32,3072]{1,0:T(8,128)(2,1)S(1)} %collective-permute-done.5.refs_0_, bf16[3072,384]{1,0:T(8,128)(2,1)S(1)} %get-tuple-element.77.refs_1_.refs_3_, bf16[3072,384]{1,0:T(8,128)(2,1)S(1)} %get-tuple-element.78.refs_2_.refs_4_, bf16[3072,384]{1,0:T(8,128)(2,1)S(1)} %get-tuple-element.79.refs_3_.refs_5_, ...), custom_call_target="tpu_custom_call" | custom-call | flops 1000 | bytes 1000 | tf_op jit(solution)/shard_map/down_other/pallas_call | solution.py:92
  45.1 3.7 %collective-permute-start.6 = (bf16[8,3072]{1,0:T(8,128)(2,1)S(1)}, bf16[8,3072]{1,0:T(8,128)(2,1)S(1)}, u32[]{:S(2)}, u32[]{:S(2)}) collective-permute-start(bf16[8,3072]{1,0:T(8,128)(2,1)S(1)} %get-tuple-element.114), channel_id=1, source_target_pairs={{0,12},{4,8},{8,4},{12,0},{1,13},{5,9},{9,5},{13,1},{2,14},{6,10},... | collective-permute-start | bytes 147464 | tf_op jit(solution)/shard_map/ppermute | solution.py:37
  48.7 0.0 collective-permute-start.8
  48.8 0.8 collective-permute-start.7
  49.5 3.9 %load_other_in.4 = (bf16[8,3072]{1,0:T(8,128)(2,1)S(1)}, bf16[3072,384]{1,0:T(8,128)(2,1)S(1)}, bf16[3072,384]{1,0:T(8,128)(2,1)S(1)}, bf16[3072,384]{1,0:T(8,128)(2,1)S(1)}, bf16[3072,384]{1,0:T(8,128)(2,1)S(1)}) custom-call(bf16[8,3072]{1,0:T(8,128)(2,1)S(1)} %copy-done.12, ...), custom_call_target="tpu_custom_call", output_to_operand_aliasing={{1}: (3, {}), {2}: (4, {}), {3}: (5, {}), {4}: (6, {})} | custom-call | flops 1000 | bytes 1000 | tf_op jit(solution)/shard_map/load_other_in/pallas_call | solution.py:92
  53.4 0.0 collective-permute-done.6
  53.4 0.5 collective-permute-done.8
  53.9 0.4 collective-permute-done.7
  54.3 2.8 %collective-permute-start.11 = (bf16[8,3072]{1,0:T(8,128)(2,1)S(1)}, bf16[8,3072]{1,0:T(8,128)(2,1)S(1)}, u32[]{:S(2)}, u32[]{:S(2)}) collective-permute-start(bf16[8,3072]{1,0:T(8,128)(2,1)S(1)} %add_convert_fusion.3.refs_1_), channel_id=1, source_target_pairs={{0,12},{4,8},{8,4},{12,0},{1,13},{5,9},{9,5},{13,1},{2,14},{6,10},... | collective-permute-start | bytes 147464 | tf_op jit(solution)/shard_map/ppermute | solution.py:37
  57.1 0.2 collective-permute-start.10
  57.3 1.4 %collective-permute-start.9 = (bf16[8,3072]{1,0:T(8,128)(2,1)S(1)}, bf16[8,3072]{1,0:T(8,128)(2,1)S(1)}, u32[]{:S(2)}, u32[]{:S(2)}) collective-permute-start(bf16[8,3072]{1,0:T(8,128)(2,1)S(1)} %add_convert_fusion.3.refs_1_), channel_id=1, source_target_pairs={{0,4},{4,0},{8,12},{12,8},{1,5},{5,1},{9,13},{13,9},{2,6},{6,2},{1... | collective-permute-start | bytes 147464 | tf_op jit(solution)/shard_map/ppermute | solution.py:37
  58.8 3.8 %load_other_in.5 = (bf16[3072,384]{1,0:T(8,128)(2,1)S(1)}, bf16[3072,384]{1,0:T(8,128)(2,1)S(1)}, bf16[3072,384]{1,0:T(8,128)(2,1)S(1)}, bf16[3072,384]{1,0:T(8,128)(2,1)S(1)}) custom-call(bf16[3072,6144]{1,0:T(8,128)(2,1)} %refs_0_.5, ...), custom_call_target="tpu_custom_call", output_to_operand_aliasing={{0}: (2, {}), {1}: (3, {}), {2}: (4, {}), {3}: (5, {})} | custom-call | flops 1000 | bytes 1000 | tf_op jit(solution)/shard_map/load_other_in/pallas_call | solution.py:92
  62.7 3.0 %up_other.3.refs_9_ = bf16[32,3072]{1,0:T(8,128)(2,1)S(1)} custom-call(bf16[32,3072]{1,0:T(8,128)(2,1)S(1)} %pad_maximum_fusion.refs_0_, bf16[3072,384]{1,0:T(8,128)(2,1)S(1)} %get-tuple-element.94.refs_1_.refs_2_, bf16[3072,384]{1,0:T(8,128)(2,1)S(1)} %get-tuple-element.95.refs_2_.refs_3_, bf16[3072,384]{1,0:T(8,128)(2,1)S(1)} %get-tuple-element.96.refs_3_.refs_4_, ...), custom_call_target="tpu_custom_call" | custom-call | flops 1000 | bytes 1000 | tf_op jit(solution)/shard_map/up_other/pallas_call | solution.py:92
  65.7 0.1 collective-permute-start.12
  65.8 0.6 copy-done.7
  66.4 0.7 copy-done.9
  67.1 2.8 %up_mine.3 = bf16[32,3072]{1,0:T(8,128)(2,1)S(1)} custom-call(bf16[32,3072]{1,0:T(8,128)(2,1)S(1)} %pad_maximum_fusion.refs_0_, bf16[3072,384]{1,0:T(8,128)(2,1)S(1)} %get-tuple-element.66.refs_1_, bf16[3072,384]{1,0:T(8,128)(2,1)S(1)} %get-tuple-element.67.refs_2_, bf16[3072,384]{1,0:T(8,128)(2,1)S(1)} %get-tuple-element.68.refs_3_, ...), custom_call_target="tpu_custom_call" | custom-call | flops 1000 | bytes 1000 | tf_op jit(solution)/shard_map/up_mine/pallas_call | solution.py:92
  69.9 0.0 collective-permute-done.12
  70.0 0.7 collective-permute-start.13
  70.7 6.6 %load_other_out.3 = (bf16[32,3072]{1,0:T(8,128)(2,1)S(1)}, bf16[3072,384]{1,0:T(8,128)(2,1)S(1)}, bf16[3072,384]{1,0:T(8,128)(2,1)S(1)}, bf16[3072,384]{1,0:T(8,...) custom-call(bf16[32,3072]{1,0:T(8,128)(2,1)S(1)} %add_convert_fusion, ...), custom_call_target="tpu_custom_call", output_to_operand_aliasing={{1}: (2, {}), {2}: (3, {}), {3}: (4, {}), {4}: (5, {}), {5}... | custom-call | flops 1000 | bytes 1000 | tf_op jit(solution)/shard_map/load_other_out/pallas_call | solution.py:92
  77.4 0.2 fusion.15.refs_0_
  77.6 0.1 collective-permute-start.14
  77.7 2.8 %down_mine.3.refs_9_ = f32[32,3072]{1,0:T(8,128)S(1)} custom-call(bf16[32,3072]{1,0:T(8,128)(2,1)S(1)} %fusion.15.refs_0_, bf16[3072,384]{1,0:T(8,128)(2,1)S(1)} %copy-done.11, bf16[3072,384]{1,0:T(8,128)(2,1)S(1)} %get-tuple-element.86.refs_2_, bf16[3072,384]{1,0:T(8,128)(2,1)S(1)} %get-tuple-element.87.refs_3_, ...), custom_call_target="tpu_custom_call" | custom-call | flops 1000 | bytes 1000 | tf_op jit(solution)/shard_map/down_mine/pallas_call | solution.py:92
  80.5 0.0 collective-permute-done.14.refs_0_
  80.5 2.9 %down_other.3 = bf16[32,3072]{1,0:T(8,128)(2,1)S(1)} custom-call(bf16[32,3072]{1,0:T(8,128)(2,1)S(1)} %collective-permute-done.14.refs_0_, bf16[3072,384]{1,0:T(8,128)(2,1)S(1)} %get-tuple-element.103.refs_1_, bf16[3072,384]{1,0:T(8,128)(2,1)S(1)} %get-tuple-element.104.refs_2_, bf16[3072,384]{1,0:T(8,128)(2,1)S(1)} %get-tuple-element.105.refs_3_, ...), custom_call_target="tpu_custom_call" | custom-call | flops 1000 | bytes 1000 | tf_op jit(solution)/shard_map/down_other/pallas_call | solution.py:92
  83.4 2.8 %collective-permute-start.15 = (bf16[8,3072]{1,0:T(8,128)(2,1)S(1)}, bf16[8,3072]{1,0:T(8,128)(2,1)S(1)}, u32[]{:S(2)}, u32[]{:S(2)}) collective-permute-start(bf16[8,3072]{1,0:T(8,128)(2,1)S(1)} %get-tuple-element.111), channel_id=1, source_target_pairs={{0,12},{4,8},{8,4},{12,0},{1,13},{5,9},{9,5},{13,1},{2,14},{6,10},... | collective-permute-start | bytes 147464 | tf_op jit(solution)/shard_map/ppermute | solution.py:37
  86.2 1.6 %collective-permute-start.16 = (bf16[8,3072]{1,0:T(8,128)(2,1)S(1)}, bf16[8,3072]{1,0:T(8,128)(2,1)S(1)}, u32[]{:S(2)}, u32[]{:S(2)}) collective-permute-start(bf16[8,3072]{1,0:T(8,128)(2,1)S(1)} %get-tuple-element.113), channel_id=1, source_target_pairs={{0,8},{4,12},{8,0},{12,4},{1,9},{5,13},{9,1},{13,5},{2,10},{6,14},... | collective-permute-start | bytes 147464 | tf_op jit(solution)/shard_map/ppermute | solution.py:37
  87.9 1.9 %collective-permute-done.15 = bf16[8,3072]{1,0:T(8,128)(2,1)S(1)} collective-permute-done((bf16[8,3072]{1,0:T(8,128)(2,1)S(1)}, bf16[8,3072]{1,0:T(8,128)(2,1)S(1)}, u32[]{:S(2)}, u32[]{:S(2)}) %collective-permute-start.15) | collective-permute-done | bytes 49184 | tf_op jit(solution)/shard_map/ppermute | solution.py:37
  89.8 1.7 %collective-permute-done.17 = bf16[8,3072]{1,0:T(8,128)(2,1)S(1)} collective-permute-done((bf16[8,3072]{1,0:T(8,128)(2,1)S(1)}, bf16[8,3072]{1,0:T(8,128)(2,1)S(1)}, u32[]{:S(2)}, u32[]{:S(2)}) %collective-permute-start.17) | collective-permute-done | bytes 49184 | tf_op jit(solution)/shard_map/ppermute | solution.py:37
  91.5 0.2 collective-permute-done.16
  91.8 0.7 add_convert_fusion.2
  (40 shorter events, 0.3 us)
Async XLA Ops:
  0.0 13.1 %collective-permute-start.2 = (bf16[8,3072]{1,0:T(8,128)(2,1)}, bf16[8,3072]{1,0:T(8,128)(2,1)S(1)}, u32[]{:S(2)}, u32[]{:S(2)}) collective-permute-start(bf16[8,3072]{1,0:T(8,128)(2,1)} %refs_0_.4), channel_id=1, source_target_pairs={{0,12},{4,8},{8,4},{12,0},{1,13},{5,9},{9,5},{13,1},{2,14},{6,10},... | collective-permute-start | bytes 147464 | tf_op jit(solution)/shard_map/ppermute | solution.py:37
  5.0 8.1 %collective-permute-start.1 = (bf16[8,3072]{1,0:T(8,128)(2,1)}, bf16[8,3072]{1,0:T(8,128)(2,1)S(1)}, u32[]{:S(2)}, u32[]{:S(2)}) collective-permute-start(bf16[8,3072]{1,0:T(8,128)(2,1)} %refs_0_.4), channel_id=1, source_target_pairs={{0,8},{4,12},{8,0},{12,4},{1,9},{5,13},{9,1},{13,5},{2,10},{6,14},... | collective-permute-start | bytes 147464 | tf_op jit(solution)/shard_map/ppermute | solution.py:37
  5.1 8.0 %collective-permute-start = (bf16[8,3072]{1,0:T(8,128)(2,1)}, bf16[8,3072]{1,0:T(8,128)(2,1)S(1)}, u32[]{:S(2)}, u32[]{:S(2)}) collective-permute-start(bf16[8,3072]{1,0:T(8,128)(2,1)} %refs_0_.4), channel_id=1, source_target_pairs={{0,4},{4,0},{8,12},{12,8},{1,5},{5,1},{9,13},{13,9},{2,6},{6,2},{1... | collective-permute-start | bytes 147464 | tf_op jit(solution)/shard_map/ppermute | solution.py:37
  19.8 10.7 %copy-start = (bf16[3072,384]{1,0:T(8,128)(2,1)}, bf16[3072,384]{1,0:T(8,128)(2,1)S(1)}, u32[]{:S(2)}) copy-start(bf16[3072,384]{1,0:T(8,128)(2,1)S(1)} %get-tuple-element.69.refs_4_) | copy-start | bytes 7077892
  19.8 10.7 %copy-start.2 = (bf16[3072,384]{1,0:T(8,128)(2,1)}, bf16[3072,384]{1,0:T(8,128)(2,1)S(1)}, u32[]{:S(2)}) copy-start(bf16[3072,384]{1,0:T(8,128)(2,1)S(1)} %get-tuple-element.70.refs_5_) | copy-start | bytes 7077892
  19.8 10.7 %copy-start.4 = (bf16[3072,384]{1,0:T(8,128)(2,1)}, bf16[3072,384]{1,0:T(8,128)(2,1)S(1)}, u32[]{:S(2)}) copy-start(bf16[3072,384]{1,0:T(8,128)(2,1)S(1)} %get-tuple-element.71.refs_6_) | copy-start | bytes 7077892
  19.9 10.7 %copy-start.6 = (bf16[3072,384]{1,0:T(8,128)(2,1)}, bf16[3072,384]{1,0:T(8,128)(2,1)S(1)}, u32[]{:S(2)}) copy-start(bf16[3072,384]{1,0:T(8,128)(2,1)S(1)} %get-tuple-element.72.refs_7_) | copy-start | bytes 7077892
  19.9 10.7 %copy-start.8 = (bf16[3072,384]{1,0:T(8,128)(2,1)}, bf16[3072,384]{1,0:T(8,128)(2,1)S(1)}, u32[]{:S(2)}) copy-start(bf16[3072,384]{1,0:T(8,128)(2,1)S(1)} %get-tuple-element.73.refs_8_) | copy-start | bytes 7077892
  19.9 10.7 %collective-permute-start.3 = (bf16[32,3072]{1,0:T(8,128)(2,1)S(1)}, bf16[32,3072]{1,0:T(8,128)(2,1)S(1)}, u32[]{:S(2)}, u32[]{:S(2)}) collective-permute-start(bf16[32,3072]{1,0:T(8,128)(2,1)S(1)} %get-tuple-element.74.refs_10_), channel_id=1, source_target_pairs={{0,1},{1,0},{2,3},{3,2},{4,5},{5,4},{6,7},{7,6},{8,9},{9,8},{10,11... | collective-permute-start | bytes 589832 | tf_op jit(solution)/shard_map/ppermute | solution.py:37
  30.6 8.8 %copy-start.10 = (bf16[3072,384]{1,0:T(8,128)(2,1)}, bf16[3072,384]{1,0:T(8,128)(2,1)S(1)}, u32[]{:S(2)}) copy-start(bf16[3072,384]{1,0:T(8,128)(2,1)S(1)} %get-tuple-element.85.refs_1_) | copy-start | bytes 7077892
  30.7 8.4 %collective-permute-start.4 = (bf16[32,3072]{1,0:T(8,128)(2,1)S(1)}, bf16[32,3072]{1,0:T(8,128)(2,1)S(1)}, u32[]{:S(2)}, u32[]{:S(2)}) collective-permute-start(bf16[32,3072]{1,0:T(8,128)(2,1)S(1)} %add_convert_fusion.1.refs_0_), channel_id=1, source_target_pairs={{0,2},{1,3},{2,0},{3,1},{4,6},{5,7},{6,4},{7,5},{8,10},{9,11},{10,... | collective-permute-start | bytes 589832 | tf_op jit(solution)/shard_map/ppermute | solution.py:37
  39.3 2.9 %collective-permute-start.5 = (bf16[32,3072]{1,0:T(8,128)(2,1)S(1)}, bf16[32,3072]{1,0:T(8,128)(2,1)S(1)}, u32[]{:S(2)}, u32[]{:S(2)}) collective-permute-start(bf16[32,3072]{1,0:T(8,128)(2,1)S(1)} %fusion.7.refs_0_), channel_id=1, source_target_pairs={{0,1},{1,0},{2,3},{3,2},{4,5},{5,4},{6,7},{7,6},{8,9},{9,8},{10,11... | collective-permute-start | bytes 589832 | tf_op jit(solution)/shard_map/ppermute | solution.py:37
  42.2 7.3 %copy-start.12 = (bf16[8,3072]{1,0:T(8,128)(2,1)S(1)}, bf16[8,3072]{1,0:T(8,128)(2,1)}, u32[]{:S(2)}) copy-start(bf16[8,3072]{1,0:T(8,128)(2,1)} %refs_0_.4) | copy-start | bytes 147460
  45.1 8.3 %collective-permute-start.6 = (bf16[8,3072]{1,0:T(8,128)(2,1)S(1)}, bf16[8,3072]{1,0:T(8,128)(2,1)S(1)}, u32[]{:S(2)}, u32[]{:S(2)}) collective-permute-start(bf16[8,3072]{1,0:T(8,128)(2,1)S(1)} %get-tuple-element.114), channel_id=1, source_target_pairs={{0,12},{4,8},{8,4},{12,0},{1,13},{5,9},{9,5},{13,1},{2,14},{6,10},... | collective-permute-start | bytes 147464 | tf_op jit(solution)/shard_map/ppermute | solution.py:37
  48.7 5.1 %collective-permute-start.8 = (bf16[8,3072]{1,0:T(8,128)(2,1)S(1)}, bf16[8,3072]{1,0:T(8,128)(2,1)S(1)}, u32[]{:S(2)}, u32[]{:S(2)}) collective-permute-start(bf16[8,3072]{1,0:T(8,128)(2,1)S(1)} %get-tuple-element.115), channel_id=1, source_target_pairs={{0,4},{4,0},{8,12},{12,8},{1,5},{5,1},{9,13},{13,9},{2,6},{6,2},{1... | collective-permute-start | bytes 147464 | tf_op jit(solution)/shard_map/ppermute | solution.py:37
  48.8 5.5 %collective-permute-start.7 = (bf16[8,3072]{1,0:T(8,128)(2,1)S(1)}, bf16[8,3072]{1,0:T(8,128)(2,1)S(1)}, u32[]{:S(2)}, u32[]{:S(2)}) collective-permute-start(bf16[8,3072]{1,0:T(8,128)(2,1)S(1)} %get-tuple-element.116), channel_id=1, source_target_pairs={{0,8},{4,12},{8,0},{12,4},{1,9},{5,13},{9,1},{13,5},{2,10},{6,14},... | collective-permute-start | bytes 147464 | tf_op jit(solution)/shard_map/ppermute | solution.py:37
  54.3 8.3 %collective-permute-start.11 = (bf16[8,3072]{1,0:T(8,128)(2,1)S(1)}, bf16[8,3072]{1,0:T(8,128)(2,1)S(1)}, u32[]{:S(2)}, u32[]{:S(2)}) collective-permute-start(bf16[8,3072]{1,0:T(8,128)(2,1)S(1)} %add_convert_fusion.3.refs_1_), channel_id=1, source_target_pairs={{0,12},{4,8},{8,4},{12,0},{1,13},{5,9},{9,5},{13,1},{2,14},{6,10},... | collective-permute-start | bytes 147464 | tf_op jit(solution)/shard_map/ppermute | solution.py:37
  57.1 5.5 %collective-permute-start.10 = (bf16[8,3072]{1,0:T(8,128)(2,1)S(1)}, bf16[8,3072]{1,0:T(8,128)(2,1)S(1)}, u32[]{:S(2)}, u32[]{:S(2)}) collective-permute-start(bf16[8,3072]{1,0:T(8,128)(2,1)S(1)} %add_convert_fusion.3.refs_1_), channel_id=1, source_target_pairs={{0,8},{4,12},{8,0},{12,4},{1,9},{5,13},{9,1},{13,5},{2,10},{6,14},... | collective-permute-start | bytes 147464 | tf_op jit(solution)/shard_map/ppermute | solution.py:37
  57.3 5.3 %collective-permute-start.9 = (bf16[8,3072]{1,0:T(8,128)(2,1)S(1)}, bf16[8,3072]{1,0:T(8,128)(2,1)S(1)}, u32[]{:S(2)}, u32[]{:S(2)}) collective-permute-start(bf16[8,3072]{1,0:T(8,128)(2,1)S(1)} %add_convert_fusion.3.refs_1_), channel_id=1, source_target_pairs={{0,4},{4,0},{8,12},{12,8},{1,5},{5,1},{9,13},{13,9},{2,6},{6,2},{1... | collective-permute-start | bytes 147464 | tf_op jit(solution)/shard_map/ppermute | solution.py:37
  62.7 3.1 %copy-start.1 = (bf16[3072,384]{1,0:T(8,128)(2,1)S(1)}, bf16[3072,384]{1,0:T(8,128)(2,1)}, u32[]{:S(2)}) copy-start(bf16[3072,384]{1,0:T(8,128)(2,1)} %copy-done) | copy-start | bytes 7077892
  62.7 3.1 %copy-start.3 = (bf16[3072,384]{1,0:T(8,128)(2,1)S(1)}, bf16[3072,384]{1,0:T(8,128)(2,1)}, u32[]{:S(2)}) copy-start(bf16[3072,384]{1,0:T(8,128)(2,1)} %copy-done.2) | copy-start | bytes 7077892
  62.7 3.1 %copy-start.5 = (bf16[3072,384]{1,0:T(8,128)(2,1)S(1)}, bf16[3072,384]{1,0:T(8,128)(2,1)}, u32[]{:S(2)}) copy-start(bf16[3072,384]{1,0:T(8,128)(2,1)} %copy-done.4) | copy-start | bytes 7077892
  62.7 3.7 %copy-start.7 = (bf16[3072,384]{1,0:T(8,128)(2,1)S(1)}, bf16[3072,384]{1,0:T(8,128)(2,1)}, u32[]{:S(2)}) copy-start(bf16[3072,384]{1,0:T(8,128)(2,1)} %copy-done.6) | copy-start | bytes 7077892
  62.7 4.4 %copy-start.9 = (bf16[3072,384]{1,0:T(8,128)(2,1)S(1)}, bf16[3072,384]{1,0:T(8,128)(2,1)}, u32[]{:S(2)}) copy-start(bf16[3072,384]{1,0:T(8,128)(2,1)} %copy-done.8) | copy-start | bytes 7077892
  65.7 4.2 %collective-permute-start.12 = (bf16[32,3072]{1,0:T(8,128)(2,1)S(1)}, bf16[32,3072]{1,0:T(8,128)(2,1)S(1)}, u32[]{:S(2)}, u32[]{:S(2)}) collective-permute-start(bf16[32,3072]{1,0:T(8,128)(2,1)S(1)} %up_other.3.refs_9_), channel_id=1, source_target_pairs={{0,1},{1,0},{2,3},{3,2},{4,5},{5,4},{6,7},{7,6},{8,9},{9,8},{10,11... | collective-permute-start | bytes 589832 | tf_op jit(solution)/shard_map/ppermute | solution.py:37
  70.0 7.6 %copy-start.11 = (bf16[3072,384]{1,0:T(8,128)(2,1)S(1)}, bf16[3072,384]{1,0:T(8,128)(2,1)}, u32[]{:S(2)}) copy-start(bf16[3072,384]{1,0:T(8,128)(2,1)} %copy-done.10) | copy-start | bytes 7077892
  70.0 7.4 %collective-permute-start.13 = (bf16[32,3072]{1,0:T(8,128)(2,1)S(1)}, bf16[32,3072]{1,0:T(8,128)(2,1)S(1)}, u32[]{:S(2)}, u32[]{:S(2)}) collective-permute-start(bf16[32,3072]{1,0:T(8,128)(2,1)S(1)} %add_convert_fusion.refs_0_), channel_id=1, source_target_pairs={{0,2},{1,3},{2,0},{3,1},{4,6},{5,7},{6,4},{7,5},{8,10},{9,11},{10,... | collective-permute-start | bytes 589832 | tf_op jit(solution)/shard_map/ppermute | solution.py:37
  77.6 2.9 %collective-permute-start.14 = (bf16[32,3072]{1,0:T(8,128)(2,1)S(1)}, bf16[32,3072]{1,0:T(8,128)(2,1)S(1)}, u32[]{:S(2)}, u32[]{:S(2)}) collective-permute-start(bf16[32,3072]{1,0:T(8,128)(2,1)S(1)} %fusion.15.refs_0_), channel_id=1, source_target_pairs={{0,1},{1,0},{2,3},{3,2},{4,5},{5,4},{6,7},{7,6},{8,9},{9,8},{10,11... | collective-permute-start | bytes 589832 | tf_op jit(solution)/shard_map/ppermute | solution.py:37
  83.4 6.4 %collective-permute-start.15 = (bf16[8,3072]{1,0:T(8,128)(2,1)S(1)}, bf16[8,3072]{1,0:T(8,128)(2,1)S(1)}, u32[]{:S(2)}, u32[]{:S(2)}) collective-permute-start(bf16[8,3072]{1,0:T(8,128)(2,1)S(1)} %get-tuple-element.111), channel_id=1, source_target_pairs={{0,12},{4,8},{8,4},{12,0},{1,13},{5,9},{9,5},{13,1},{2,14},{6,10},... | collective-permute-start | bytes 147464 | tf_op jit(solution)/shard_map/ppermute | solution.py:37
  86.2 5.3 %collective-permute-start.17 = (bf16[8,3072]{1,0:T(8,128)(2,1)S(1)}, bf16[8,3072]{1,0:T(8,128)(2,1)S(1)}, u32[]{:S(2)}, u32[]{:S(2)}) collective-permute-start(bf16[8,3072]{1,0:T(8,128)(2,1)S(1)} %get-tuple-element.112), channel_id=1, source_target_pairs={{0,4},{4,0},{8,12},{12,8},{1,5},{5,1},{9,13},{13,9},{2,6},{6,2},{1... | collective-permute-start | bytes 147464 | tf_op jit(solution)/shard_map/ppermute | solution.py:37
  86.2 5.5 %collective-permute-start.16 = (bf16[8,3072]{1,0:T(8,128)(2,1)S(1)}, bf16[8,3072]{1,0:T(8,128)(2,1)S(1)}, u32[]{:S(2)}, u32[]{:S(2)}) collective-permute-start(bf16[8,3072]{1,0:T(8,128)(2,1)S(1)} %get-tuple-element.113), channel_id=1, source_target_pairs={{0,8},{4,12},{8,0},{12,4},{1,9},{5,13},{9,1},{13,5},{2,10},{6,14},... | collective-permute-start | bytes 147464 | tf_op jit(solution)/shard_map/ppermute | solution.py:37

commit v4 on v3

--- a/solution.py
+++ b/solution.py
@@ -8,6 +8,7 @@
 STEPS = 2
 BLOCKS = 8
 EARLY = 4
+WITH_UP = 4
 bf16, f32 = jnp.bfloat16, jnp.float32
 
 
@@ -119,23 +120,33 @@
             total = total + swap(part[k * rows : (k + 1) * rows], "hidden", nz, k).astype(f32)
         return (old.astype(f32) + total).astype(bf16)
 
+    def rows_of(x):
+        far = swap(x, "hidden", nz, 2)
+        x, first = stage([], [load(w_in, 1, -1, 0, BLOCKS // 2)], "load_other_in", carry=x)
+        near = swap(jnp.concatenate([x, far], 0), "hidden", nz, 1)
+        x, second = stage([], [load(w_in, 1, -1, BLOCKS // 2, BLOCKS)], "load_other_in", [far], carry=x)
+        return jnp.concatenate([x, near[:rows], far, near[rows:]], 0), first + second
+
     state = tokens
-    x = gather(state, nz)
-    (other_in,) = stage([], [load(w_in, 1, -1)], "load_other_in")
+    x, other_in = rows_of(state)
     for step in range(STEPS):
         first, last = step == 0, step + 1 == STEPS
         sent, got = stage([(x, other_in)], [load(w_in, 1, 1)] if first else [], "up_other")
         mine_in = got if first else mine_in
-        kept, got = stage([(x, mine_in)], [load(w_out, 0, 1)] if first else [], "up_mine", [sent])
+        kept, got = stage([(x, mine_in)], [load(w_out, 0, 1, 0, WITH_UP)] if first else [], "up_mine", [sent])
         mine_out = got if first else mine_out
         chip = (kept.astype(f32) + swap(sent, "width", nw, 1).astype(f32)).astype(bf16)
         across = swap(chip, "width", nw, 2)
-        chip, other_out = stage([], [load(w_out, 0, -1)], "load_other_out", carry=chip, over=other_in)
+        begun = WITH_UP if first else BLOCKS
+        wanted = [load(w_out, 0, 1, begun, BLOCKS)] * (begun < BLOCKS) + [load(w_out, 0, -1, 0, begun)]
+        chip, got = stage([], wanted, "load_out", carry=chip, over=other_in)
+        mine_out, other_out = mine_out + got[: BLOCKS - begun], got[BLOCKS - begun :]
         total = chip.astype(f32) + across.astype(f32)
         mine = jax.nn.gelu(total, approximate=True).astype(bf16)
         other = swap(mine, "width", nw, 1)
-        part, _ = stage([(mine, mine_out)], [], "down_mine", [], None, f32)
-        part, _ = stage([(other, other_out)], [], "down_other", [], part)
+        part, got = stage([(mine, mine_out)], [load(w_out, 0, -1, begun, BLOCKS)] if first else [], "down_mine", [], None, f32)
+        part, _ = stage([(other, other_out + got)], [], "down_other", [], part)
+        other_out = other_out + got
         if last:
             state = scattered(part, state, part[:rows].astype(f32))
         else:

time: 92.6 us -> 90.8 us (0.981)
  waiting for transfers between devices: 4.8 us -> 3.73 us
    ppermute x18 -> x17, waiting for transfers between devices: 4.8 us -> 3.73 us  [swap(): return lax.ppermute(x, axis, [(i, i ^ mask) for i in range(n)])]
    pallas_call x13 -> x14, Pallas kernels: 62 us -> 61.4 us  [stage(): pl.pallas_call(kernel, out_shape=shapes, in_specs=[vmem] * n_g + [hbm] *...]
    ppermute x18 -> x17, starting transfers between devices: 21.7 us -> 21.6 us  [swap(): return lax.ppermute(x, axis, [(i, i ^ mask) for i in range(n)])]
    unnamed x29 -> x28, local copies, waits for them, and re-layouts: 2.18 us -> 2.16 us
  transfers between devices with their start and end apart: 18 -> 17, of which waited for: 5 -> 3; matrix products, arithmetic and copies ran while one was open for 1% -> 0% of each run, Pallas kernels for 50% -> 51%
where the time goes in v4:
time: 90.8 us; the launch traced here: 90.6 us
  Pallas kernels  61.4 us (68%)
  starting transfers between devices  21.6 us (24%)
  waiting for transfers between devices  3.73 us (4%)
  local copies, waits for them, and re-layouts  2.2 us (2%)
  other arithmetic  1.18 us (1%)
    pallas_call x14, Pallas kernels, stage(): pl.pallas_call(kernel, out_shape=shapes, in_specs=[vmem] * n_g + [hbm] *...  61.4 us
    ppermute x17, starting transfers between devices, swap(): return lax.ppermute(x, axis, [(i, i ^ mask) for i in range(n)])  21.6 us
    ppermute x17, waiting for transfers between devices, swap(): return lax.ppermute(x, axis, [(i, i ^ mask) for i in range(n)])  3.73 us
    unnamed x28, local copies, waits for them, and re-layouts  2.16 us
  transfers between devices with their start and end apart: 17, of which 3 were waited for; matrix products, arithmetic and copies ran while one was open for 0% of the time, Pallas kernels for 51%

profile of v4, /device:TPU:0, one launch (start us, length us, event | category | flops | bytes accessed | tf_op | source)
XLA Modules:
  0.0 90.6 jit_solution(13206503406433418842)
XLA Ops:
  0.0 4.0 %collective-permute-start = (bf16[8,3072]{1,0:T(8,128)(2,1)}, bf16[8,3072]{1,0:T(8,128)(2,1)S(1)}, u32[]{:S(2)}, u32[]{:S(2)}) collective-permute-start(bf16[8,3072]{1,0:T(8,128)(2,1)} %refs_0_.4), channel_id=1, source_target_pairs={{0,8},{4,12},{8,0},{12,4},{1,9},{5,13},{9,1},{13,5},{2,10},{6,14},... | collective-permute-start | bytes 147464 | tf_op jit(solution)/shard_map/ppermute | solution.py:38
  4.0 0.8 copy-done.12
  4.9 3.8 %load_other_in.4 = (bf16[8,3072]{1,0:T(8,128)(2,1)S(1)}, bf16[3072,384]{1,0:T(8,128)(2,1)S(1)}, bf16[3072,384]{1,0:T(8,128)(2,1)S(1)}, bf16[3072,384]{1,0:T(8,128)(2,1)S(1)}, bf16[3072,384]{1,0:T(8,128)(2,1)S(1)}) custom-call(bf16[8,3072]{1,0:T(8,128)(2,1)S(1)} %copy-done.12, bf16[3072,6144]{1,0:T(8,128)(2,1)} %refs_0_.5), custom_call_target="tpu_custom_call" | custom-call | flops 1000 | bytes 1000 | tf_op jit(solution)/shard_map/load_other_in/pallas_call | solution.py:93
  8.7 0.0 collective-permute-done.refs_2_
  8.8 1.6 %collective-permute-start.1 = (bf16[16,3072]{1,0:T(8,128)(2,1)S(1)}, bf16[16,3072]{1,0:T(8,128)(2,1)S(1)}, u32[]{:S(2)}, u32[]{:S(2)}) collective-permute-start(bf16[16,3072]{1,0:T(8,128)(2,1)S(1)} %pad_maximum_fusion.2), channel_id=1, source_target_pairs={{0,4},{4,0},{8,12},{12,8},{1,5},{5,1},{9,13},{13,9},{2,6},{6,2},{1... | collective-permute-start | bytes 294920 | tf_op jit(solution)/shard_map/ppermute | solution.py:38
  10.4 3.8 %load_other_in.5 = (bf16[8,3072]{1,0:T(8,128)(2,1)S(1)}, bf16[3072,384]{1,0:T(8,128)(2,1)S(1)}, bf16[3072,384]{1,0:T(8,128)(2,1)S(1)}, bf16[3072,384]{1,0:T(8,128)(2,1)S(1)}, bf16[3072,384]{1,0:T(8,128)(2,1)S(1)}) custom-call(bf16[8,3072]{1,0:T(8,128)(2,1)S(1)} %get-tuple-element.61.refs_0_, bf16[3072,6144]{1,0:T(8,128)(2,1)} %refs_0_.5, ...), custom_call_target="tpu_custom_call" | custom-call | flops 1000 | bytes 1000 | tf_op jit(solution)/shard_map/load_other_in/pallas_call | solution.py:93
  14.3 6.7 %up_other.2 = (bf16[32,3072]{1,0:T(8,128)(2,1)S(1)}, bf16[3072,384]{1,0:T(8,128)(2,1)S(1)}, bf16[3072,384]{1,0:T(8,128)(2,1)S(1)}, bf16[3072,384]{1,0:T(8,128)(2...) custom-call(bf16[32,3072]{1,0:T(8,128)(2,1)S(1)} %pad_maximum_fusion, ...), custom_call_target="tpu_custom_call" | custom-call | flops 1000 | bytes 1000 | tf_op jit(solution)/shard_map/up_other/pallas_call | solution.py:93
  21.0 0.1 collective-permute-start.2
  21.1 7.8 %up_mine.2 = (bf16[32,3072]{1,0:T(8,128)(2,1)S(1)}, bf16[3072,384]{1,0:T(8,128)(2,1)S(1)}, bf16[3072,384]{1,0:T(8,128)(2,1)S(1)}, bf16[3072,384]{1,0:T(8,128)(2,1)S(1)}, bf16[3072,384]{1,0:T(8,128)(2,1)S(1)}) custom-call(bf16[32,3072]{1,0:T(8,128)(2,1)S(1)} %pad_maximum_fusion.refs_0_, bf16[3072,384]{1,0:T(8,128)(2,1)S(1)} %get-tuple-element.71.refs_1_, ...), custom_call_target="tpu_custom_call" | custom-call | flops 1000 | bytes 1000 | tf_op jit(solution)/shard_map/up_mine/pallas_call | solution.py:93
  29.0 1.6 %collective-permute-start.3 = (bf16[32,3072]{1,0:T(8,128)(2,1)S(1)}, bf16[32,3072]{1,0:T(8,128)(2,1)S(1)}, u32[]{:S(2)}, u32[]{:S(2)}) collective-permute-start(bf16[32,3072]{1,0:T(8,128)(2,1)S(1)} %add_convert_fusion.1.refs_0_), channel_id=1, source_target_pairs={{0,2},{1,3},{2,0},{3,1},{4,6},{5,7},{6,4},{7,5},{8,10},{9,11},{10,... | collective-permute-start | bytes 589832 | tf_op jit(solution)/shard_map/ppermute | solution.py:38
  30.6 6.6 %load_out.2 = (bf16[32,3072]{1,0:T(8,128)(2,1)S(1)}, bf16[3072,384]{1,0:T(8,128)(2,1)S(1)}, bf16[3072,384]{1,0:T(8,128)(2,1)S(1)}, bf16[3072,384]{1,0:T(8,128)(2...) custom-call(bf16[32,3072]{1,0:T(8,128)(2,1)S(1)} %add_convert_fusion, ...), custom_call_target="tpu_custom_call", output_to_operand_aliasing={{1}: (3, {}), {2}: (4, {}), {3}: (5, {}), {4}: (6, {}), {5}... | custom-call | flops 1000 | bytes 1000 | tf_op jit(solution)/shard_map/load_out/pallas_call | solution.py:93
  37.2 0.0 collective-permute-done.3
  37.2 0.2 fusion.7.refs_0_
  37.4 0.1 collective-permute-start.4
  37.5 3.9 %down_mine.2 = (f32[32,3072]{1,0:T(8,128)S(1)}, bf16[3072,384]{1,0:T(8,128)(2,1)S(1)}, bf16[3072,384]{1,0:T(8,128)(2,1)S(1)}, bf16[3072,384]{1,0:T(8,128)(2,1)S(1)}, bf16[3072,384]{1,0:T(8,128)(2,1)S(1)}) custom-call(bf16[32,3072]{1,0:T(8,128)(2,1)S(1)} %fusion.7.refs_0_, bf16[3072,384]{1,0:T(8,128)(2,1)S(1)} %get-tuple-element.86.refs_1_, ...), custom_call_target="tpu_custom_call" | custom-call | flops 1000 | bytes 1000 | tf_op jit(solution)/shard_map/down_mine/pallas_call | solution.py:93
  41.4 0.0 collective-permute-done.4.refs_0_
  41.4 0.0 copy-start.13
  41.4 2.9 %down_other.2.refs_2_ = bf16[32,3072]{1,0:T(8,128)(2,1)S(1)} custom-call(bf16[32,3072]{1,0:T(8,128)(2,1)S(1)} %collective-permute-done.4.refs_0_, bf16[3072,384]{1,0:T(8,128)(2,1)S(1)} %get-tuple-element.82.refs_1_.refs_3_, bf16[3072,384]{1,0:T(8,128)(2,1)S(1)} %get-tuple-element.83.refs_2_.refs_4_, bf16[3072,384]{1,0:T(8,128)(2,1)S(1)} %get-tuple-element.84.refs_3_.refs_5_, ...), custom_call_target="tpu_custom_call" | custom-call | flops 1000 | bytes 1000 | tf_op jit(solution)/shard_map/down_other/pallas_call | solution.py:93
  44.3 1.1 %collective-permute-start.5 = (bf16[8,3072]{1,0:T(8,128)(2,1)S(1)}, bf16[8,3072]{1,0:T(8,128)(2,1)S(1)}, u32[]{:S(2)}, u32[]{:S(2)}) collective-permute-start(bf16[8,3072]{1,0:T(8,128)(2,1)S(1)} %get-tuple-element.120), channel_id=1, source_target_pairs={{0,12},{4,8},{8,4},{12,0},{1,13},{5,9},{9,5},{13,1},{2,14},{6,10},... | collective-permute-start | bytes 147464 | tf_op jit(solution)/shard_map/ppermute | solution.py:38
  45.4 0.4 collective-permute-start.7
  45.8 2.9 %collective-permute-start.6 = (bf16[8,3072]{1,0:T(8,128)(2,1)S(1)}, bf16[8,3072]{1,0:T(8,128)(2,1)S(1)}, u32[]{:S(2)}, u32[]{:S(2)}) collective-permute-start(bf16[8,3072]{1,0:T(8,128)(2,1)S(1)} %get-tuple-element.122), channel_id=1, source_target_pairs={{0,8},{4,12},{8,0},{12,4},{1,9},{5,13},{9,1},{13,5},{2,10},{6,14},... | collective-permute-start | bytes 147464 | tf_op jit(solution)/shard_map/ppermute | solution.py:38
  48.8 3.9 %load_other_in.6 = (bf16[8,3072]{1,0:T(8,128)(2,1)S(1)}, bf16[3072,384]{1,0:T(8,128)(2,1)S(1)}, bf16[3072,384]{1,0:T(8,128)(2,1)S(1)}, bf16[3072,384]{1,0:T(8,128)(2,1)S(1)}, bf16[3072,384]{1,0:T(8,128)(2,1)S(1)}) custom-call(bf16[8,3072]{1,0:T(8,128)(2,1)S(1)} %copy-done.13, ...), custom_call_target="tpu_custom_call", output_to_operand_aliasing={{1}: (3, {}), {2}: (4, {}), {3}: (5, {}), {4}: (6, {})} | custom-call | flops 1000 | bytes 1000 | tf_op jit(solution)/shard_map/load_other_in/pallas_call | solution.py:93
  52.6 0.0 collective-permute-done.5
  52.6 0.0 collective-permute-done.6
  52.7 1.1 %collective-permute-start.10 = (bf16[8,3072]{1,0:T(8,128)(2,1)S(1)}, bf16[8,3072]{1,0:T(8,128)(2,1)S(1)}, u32[]{:S(2)}, u32[]{:S(2)}) collective-permute-start(bf16[8,3072]{1,0:T(8,128)(2,1)S(1)} %add_convert_fusion.3.refs_1_), channel_id=1, source_target_pairs={{0,12},{4,8},{8,4},{12,0},{1,13},{5,9},{9,5},{13,1},{2,14},{6,10},... | collective-permute-start | bytes 147464 | tf_op jit(solution)/shard_map/ppermute | solution.py:38
  53.8 0.7 collective-permute-start.9
  54.5 2.6 %collective-permute-start.8 = (bf16[8,3072]{1,0:T(8,128)(2,1)S(1)}, bf16[8,3072]{1,0:T(8,128)(2,1)S(1)}, u32[]{:S(2)}, u32[]{:S(2)}) collective-permute-start(bf16[8,3072]{1,0:T(8,128)(2,1)S(1)} %add_convert_fusion.3.refs_1_), channel_id=1, source_target_pairs={{0,4},{4,0},{8,12},{12,8},{1,5},{5,1},{9,13},{13,9},{2,6},{6,2},{1... | collective-permute-start | bytes 147464 | tf_op jit(solution)/shard_map/ppermute | solution.py:38
  57.1 3.8 %load_other_in.7 = (bf16[3072,384]{1,0:T(8,128)(2,1)S(1)}, bf16[3072,384]{1,0:T(8,128)(2,1)S(1)}, bf16[3072,384]{1,0:T(8,128)(2,1)S(1)}, bf16[3072,384]{1,0:T(8,128)(2,1)S(1)}) custom-call(bf16[3072,6144]{1,0:T(8,128)(2,1)} %refs_0_.5, ...), custom_call_target="tpu_custom_call", output_to_operand_aliasing={{0}: (2, {}), {1}: (3, {}), {2}: (4, {}), {3}: (5, {})} | custom-call | flops 1000 | bytes 1000 | tf_op jit(solution)/shard_map/load_other_in/pallas_call | solution.py:93
  61.0 0.0 collective-permute-done.8
  61.1 3.0 %up_other.3.refs_9_ = bf16[32,3072]{1,0:T(8,128)(2,1)S(1)} custom-call(bf16[32,3072]{1,0:T(8,128)(2,1)S(1)} %pad_maximum_fusion.1.refs_0_, bf16[3072,384]{1,0:T(8,128)(2,1)S(1)} %get-tuple-element.100.refs_1_.refs_2_, bf16[3072,384]{1,0:T(8,128)(2,1)S(1)} %get-tuple-element.101.refs_2_.refs_3_, bf16[3072,384]{1,0:T(8,128)(2,1)S(1)} %get-tuple-element.102.refs_3_.refs_4_, ...), custom_call_target="tpu_custom_call" | custom-call | flops 1000 | bytes 1000 | tf_op jit(solution)/shard_map/up_other/pallas_call | solution.py:93
  64.1 0.1 collective-permute-start.11
  64.2 0.6 copy-done.7
  64.8 0.7 copy-done.9
  65.5 2.8 %up_mine.3 = bf16[32,3072]{1,0:T(8,128)(2,1)S(1)} custom-call(bf16[32,3072]{1,0:T(8,128)(2,1)S(1)} %pad_maximum_fusion.1.refs_0_, bf16[3072,384]{1,0:T(8,128)(2,1)S(1)} %get-tuple-element.71.refs_1_, bf16[3072,384]{1,0:T(8,128)(2,1)S(1)} %get-tuple-element.72.refs_2_, bf16[3072,384]{1,0:T(8,128)(2,1)S(1)} %get-tuple-element.73.refs_3_, ...), custom_call_target="tpu_custom_call" | custom-call | flops 1000 | bytes 1000 | tf_op jit(solution)/shard_map/up_mine/pallas_call | solution.py:93
  68.3 0.0 collective-permute-done.11
  68.4 0.7 collective-permute-start.12
  69.1 6.6 %load_out.3 = (bf16[32,3072]{1,0:T(8,128)(2,1)S(1)}, bf16[3072,384]{1,0:T(8,128)(2,1)S(1)}, bf16[3072,384]{1,0:T(8,128)(2,1)S(1)}, bf16[3072,384]{1,0:T(8,128)(2...) custom-call(bf16[32,3072]{1,0:T(8,128)(2,1)S(1)} %add_convert_fusion, ...), custom_call_target="tpu_custom_call", output_to_operand_aliasing={{1}: (2, {}), {2}: (3, {}), {3}: (4, {}), {4}: (5, {}), {5}... | custom-call | flops 1000 | bytes 1000 | tf_op jit(solution)/shard_map/load_out/pallas_call | solution.py:93
  75.8 0.2 fusion.15.refs_0_
  76.0 0.1 collective-permute-start.13
  76.0 2.8 %down_mine.3.refs_9_ = f32[32,3072]{1,0:T(8,128)S(1)} custom-call(bf16[32,3072]{1,0:T(8,128)(2,1)S(1)} %fusion.15.refs_0_, bf16[3072,384]{1,0:T(8,128)(2,1)S(1)} %copy-done.11, bf16[3072,384]{1,0:T(8,128)(2,1)S(1)} %get-tuple-element.87.refs_2_, bf16[3072,384]{1,0:T(8,128)(2,1)S(1)} %get-tuple-element.88.refs_3_, ...), custom_call_target="tpu_custom_call" | custom-call | flops 1000 | bytes 1000 | tf_op jit(solution)/shard_map/down_mine/pallas_call | solution.py:93
  78.9 0.0 collective-permute-done.13.refs_0_
  78.9 2.9 %down_other.3 = bf16[32,3072]{1,0:T(8,128)(2,1)S(1)} custom-call(bf16[32,3072]{1,0:T(8,128)(2,1)S(1)} %collective-permute-done.13.refs_0_, bf16[3072,384]{1,0:T(8,128)(2,1)S(1)} %get-tuple-element.109.refs_1_, bf16[3072,384]{1,0:T(8,128)(2,1)S(1)} %get-tuple-element.110.refs_2_, bf16[3072,384]{1,0:T(8,128)(2,1)S(1)} %get-tuple-element.111.refs_3_, ...), custom_call_target="tpu_custom_call" | custom-call | flops 1000 | bytes 1000 | tf_op jit(solution)/shard_map/down_other/pallas_call | solution.py:93
  81.8 1.1 %collective-permute-start.14 = (bf16[8,3072]{1,0:T(8,128)(2,1)S(1)}, bf16[8,3072]{1,0:T(8,128)(2,1)S(1)}, u32[]{:S(2)}, u32[]{:S(2)}) collective-permute-start(bf16[8,3072]{1,0:T(8,128)(2,1)S(1)} %get-tuple-element.117), channel_id=1, source_target_pairs={{0,12},{4,8},{8,4},{12,0},{1,13},{5,9},{9,5},{13,1},{2,14},{6,10},... | collective-permute-start | bytes 147464 | tf_op jit(solution)/shard_map/ppermute | solution.py:38
  83.0 3.3 %collective-permute-start.15 = (bf16[8,3072]{1,0:T(8,128)(2,1)S(1)}, bf16[8,3072]{1,0:T(8,128)(2,1)S(1)}, u32[]{:S(2)}, u32[]{:S(2)}) collective-permute-start(bf16[8,3072]{1,0:T(8,128)(2,1)S(1)} %get-tuple-element.119), channel_id=1, source_target_pairs={{0,8},{4,12},{8,0},{12,4},{1,9},{5,13},{9,1},{13,5},{2,10},{6,14},... | collective-permute-start | bytes 147464 | tf_op jit(solution)/shard_map/ppermute | solution.py:38
  86.3 2.0 %collective-permute-done.14 = bf16[8,3072]{1,0:T(8,128)(2,1)S(1)} collective-permute-done((bf16[8,3072]{1,0:T(8,128)(2,1)S(1)}, bf16[8,3072]{1,0:T(8,128)(2,1)S(1)}, u32[]{:S(2)}, u32[]{:S(2)}) %collective-permute-start.14) | collective-permute-done | bytes 49184 | tf_op jit(solution)/shard_map/ppermute | solution.py:38
  88.3 0.7 collective-permute-done.16
  88.9 1.0 %collective-permute-done.15 = bf16[8,3072]{1,0:T(8,128)(2,1)S(1)} collective-permute-done((bf16[8,3072]{1,0:T(8,128)(2,1)S(1)}, bf16[8,3072]{1,0:T(8,128)(2,1)S(1)}, u32[]{:S(2)}, u32[]{:S(2)}) %collective-permute-start.15) | collective-permute-done | bytes 49184 | tf_op jit(solution)/shard_map/ppermute | solution.py:38
  90.0 0.7 add_convert_fusion.2
  (40 shorter events, 0.3 us)
Async XLA Ops:
  0.0 8.7 %collective-permute-start = (bf16[8,3072]{1,0:T(8,128)(2,1)}, bf16[8,3072]{1,0:T(8,128)(2,1)S(1)}, u32[]{:S(2)}, u32[]{:S(2)}) collective-permute-start(bf16[8,3072]{1,0:T(8,128)(2,1)} %refs_0_.4), channel_id=1, source_target_pairs={{0,8},{4,12},{8,0},{12,4},{1,9},{5,13},{9,1},{13,5},{2,10},{6,14},... | collective-permute-start | bytes 147464 | tf_op jit(solution)/shard_map/ppermute | solution.py:38
  4.0 0.8 copy-start.12
  8.8 5.5 %collective-permute-start.1 = (bf16[16,3072]{1,0:T(8,128)(2,1)S(1)}, bf16[16,3072]{1,0:T(8,128)(2,1)S(1)}, u32[]{:S(2)}, u32[]{:S(2)}) collective-permute-start(bf16[16,3072]{1,0:T(8,128)(2,1)S(1)} %pad_maximum_fusion.2), channel_id=1, source_target_pairs={{0,4},{4,0},{8,12},{12,8},{1,5},{5,1},{9,13},{13,9},{2,6},{6,2},{1... | collective-permute-start | bytes 294920 | tf_op jit(solution)/shard_map/ppermute | solution.py:38
  21.0 7.9 %copy-start = (bf16[3072,384]{1,0:T(8,128)(2,1)}, bf16[3072,384]{1,0:T(8,128)(2,1)S(1)}, u32[]{:S(2)}) copy-start(bf16[3072,384]{1,0:T(8,128)(2,1)S(1)} %get-tuple-element.74.refs_4_) | copy-start | bytes 7077892
  21.0 7.9 %copy-start.2 = (bf16[3072,384]{1,0:T(8,128)(2,1)}, bf16[3072,384]{1,0:T(8,128)(2,1)S(1)}, u32[]{:S(2)}) copy-start(bf16[3072,384]{1,0:T(8,128)(2,1)S(1)} %get-tuple-element.75.refs_5_) | copy-start | bytes 7077892
  21.0 7.9 %copy-start.4 = (bf16[3072,384]{1,0:T(8,128)(2,1)}, bf16[3072,384]{1,0:T(8,128)(2,1)S(1)}, u32[]{:S(2)}) copy-start(bf16[3072,384]{1,0:T(8,128)(2,1)S(1)} %get-tuple-element.76.refs_6_) | copy-start | bytes 7077892
  21.0 7.9 %copy-start.6 = (bf16[3072,384]{1,0:T(8,128)(2,1)}, bf16[3072,384]{1,0:T(8,128)(2,1)S(1)}, u32[]{:S(2)}) copy-start(bf16[3072,384]{1,0:T(8,128)(2,1)S(1)} %get-tuple-element.77.refs_7_) | copy-start | bytes 7077892
  21.0 7.9 %copy-start.8 = (bf16[3072,384]{1,0:T(8,128)(2,1)}, bf16[3072,384]{1,0:T(8,128)(2,1)S(1)}, u32[]{:S(2)}) copy-start(bf16[3072,384]{1,0:T(8,128)(2,1)S(1)} %get-tuple-element.78.refs_8_) | copy-start | bytes 7077892
  21.0 7.9 %collective-permute-start.2 = (bf16[32,3072]{1,0:T(8,128)(2,1)S(1)}, bf16[32,3072]{1,0:T(8,128)(2,1)S(1)}, u32[]{:S(2)}, u32[]{:S(2)}) collective-permute-start(bf16[32,3072]{1,0:T(8,128)(2,1)S(1)} %get-tuple-element.79.refs_10_), channel_id=1, source_target_pairs={{0,1},{1,0},{2,3},{3,2},{4,5},{5,4},{6,7},{7,6},{8,9},{9,8},{10,11... | collective-permute-start | bytes 589832 | tf_op jit(solution)/shard_map/ppermute | solution.py:38
  28.9 8.6 %copy-start.10 = (bf16[3072,384]{1,0:T(8,128)(2,1)}, bf16[3072,384]{1,0:T(8,128)(2,1)S(1)}, u32[]{:S(2)}) copy-start(bf16[3072,384]{1,0:T(8,128)(2,1)S(1)} %get-tuple-element.86.refs_1_) | copy-start | bytes 7077892
  29.0 8.2 %collective-permute-start.3 = (bf16[32,3072]{1,0:T(8,128)(2,1)S(1)}, bf16[32,3072]{1,0:T(8,128)(2,1)S(1)}, u32[]{:S(2)}, u32[]{:S(2)}) collective-permute-start(bf16[32,3072]{1,0:T(8,128)(2,1)S(1)} %add_convert_fusion.1.refs_0_), channel_id=1, source_target_pairs={{0,2},{1,3},{2,0},{3,1},{4,6},{5,7},{6,4},{7,5},{8,10},{9,11},{10,... | collective-permute-start | bytes 589832 | tf_op jit(solution)/shard_map/ppermute | solution.py:38
  37.4 4.0 %collective-permute-start.4 = (bf16[32,3072]{1,0:T(8,128)(2,1)S(1)}, bf16[32,3072]{1,0:T(8,128)(2,1)S(1)}, u32[]{:S(2)}, u32[]{:S(2)}) collective-permute-start(bf16[32,3072]{1,0:T(8,128)(2,1)S(1)} %fusion.7.refs_0_), channel_id=1, source_target_pairs={{0,1},{1,0},{2,3},{3,2},{4,5},{5,4},{6,7},{7,6},{8,9},{9,8},{10,11... | collective-permute-start | bytes 589832 | tf_op jit(solution)/shard_map/ppermute | solution.py:38
  41.4 7.4 %copy-start.13 = (bf16[8,3072]{1,0:T(8,128)(2,1)S(1)}, bf16[8,3072]{1,0:T(8,128)(2,1)}, u32[]{:S(2)}) copy-start(bf16[8,3072]{1,0:T(8,128)(2,1)} %refs_0_.4) | copy-start | bytes 147460
  44.3 8.3 %collective-permute-start.5 = (bf16[8,3072]{1,0:T(8,128)(2,1)S(1)}, bf16[8,3072]{1,0:T(8,128)(2,1)S(1)}, u32[]{:S(2)}, u32[]{:S(2)}) collective-permute-start(bf16[8,3072]{1,0:T(8,128)(2,1)S(1)} %get-tuple-element.120), channel_id=1, source_target_pairs={{0,12},{4,8},{8,4},{12,0},{1,13},{5,9},{9,5},{13,1},{2,14},{6,10},... | collective-permute-start | bytes 147464 | tf_op jit(solution)/shard_map/ppermute | solution.py:38
  45.4 7.2 %collective-permute-start.7 = (bf16[8,3072]{1,0:T(8,128)(2,1)S(1)}, bf16[8,3072]{1,0:T(8,128)(2,1)S(1)}, u32[]{:S(2)}, u32[]{:S(2)}) collective-permute-start(bf16[8,3072]{1,0:T(8,128)(2,1)S(1)} %get-tuple-element.121), channel_id=1, source_target_pairs={{0,4},{4,0},{8,12},{12,8},{1,5},{5,1},{9,13},{13,9},{2,6},{6,2},{1... | collective-permute-start | bytes 147464 | tf_op jit(solution)/shard_map/ppermute | solution.py:38
  45.8 6.8 %collective-permute-start.6 = (bf16[8,3072]{1,0:T(8,128)(2,1)S(1)}, bf16[8,3072]{1,0:T(8,128)(2,1)S(1)}, u32[]{:S(2)}, u32[]{:S(2)}) collective-permute-start(bf16[8,3072]{1,0:T(8,128)(2,1)S(1)} %get-tuple-element.122), channel_id=1, source_target_pairs={{0,8},{4,12},{8,0},{12,4},{1,9},{5,13},{9,1},{13,5},{2,10},{6,14},... | collective-permute-start | bytes 147464 | tf_op jit(solution)/shard_map/ppermute | solution.py:38
  52.7 8.3 %collective-permute-start.10 = (bf16[8,3072]{1,0:T(8,128)(2,1)S(1)}, bf16[8,3072]{1,0:T(8,128)(2,1)S(1)}, u32[]{:S(2)}, u32[]{:S(2)}) collective-permute-start(bf16[8,3072]{1,0:T(8,128)(2,1)S(1)} %add_convert_fusion.3.refs_1_), channel_id=1, source_target_pairs={{0,12},{4,8},{8,4},{12,0},{1,13},{5,9},{9,5},{13,1},{2,14},{6,10},... | collective-permute-start | bytes 147464 | tf_op jit(solution)/shard_map/ppermute | solution.py:38
  53.8 7.2 %collective-permute-start.9 = (bf16[8,3072]{1,0:T(8,128)(2,1)S(1)}, bf16[8,3072]{1,0:T(8,128)(2,1)S(1)}, u32[]{:S(2)}, u32[]{:S(2)}) collective-permute-start(bf16[8,3072]{1,0:T(8,128)(2,1)S(1)} %add_convert_fusion.3.refs_1_), channel_id=1, source_target_pairs={{0,8},{4,12},{8,0},{12,4},{1,9},{5,13},{9,1},{13,5},{2,10},{6,14},... | collective-permute-start | bytes 147464 | tf_op jit(solution)/shard_map/ppermute | solution.py:38
  54.5 6.5 %collective-permute-start.8 = (bf16[8,3072]{1,0:T(8,128)(2,1)S(1)}, bf16[8,3072]{1,0:T(8,128)(2,1)S(1)}, u32[]{:S(2)}, u32[]{:S(2)}) collective-permute-start(bf16[8,3072]{1,0:T(8,128)(2,1)S(1)} %add_convert_fusion.3.refs_1_), channel_id=1, source_target_pairs={{0,4},{4,0},{8,12},{12,8},{1,5},{5,1},{9,13},{13,9},{2,6},{6,2},{1... | collective-permute-start | bytes 147464 | tf_op jit(solution)/shard_map/ppermute | solution.py:38
  61.1 3.1 %copy-start.1 = (bf16[3072,384]{1,0:T(8,128)(2,1)S(1)}, bf16[3072,384]{1,0:T(8,128)(2,1)}, u32[]{:S(2)}) copy-start(bf16[3072,384]{1,0:T(8,128)(2,1)} %copy-done) | copy-start | bytes 7077892
  61.1 3.1 %copy-start.3 = (bf16[3072,384]{1,0:T(8,128)(2,1)S(1)}, bf16[3072,384]{1,0:T(8,128)(2,1)}, u32[]{:S(2)}) copy-start(bf16[3072,384]{1,0:T(8,128)(2,1)} %copy-done.2) | copy-start | bytes 7077892
  61.1 3.1 %copy-start.5 = (bf16[3072,384]{1,0:T(8,128)(2,1)S(1)}, bf16[3072,384]{1,0:T(8,128)(2,1)}, u32[]{:S(2)}) copy-start(bf16[3072,384]{1,0:T(8,128)(2,1)} %copy-done.4) | copy-start | bytes 7077892
  61.1 3.7 %copy-start.7 = (bf16[3072,384]{1,0:T(8,128)(2,1)S(1)}, bf16[3072,384]{1,0:T(8,128)(2,1)}, u32[]{:S(2)}) copy-start(bf16[3072,384]{1,0:T(8,128)(2,1)} %copy-done.6) | copy-start | bytes 7077892
  61.1 4.4 %copy-start.9 = (bf16[3072,384]{1,0:T(8,128)(2,1)S(1)}, bf16[3072,384]{1,0:T(8,128)(2,1)}, u32[]{:S(2)}) copy-start(bf16[3072,384]{1,0:T(8,128)(2,1)} %copy-done.8) | copy-start | bytes 7077892
  64.1 4.2 %collective-permute-start.11 = (bf16[32,3072]{1,0:T(8,128)(2,1)S(1)}, bf16[32,3072]{1,0:T(8,128)(2,1)S(1)}, u32[]{:S(2)}, u32[]{:S(2)}) collective-permute-start(bf16[32,3072]{1,0:T(8,128)(2,1)S(1)} %up_other.3.refs_9_), channel_id=1, source_target_pairs={{0,1},{1,0},{2,3},{3,2},{4,5},{5,4},{6,7},{7,6},{8,9},{9,8},{10,11... | collective-permute-start | bytes 589832 | tf_op jit(solution)/shard_map/ppermute | solution.py:38
  68.4 7.6 %copy-start.11 = (bf16[3072,384]{1,0:T(8,128)(2,1)S(1)}, bf16[3072,384]{1,0:T(8,128)(2,1)}, u32[]{:S(2)}) copy-start(bf16[3072,384]{1,0:T(8,128)(2,1)} %copy-done.10) | copy-start | bytes 7077892
  68.4 7.4 %collective-permute-start.12 = (bf16[32,3072]{1,0:T(8,128)(2,1)S(1)}, bf16[32,3072]{1,0:T(8,128)(2,1)S(1)}, u32[]{:S(2)}, u32[]{:S(2)}) collective-permute-start(bf16[32,3072]{1,0:T(8,128)(2,1)S(1)} %add_convert_fusion.refs_0_), channel_id=1, source_target_pairs={{0,2},{1,3},{2,0},{3,1},{4,6},{5,7},{6,4},{7,5},{8,10},{9,11},{10,... | collective-permute-start | bytes 589832 | tf_op jit(solution)/shard_map/ppermute | solution.py:38
  76.0 2.9 %collective-permute-start.13 = (bf16[32,3072]{1,0:T(8,128)(2,1)S(1)}, bf16[32,3072]{1,0:T(8,128)(2,1)S(1)}, u32[]{:S(2)}, u32[]{:S(2)}) collective-permute-start(bf16[32,3072]{1,0:T(8,128)(2,1)S(1)} %fusion.15.refs_0_), channel_id=1, source_target_pairs={{0,1},{1,0},{2,3},{3,2},{4,5},{5,4},{6,7},{7,6},{8,9},{9,8},{10,11... | collective-permute-start | bytes 589832 | tf_op jit(solution)/shard_map/ppermute | solution.py:38
  81.8 6.5 %collective-permute-start.14 = (bf16[8,3072]{1,0:T(8,128)(2,1)S(1)}, bf16[8,3072]{1,0:T(8,128)(2,1)S(1)}, u32[]{:S(2)}, u32[]{:S(2)}) collective-permute-start(bf16[8,3072]{1,0:T(8,128)(2,1)S(1)} %get-tuple-element.117), channel_id=1, source_target_pairs={{0,12},{4,8},{8,4},{12,0},{1,13},{5,9},{9,5},{13,1},{2,14},{6,10},... | collective-permute-start | bytes 147464 | tf_op jit(solution)/shard_map/ppermute | solution.py:38
  83.0 6.0 %collective-permute-start.16 = (bf16[8,3072]{1,0:T(8,128)(2,1)S(1)}, bf16[8,3072]{1,0:T(8,128)(2,1)S(1)}, u32[]{:S(2)}, u32[]{:S(2)}) collective-permute-start(bf16[8,3072]{1,0:T(8,128)(2,1)S(1)} %get-tuple-element.118), channel_id=1, source_target_pairs={{0,4},{4,0},{8,12},{12,8},{1,5},{5,1},{9,13},{13,9},{2,6},{6,2},{1... | collective-permute-start | bytes 147464 | tf_op jit(solution)/shard_map/ppermute | solution.py:38
  83.0 7.0 %collective-permute-start.15 = (bf16[8,3072]{1,0:T(8,128)(2,1)S(1)}, bf16[8,3072]{1,0:T(8,128)(2,1)S(1)}, u32[]{:S(2)}, u32[]{:S(2)}) collective-permute-start(bf16[8,3072]{1,0:T(8,128)(2,1)S(1)} %get-tuple-element.119), channel_id=1, source_target_pairs={{0,8},{4,12},{8,0},{12,4},{1,9},{5,13},{9,1},{13,5},{2,10},{6,14},... | collective-permute-start | bytes 147464 | tf_op jit(solution)/shard_map/ppermute | solution.py:38

commit v5 on v4

--- a/solution.py
+++ b/solution.py
@@ -7,8 +7,7 @@
 
 STEPS = 2
 BLOCKS = 8
-EARLY = 4
-WITH_UP = 4
+HALF = BLOCKS // 2
 bf16, f32 = jnp.bfloat16, jnp.float32
 
 
@@ -97,7 +96,7 @@
         out_specs=[vmem] * len(shapes),
         input_output_aliases={n_g + n_a + len(behind) + i: len(shapes) - n_l + i for i in range(len(over))},
         scratch_shapes=[pltpu.SemaphoreType.DMA((n_l,))] if loads else [],
-        compiler_params=pltpu.CompilerParams(vmem_limit_bytes=2 * 2**20),
+        compiler_params=pltpu.CompilerParams(vmem_limit_bytes=2**19),
         cost_estimate=pl.CostEstimate(flops=1000, bytes_accessed=1000, transcendentals=0),
         name=name,
     )(*given, *[pltpu.with_memory_space_constraint(load[0], pltpu.HBM) for load in loads], *behind, *over)
@@ -129,31 +128,35 @@
 
     state = tokens
     x, other_in = rows_of(state)
+    low, high = slice(0, HALF), slice(HALF, BLOCKS)
     for step in range(STEPS):
         first, last = step == 0, step + 1 == STEPS
-        sent, got = stage([(x, other_in)], [load(w_in, 1, 1)] if first else [], "up_other")
-        mine_in = got if first else mine_in
-        kept, got = stage([(x, mine_in)], [load(w_out, 0, 1, 0, WITH_UP)] if first else [], "up_mine", [sent])
-        mine_out = got if first else mine_out
+        if first:
+            sent, mine_in = stage([(x, other_in)], [load(w_in, 1, 1)], "up_other")
+            kept, kept_out = stage([(x, mine_in)], [load(w_out, 0, 1, 0, HALF)], "up_mine", [sent])
+        else:
+            sent, got = stage([(x, other_in)], [load(w_in, 1, 1, 0, HALF)], "up_other", over=mine_out[high])
+            mine_in = got + mine_in[high]
+            kept, _ = stage([(x, mine_in)], [], "up_mine", [sent])
         chip = (kept.astype(f32) + swap(sent, "width", nw, 1).astype(f32)).astype(bf16)
         across = swap(chip, "width", nw, 2)
-        begun = WITH_UP if first else BLOCKS
-        wanted = [load(w_out, 0, 1, begun, BLOCKS)] * (begun < BLOCKS) + [load(w_out, 0, -1, 0, begun)]
-        chip, got = stage([], wanted, "load_out", carry=chip, over=other_in)
-        mine_out, other_out = mine_out + got[: BLOCKS - begun], got[BLOCKS - begun :]
+        wanted = [load(w_out, 0, 1, HALF, BLOCKS), load(w_out, 0, -1, 0, HALF)]
+        chip, got = stage([], wanted, "load_out", carry=chip, over=mine_in[low] + other_in[low])
+        mine_out, other_out = kept_out + got[low], got[high]
         total = chip.astype(f32) + across.astype(f32)
         mine = jax.nn.gelu(total, approximate=True).astype(bf16)
         other = swap(mine, "width", nw, 1)
-        part, got = stage([(mine, mine_out)], [load(w_out, 0, -1, begun, BLOCKS)] if first else [], "down_mine", [], None, f32)
-        part, _ = stage([(other, other_out + got)], [], "down_other", [], part)
+        wanted = [load(w_out, 0, -1, HALF, BLOCKS)]
+        part, got = stage([(mine, mine_out)], wanted, "down_mine", [], None, f32, over=other_in[high])
         other_out = other_out + got
+        part, _ = stage([(other, other_out)], [], "down_other", [], part)
         if last:
             state = scattered(part, state, part[:rows].astype(f32))
         else:
-            half = [load(w_in, 1, -1, 0, EARLY)], [load(w_in, 1, -1, EARLY, BLOCKS)]
-            old, got = stage([], half[0], "load_other_in", [part], carry=state, over=other_out[:EARLY])
+            early, late = [load(w_in, 1, -1, 0, HALF)], [load(w_in, 1, -1, HALF, BLOCKS)]
+            old, got = stage([], early, "load_other_in", [part], carry=state, over=other_out[low])
             state = scattered(part, old, part[:rows].astype(f32))
-            other_in = got + stage([], half[1], "load_other_in", [state], over=other_out[EARLY:])[0]
+            other_in = got + stage([], late, "load_other_in", [state], over=other_out[high])[0]
             x = gather(state, nz)
     return state
 

time: 90.8 us -> 88.5 us (0.975)
  Pallas kernels: 61.4 us -> 60.3 us
  local copies, waits for them, and re-layouts: 2.2 us -> 1.27 us
    pallas_call x14, Pallas kernels: 61.4 us -> 60.3 us  [stage(): pl.pallas_call(kernel, out_shape=shapes, in_specs=[vmem] * n_g + [hbm] *...]
    unnamed x28 -> x8, local copies, waits for them, and re-layouts: 2.16 us -> 1.23 us
  transfers between devices with their start and end apart: 17 -> 17, of which waited for: 3 -> 3; matrix products, arithmetic and copies ran while one was open for 0% -> 0% of each run, Pallas kernels for 51% -> 50%
where the time goes in v5:
time: 88.5 us; the launch traced here: 88.3 us
  Pallas kernels  60.3 us (68%)
  starting transfers between devices  21.5 us (24%)
  waiting for transfers between devices  3.73 us (4%)
  local copies, waits for them, and re-layouts  1.27 us (1%)
  other arithmetic  1.17 us (1%)
    pallas_call x14, Pallas kernels, stage(): pl.pallas_call(kernel, out_shape=shapes, in_specs=[vmem] * n_g + [hbm] *...  60.3 us
    ppermute x17, starting transfers between devices, swap(): return lax.ppermute(x, axis, [(i, i ^ mask) for i in range(n)])  21.5 us
    ppermute x17, waiting for transfers between devices, swap(): return lax.ppermute(x, axis, [(i, i ^ mask) for i in range(n)])  3.73 us
  transfers between devices with their start and end apart: 17, of which 3 were waited for; matrix products, arithmetic and copies ran while one was open for 0% of the time, Pallas kernels for 50%

profile of v5, /device:TPU:0, one launch (start us, length us, event | category | flops | bytes accessed | tf_op | source)
XLA Modules:
  0.0 88.3 jit_solution(13395393666866872691)
XLA Ops:
  0.0 4.0 %collective-permute-start = (bf16[8,3072]{1,0:T(8,128)(2,1)}, bf16[8,3072]{1,0:T(8,128)(2,1)S(1)}, u32[]{:S(2)}, u32[]{:S(2)}) collective-permute-start(bf16[8,3072]{1,0:T(8,128)(2,1)} %refs_0_.4), channel_id=1, source_target_pairs={{0,8},{4,12},{8,0},{12,4},{1,9},{5,13},{9,1},{13,5},{2,10},{6,14},... | collective-permute-start | bytes 147464 | tf_op jit(solution)/shard_map/ppermute | solution.py:37
  4.0 0.8 copy-done.2
  4.9 3.8 %load_other_in.4 = (bf16[8,3072]{1,0:T(8,128)(2,1)S(1)}, bf16[3072,384]{1,0:T(8,128)(2,1)S(1)}, bf16[3072,384]{1,0:T(8,128)(2,1)S(1)}, bf16[3072,384]{1,0:T(8,128)(2,1)S(1)}, bf16[3072,384]{1,0:T(8,128)(2,1)S(1)}) custom-call(bf16[8,3072]{1,0:T(8,128)(2,1)S(1)} %copy-done.2, bf16[3072,6144]{1,0:T(8,128)(2,1)} %refs_9_.8), custom_call_target="tpu_custom_call" | custom-call | flops 1000 | bytes 1000 | tf_op jit(solution)/shard_map/load_other_in/pallas_call | solution.py:92
  8.7 0.0 collective-permute-done.refs_2_
  8.8 1.6 %collective-permute-start.1 = (bf16[16,3072]{1,0:T(8,128)(2,1)S(1)}, bf16[16,3072]{1,0:T(8,128)(2,1)S(1)}, u32[]{:S(2)}, u32[]{:S(2)}) collective-permute-start(bf16[16,3072]{1,0:T(8,128)(2,1)S(1)} %pad_maximum_fusion.2), channel_id=1, source_target_pairs={{0,4},{4,0},{8,12},{12,8},{1,5},{5,1},{9,13},{13,9},{2,6},{6,2},{1... | collective-permute-start | bytes 294920 | tf_op jit(solution)/shard_map/ppermute | solution.py:37
  10.4 3.8 %load_other_in.5 = (bf16[8,3072]{1,0:T(8,128)(2,1)S(1)}, bf16[3072,384]{1,0:T(8,128)(2,1)S(1)}, bf16[3072,384]{1,0:T(8,128)(2,1)S(1)}, bf16[3072,384]{1,0:T(8,128)(2,1)S(1)}, bf16[3072,384]{1,0:T(8,128)(2,1)S(1)}) custom-call(bf16[8,3072]{1,0:T(8,128)(2,1)S(1)} %get-tuple-element.71.refs_0_, bf16[3072,6144]{1,0:T(8,128)(2,1)} %refs_9_.8, ...), custom_call_target="tpu_custom_call" | custom-call | flops 1000 | bytes 1000 | tf_op jit(solution)/shard_map/load_other_in/pallas_call | solution.py:92
  14.3 0.0 collective-permute-done.1
  14.3 6.7 %up_other.2 = (bf16[32,3072]{1,0:T(8,128)(2,1)S(1)}, bf16[3072,384]{1,0:T(8,128)(2,1)S(1)}, bf16[3072,384]{1,0:T(8,128)(2,1)S(1)}, bf16[3072,384]{1,0:T(8,128)(2...) custom-call(bf16[32,3072]{1,0:T(8,128)(2,1)S(1)} %pad_maximum_fusion, ...), custom_call_target="tpu_custom_call" | custom-call | flops 1000 | bytes 1000 | tf_op jit(solution)/shard_map/up_other/pallas_call | solution.py:92
  21.0 0.1 collective-permute-start.2
  21.1 4.6 %up_mine.2 = (bf16[32,3072]{1,0:T(8,128)(2,1)S(1)}, bf16[3072,384]{1,0:T(8,128)(2,1)S(1)}, bf16[3072,384]{1,0:T(8,128)(2,1)S(1)}, bf16[3072,384]{1,0:T(8,128)(2,1)S(1)}, bf16[3072,384]{1,0:T(8,128)(2,1)S(1)}) custom-call(bf16[32,3072]{1,0:T(8,128)(2,1)S(1)} %pad_maximum_fusion.refs_0_, bf16[3072,384]{1,0:T(8,128)(2,1)S(1)} %get-tuple-element.81.refs_1_.refs_3_, ...), custom_call_target="tpu_custom_call" | custom-call | flops 1000 | bytes 1000 | tf_op jit(solution)/shard_map/up_mine/pallas_call | solution.py:92
  25.8 1.6 %collective-permute-start.3 = (bf16[32,3072]{1,0:T(8,128)(2,1)S(1)}, bf16[32,3072]{1,0:T(8,128)(2,1)S(1)}, u32[]{:S(2)}, u32[]{:S(2)}) collective-permute-start(bf16[32,3072]{1,0:T(8,128)(2,1)S(1)} %add_convert_fusion.1.refs_0_), channel_id=1, source_target_pairs={{0,2},{1,3},{2,0},{3,1},{4,6},{5,7},{6,4},{7,5},{8,10},{9,11},{10,... | collective-permute-start | bytes 589832 | tf_op jit(solution)/shard_map/ppermute | solution.py:37
  27.3 6.6 %load_out.2 = (bf16[32,3072]{1,0:T(8,128)(2,1)S(1)}, bf16[3072,384]{1,0:T(8,128)(2,1)S(1)}, bf16[3072,384]{1,0:T(8,128)(2,1)S(1)}, bf16[3072,384]{1,0:T(8,128)(2...) custom-call(bf16[32,3072]{1,0:T(8,128)(2,1)S(1)} %add_convert_fusion, ...), custom_call_target="tpu_custom_call", output_to_operand_aliasing={{1}: (3, {}), {2}: (4, {}), {3}: (5, {}), {4}: (6, {}), {5}... | custom-call | flops 1000 | bytes 1000 | tf_op jit(solution)/shard_map/load_out/pallas_call | solution.py:92
  34.0 0.0 collective-permute-done.3
  34.0 0.2 fusion.7.refs_0_
  34.2 0.1 collective-permute-start.4
  34.2 3.9 %down_mine.2 = (f32[32,3072]{1,0:T(8,128)S(1)}, bf16[3072,384]{1,0:T(8,128)(2,1)S(1)}, bf16[3072,384]{1,0:T(8,128)(2,1)S(1)}, bf16[3072,384]{1,0:T(8,128)(2,1)S(1)}, bf16[3072,384]{1,0:T(8,128)(2,1)S(1)}) custom-call(bf16[32,3072]{1,0:T(8,128)(2,1)S(1)} %fusion.7.refs_0_, ...), custom_call_target="tpu_custom_call", output_to_operand_aliasing={{1}: (10, {}), {2}: (11, {}), {3}: (12, {}), {4}: (13, {})} | custom-call | flops 1000 | bytes 1000 | tf_op jit(solution)/shard_map/down_mine/pallas_call | solution.py:92
  38.1 0.0 collective-permute-done.4.refs_0_
  38.1 0.0 copy-start.3
  38.1 2.9 %down_other.2.refs_2_ = bf16[32,3072]{1,0:T(8,128)(2,1)S(1)} custom-call(bf16[32,3072]{1,0:T(8,128)(2,1)S(1)} %collective-permute-done.4.refs_0_, bf16[3072,384]{1,0:T(8,128)(2,1)S(1)} %get-tuple-element.92.refs_1_.refs_3_, bf16[3072,384]{1,0:T(8,128)(2,1)S(1)} %get-tuple-element.93.refs_2_.refs_4_, bf16[3072,384]{1,0:T(8,128)(2,1)S(1)} %get-tuple-element.94.refs_3_.refs_5_, ...), custom_call_target="tpu_custom_call" | custom-call | flops 1000 | bytes 1000 | tf_op jit(solution)/shard_map/down_other/pallas_call | solution.py:92
  41.0 1.1 %collective-permute-start.5 = (bf16[8,3072]{1,0:T(8,128)(2,1)S(1)}, bf16[8,3072]{1,0:T(8,128)(2,1)S(1)}, u32[]{:S(2)}, u32[]{:S(2)}) collective-permute-start(bf16[8,3072]{1,0:T(8,128)(2,1)S(1)} %get-tuple-element.140), channel_id=1, source_target_pairs={{0,12},{4,8},{8,4},{12,0},{1,13},{5,9},{9,5},{13,1},{2,14},{6,10},... | collective-permute-start | bytes 147464 | tf_op jit(solution)/shard_map/ppermute | solution.py:37
  42.2 0.4 collective-permute-start.7
  42.6 2.9 %collective-permute-start.6 = (bf16[8,3072]{1,0:T(8,128)(2,1)S(1)}, bf16[8,3072]{1,0:T(8,128)(2,1)S(1)}, u32[]{:S(2)}, u32[]{:S(2)}) collective-permute-start(bf16[8,3072]{1,0:T(8,128)(2,1)S(1)} %get-tuple-element.142), channel_id=1, source_target_pairs={{0,8},{4,12},{8,0},{12,4},{1,9},{5,13},{9,1},{13,5},{2,10},{6,14},... | collective-permute-start | bytes 147464 | tf_op jit(solution)/shard_map/ppermute | solution.py:37
  45.5 3.9 %load_other_in.6 = (bf16[8,3072]{1,0:T(8,128)(2,1)S(1)}, bf16[3072,384]{1,0:T(8,128)(2,1)S(1)}, bf16[3072,384]{1,0:T(8,128)(2,1)S(1)}, bf16[3072,384]{1,0:T(8,128)(2,1)S(1)}, bf16[3072,384]{1,0:T(8,128)(2,1)S(1)}) custom-call(bf16[8,3072]{1,0:T(8,128)(2,1)S(1)} %copy-done.3, ...), custom_call_target="tpu_custom_call", output_to_operand_aliasing={{1}: (3, {}), {2}: (4, {}), {3}: (5, {}), {4}: (6, {})} | custom-call | flops 1000 | bytes 1000 | tf_op jit(solution)/shard_map/load_other_in/pallas_call | solution.py:92
  49.3 0.0 collective-permute-done.5
  49.4 0.0 collective-permute-done.7
  49.4 1.1 %collective-permute-start.10 = (bf16[8,3072]{1,0:T(8,128)(2,1)S(1)}, bf16[8,3072]{1,0:T(8,128)(2,1)S(1)}, u32[]{:S(2)}, u32[]{:S(2)}) collective-permute-start(bf16[8,3072]{1,0:T(8,128)(2,1)S(1)} %add_convert_fusion.3.refs_1_), channel_id=1, source_target_pairs={{0,12},{4,8},{8,4},{12,0},{1,13},{5,9},{9,5},{13,1},{2,14},{6,10},... | collective-permute-start | bytes 147464 | tf_op jit(solution)/shard_map/ppermute | solution.py:37
  50.6 0.7 collective-permute-start.9
  51.3 2.6 %collective-permute-start.8 = (bf16[8,3072]{1,0:T(8,128)(2,1)S(1)}, bf16[8,3072]{1,0:T(8,128)(2,1)S(1)}, u32[]{:S(2)}, u32[]{:S(2)}) collective-permute-start(bf16[8,3072]{1,0:T(8,128)(2,1)S(1)} %add_convert_fusion.3.refs_1_), channel_id=1, source_target_pairs={{0,4},{4,0},{8,12},{12,8},{1,5},{5,1},{9,13},{13,9},{2,6},{6,2},{1... | collective-permute-start | bytes 147464 | tf_op jit(solution)/shard_map/ppermute | solution.py:37
  53.9 3.8 %load_other_in.7 = (bf16[3072,384]{1,0:T(8,128)(2,1)S(1)}, bf16[3072,384]{1,0:T(8,128)(2,1)S(1)}, bf16[3072,384]{1,0:T(8,128)(2,1)S(1)}, bf16[3072,384]{1,0:T(8,128)(2,1)S(1)}) custom-call(bf16[3072,6144]{1,0:T(8,128)(2,1)} %refs_9_.8, ...), custom_call_target="tpu_custom_call", output_to_operand_aliasing={{0}: (2, {}), {1}: (3, {}), {2}: (4, {}), {3}: (5, {})} | custom-call | flops 1000 | bytes 1000 | tf_op jit(solution)/shard_map/load_other_in/pallas_call | solution.py:92
  57.7 0.0 collective-permute-done.10
  57.8 4.0 %up_other.3 = (bf16[32,3072]{1,0:T(8,128)(2,1)S(1)}, bf16[3072,384]{1,0:T(8,128)(2,1)S(1)}, bf16[3072,384]{1,0:T(8,128)(2,1)S(1)}, bf16[3072,384]{1,0:T(8,128)(2,1)S(1)}, bf16[3072,384]{1,0:T(8,128)(2,1)S(1)}) custom-call(bf16[32,3072]{1,0:T(8,128)(2,1)S(1)} %pad_maximum_fusion.1.refs_0_,, ...), custom_call_target="tpu_custom_call", output_to_operand_aliasing={{1}: (10, {}), {2}: (11, {}), {3}: (12, {}), {4}: (13, {})} | custom-call | flops 1000 | bytes 1000 | tf_op jit(solution)/shard_map/up_other/pallas_call | solution.py:92
  61.8 0.1 collective-permute-start.11
  61.9 0.4 copy-done.1
  62.3 2.8 %up_mine.3 = bf16[32,3072]{1,0:T(8,128)(2,1)S(1)} custom-call(bf16[32,3072]{1,0:T(8,128)(2,1)S(1)} %pad_maximum_fusion.1.refs_0_, bf16[3072,384]{1,0:T(8,128)(2,1)S(1)} %get-tuple-element.118.refs_1_.refs_3_, bf16[3072,384]{1,0:T(8,128)(2,1)S(1)} %get-tuple-element.119.refs_2_.refs_4_, bf16[3072,384]{1,0:T(8,128)(2,1)S(1)} %get-tuple-element.120.refs_3_.refs_5_, ...), custom_call_target="tpu_custom_call" | custom-call | flops 1000 | bytes 1000 | tf_op jit(solution)/shard_map/up_mine/pallas_call | solution.py:92
  65.1 0.0 collective-permute-done.11
  65.1 0.1 add_convert_fusion.refs_0_
  65.2 0.6 collective-permute-start.12
  65.8 6.6 %load_out.3 = (bf16[32,3072]{1,0:T(8,128)(2,1)S(1)}, bf16[3072,384]{1,0:T(8,128)(2,1)S(1)}, bf16[3072,384]{1,0:T(8,128)(2,1)S(1)}, bf16[3072,384]{1,0:T(8,128)(2...) custom-call(bf16[32,3072]{1,0:T(8,128)(2,1)S(1)} %add_convert_fusion, ...), custom_call_target="tpu_custom_call", output_to_operand_aliasing={{1}: (3, {}), {2}: (4, {}), {3}: (5, {}), {4}: (6, {}), {5}... | custom-call | flops 1000 | bytes 1000 | tf_op jit(solution)/shard_map/load_out/pallas_call | solution.py:92
  72.5 0.2 fusion.15.refs_0_
  72.6 0.1 collective-permute-start.13
  72.7 3.9 %down_mine.3 = (f32[32,3072]{1,0:T(8,128)S(1)}, bf16[3072,384]{1,0:T(8,128)(2,1)S(1)}, bf16[3072,384]{1,0:T(8,128)(2,1)S(1)}, bf16[3072,384]{1,0:T(8,128)(2,1)S(1)}, bf16[3072,384]{1,0:T(8,128)(2,1)S(1)}) custom-call(bf16[32,3072]{1,0:T(8,128)(2,1)S(1)} %fusion.15.refs_0_, ...), custom_call_target="tpu_custom_call", output_to_operand_aliasing={{1}: (10, {}), {2}: (11, {}), {3}: (12, {}), {4}: (13, {})} | custom-call | flops 1000 | bytes 1000 | tf_op jit(solution)/shard_map/down_mine/pallas_call | solution.py:92
  76.6 2.9 %down_other.3 = bf16[32,3072]{1,0:T(8,128)(2,1)S(1)} custom-call(bf16[32,3072]{1,0:T(8,128)(2,1)S(1)} %collective-permute-done.13.refs_0_, bf16[3072,384]{1,0:T(8,128)(2,1)S(1)} %get-tuple-element.124.refs_1_, bf16[3072,384]{1,0:T(8,128)(2,1)S(1)} %get-tuple-element.125.refs_2_, bf16[3072,384]{1,0:T(8,128)(2,1)S(1)} %get-tuple-element.126.refs_3_, ...), custom_call_target="tpu_custom_call" | custom-call | flops 1000 | bytes 1000 | tf_op jit(solution)/shard_map/down_other/pallas_call | solution.py:92
  79.5 1.1 %collective-permute-start.14 = (bf16[8,3072]{1,0:T(8,128)(2,1)S(1)}, bf16[8,3072]{1,0:T(8,128)(2,1)S(1)}, u32[]{:S(2)}, u32[]{:S(2)}) collective-permute-start(bf16[8,3072]{1,0:T(8,128)(2,1)S(1)} %get-tuple-element.137), channel_id=1, source_target_pairs={{0,12},{4,8},{8,4},{12,0},{1,13},{5,9},{9,5},{13,1},{2,14},{6,10},... | collective-permute-start | bytes 147464 | tf_op jit(solution)/shard_map/ppermute | solution.py:37
  80.7 3.3 %collective-permute-start.15 = (bf16[8,3072]{1,0:T(8,128)(2,1)S(1)}, bf16[8,3072]{1,0:T(8,128)(2,1)S(1)}, u32[]{:S(2)}, u32[]{:S(2)}) collective-permute-start(bf16[8,3072]{1,0:T(8,128)(2,1)S(1)} %get-tuple-element.139), channel_id=1, source_target_pairs={{0,8},{4,12},{8,0},{12,4},{1,9},{5,13},{9,1},{13,5},{2,10},{6,14},... | collective-permute-start | bytes 147464 | tf_op jit(solution)/shard_map/ppermute | solution.py:37
  84.0 2.0 %collective-permute-done.14 = bf16[8,3072]{1,0:T(8,128)(2,1)S(1)} collective-permute-done((bf16[8,3072]{1,0:T(8,128)(2,1)S(1)}, bf16[8,3072]{1,0:T(8,128)(2,1)S(1)}, u32[]{:S(2)}, u32[]{:S(2)}) %collective-permute-start.14) | collective-permute-done | bytes 49184 | tf_op jit(solution)/shard_map/ppermute | solution.py:37
  86.0 0.7 collective-permute-done.16
  86.6 1.0 %collective-permute-done.15 = bf16[8,3072]{1,0:T(8,128)(2,1)S(1)} collective-permute-done((bf16[8,3072]{1,0:T(8,128)(2,1)S(1)}, bf16[8,3072]{1,0:T(8,128)(2,1)S(1)}, u32[]{:S(2)}, u32[]{:S(2)}) %collective-permute-start.15) | collective-permute-done | bytes 49184 | tf_op jit(solution)/shard_map/ppermute | solution.py:37
  87.6 0.7 add_convert_fusion.2
  (20 shorter events, 0.2 us)
Async XLA Ops:
  0.0 8.7 %collective-permute-start = (bf16[8,3072]{1,0:T(8,128)(2,1)}, bf16[8,3072]{1,0:T(8,128)(2,1)S(1)}, u32[]{:S(2)}, u32[]{:S(2)}) collective-permute-start(bf16[8,3072]{1,0:T(8,128)(2,1)} %refs_0_.4), channel_id=1, source_target_pairs={{0,8},{4,12},{8,0},{12,4},{1,9},{5,13},{9,1},{13,5},{2,10},{6,14},... | collective-permute-start | bytes 147464 | tf_op jit(solution)/shard_map/ppermute | solution.py:37
  4.0 0.8 copy-start.2
  8.8 5.5 %collective-permute-start.1 = (bf16[16,3072]{1,0:T(8,128)(2,1)S(1)}, bf16[16,3072]{1,0:T(8,128)(2,1)S(1)}, u32[]{:S(2)}, u32[]{:S(2)}) collective-permute-start(bf16[16,3072]{1,0:T(8,128)(2,1)S(1)} %pad_maximum_fusion.2), channel_id=1, source_target_pairs={{0,4},{4,0},{8,12},{12,8},{1,5},{5,1},{9,13},{13,9},{2,6},{6,2},{1... | collective-permute-start | bytes 294920 | tf_op jit(solution)/shard_map/ppermute | solution.py:37
  21.0 4.7 %copy-start = (bf16[3072,384]{1,0:T(8,128)(2,1)}, bf16[3072,384]{1,0:T(8,128)(2,1)S(1)}, u32[]{:S(2)}) copy-start(bf16[3072,384]{1,0:T(8,128)(2,1)S(1)} %get-tuple-element.85.refs_5_) | copy-start | bytes 7077892
  21.0 4.7 %collective-permute-start.2 = (bf16[32,3072]{1,0:T(8,128)(2,1)S(1)}, bf16[32,3072]{1,0:T(8,128)(2,1)S(1)}, u32[]{:S(2)}, u32[]{:S(2)}) collective-permute-start(bf16[32,3072]{1,0:T(8,128)(2,1)S(1)} %get-tuple-element.89.refs_10_), channel_id=1, source_target_pairs={{0,1},{1,0},{2,3},{3,2},{4,5},{5,4},{6,7},{7,6},{8,9},{9,8},{10,11... | collective-permute-start | bytes 589832 | tf_op jit(solution)/shard_map/ppermute | solution.py:37
  25.8 8.2 %collective-permute-start.3 = (bf16[32,3072]{1,0:T(8,128)(2,1)S(1)}, bf16[32,3072]{1,0:T(8,128)(2,1)S(1)}, u32[]{:S(2)}, u32[]{:S(2)}) collective-permute-start(bf16[32,3072]{1,0:T(8,128)(2,1)S(1)} %add_convert_fusion.1.refs_0_), channel_id=1, source_target_pairs={{0,2},{1,3},{2,0},{3,1},{4,6},{5,7},{6,4},{7,5},{8,10},{9,11},{10,... | collective-permute-start | bytes 589832 | tf_op jit(solution)/shard_map/ppermute | solution.py:37
  34.2 4.0 %collective-permute-start.4 = (bf16[32,3072]{1,0:T(8,128)(2,1)S(1)}, bf16[32,3072]{1,0:T(8,128)(2,1)S(1)}, u32[]{:S(2)}, u32[]{:S(2)}) collective-permute-start(bf16[32,3072]{1,0:T(8,128)(2,1)S(1)} %fusion.7.refs_0_), channel_id=1, source_target_pairs={{0,1},{1,0},{2,3},{3,2},{4,5},{5,4},{6,7},{7,6},{8,9},{9,8},{10,11... | collective-permute-start | bytes 589832 | tf_op jit(solution)/shard_map/ppermute | solution.py:37
  38.1 7.4 %copy-start.3 = (bf16[8,3072]{1,0:T(8,128)(2,1)S(1)}, bf16[8,3072]{1,0:T(8,128)(2,1)}, u32[]{:S(2)}) copy-start(bf16[8,3072]{1,0:T(8,128)(2,1)} %refs_0_.4) | copy-start | bytes 147460
  41.0 8.3 %collective-permute-start.5 = (bf16[8,3072]{1,0:T(8,128)(2,1)S(1)}, bf16[8,3072]{1,0:T(8,128)(2,1)S(1)}, u32[]{:S(2)}, u32[]{:S(2)}) collective-permute-start(bf16[8,3072]{1,0:T(8,128)(2,1)S(1)} %get-tuple-element.140), channel_id=1, source_target_pairs={{0,12},{4,8},{8,4},{12,0},{1,13},{5,9},{9,5},{13,1},{2,14},{6,10},... | collective-permute-start | bytes 147464 | tf_op jit(solution)/shard_map/ppermute | solution.py:37
  42.2 7.2 %collective-permute-start.7 = (bf16[8,3072]{1,0:T(8,128)(2,1)S(1)}, bf16[8,3072]{1,0:T(8,128)(2,1)S(1)}, u32[]{:S(2)}, u32[]{:S(2)}) collective-permute-start(bf16[8,3072]{1,0:T(8,128)(2,1)S(1)} %get-tuple-element.141), channel_id=1, source_target_pairs={{0,4},{4,0},{8,12},{12,8},{1,5},{5,1},{9,13},{13,9},{2,6},{6,2},{1... | collective-permute-start | bytes 147464 | tf_op jit(solution)/shard_map/ppermute | solution.py:37
  42.6 6.8 %collective-permute-start.6 = (bf16[8,3072]{1,0:T(8,128)(2,1)S(1)}, bf16[8,3072]{1,0:T(8,128)(2,1)S(1)}, u32[]{:S(2)}, u32[]{:S(2)}) collective-permute-start(bf16[8,3072]{1,0:T(8,128)(2,1)S(1)} %get-tuple-element.142), channel_id=1, source_target_pairs={{0,8},{4,12},{8,0},{12,4},{1,9},{5,13},{9,1},{13,5},{2,10},{6,14},... | collective-permute-start | bytes 147464 | tf_op jit(solution)/shard_map/ppermute | solution.py:37
  49.4 8.3 %collective-permute-start.10 = (bf16[8,3072]{1,0:T(8,128)(2,1)S(1)}, bf16[8,3072]{1,0:T(8,128)(2,1)S(1)}, u32[]{:S(2)}, u32[]{:S(2)}) collective-permute-start(bf16[8,3072]{1,0:T(8,128)(2,1)S(1)} %add_convert_fusion.3.refs_1_), channel_id=1, source_target_pairs={{0,12},{4,8},{8,4},{12,0},{1,13},{5,9},{9,5},{13,1},{2,14},{6,10},... | collective-permute-start | bytes 147464 | tf_op jit(solution)/shard_map/ppermute | solution.py:37
  50.6 7.2 %collective-permute-start.9 = (bf16[8,3072]{1,0:T(8,128)(2,1)S(1)}, bf16[8,3072]{1,0:T(8,128)(2,1)S(1)}, u32[]{:S(2)}, u32[]{:S(2)}) collective-permute-start(bf16[8,3072]{1,0:T(8,128)(2,1)S(1)} %add_convert_fusion.3.refs_1_), channel_id=1, source_target_pairs={{0,8},{4,12},{8,0},{12,4},{1,9},{5,13},{9,1},{13,5},{2,10},{6,14},... | collective-permute-start | bytes 147464 | tf_op jit(solution)/shard_map/ppermute | solution.py:37
  51.3 6.5 %collective-permute-start.8 = (bf16[8,3072]{1,0:T(8,128)(2,1)S(1)}, bf16[8,3072]{1,0:T(8,128)(2,1)S(1)}, u32[]{:S(2)}, u32[]{:S(2)}) collective-permute-start(bf16[8,3072]{1,0:T(8,128)(2,1)S(1)} %add_convert_fusion.3.refs_1_), channel_id=1, source_target_pairs={{0,4},{4,0},{8,12},{12,8},{1,5},{5,1},{9,13},{13,9},{2,6},{6,2},{1... | collective-permute-start | bytes 147464 | tf_op jit(solution)/shard_map/ppermute | solution.py:37
  57.8 4.5 %copy-start.1 = (bf16[3072,384]{1,0:T(8,128)(2,1)S(1)}, bf16[3072,384]{1,0:T(8,128)(2,1)}, u32[]{:S(2)}) copy-start(bf16[3072,384]{1,0:T(8,128)(2,1)} %copy-done) | copy-start | bytes 7077892
  61.8 3.3 %collective-permute-start.11 = (bf16[32,3072]{1,0:T(8,128)(2,1)S(1)}, bf16[32,3072]{1,0:T(8,128)(2,1)S(1)}, u32[]{:S(2)}, u32[]{:S(2)}) collective-permute-start(bf16[32,3072]{1,0:T(8,128)(2,1)S(1)} %get-tuple-element.122.refs_9_), channel_id=1, source_target_pairs={{0,1},{1,0},{2,3},{3,2},{4,5},{5,4},{6,7},{7,6},{8,9},{9,8},{10,11... | collective-permute-start | bytes 589832 | tf_op jit(solution)/shard_map/ppermute | solution.py:37
  65.2 7.3 %collective-permute-start.12 = (bf16[32,3072]{1,0:T(8,128)(2,1)S(1)}, bf16[32,3072]{1,0:T(8,128)(2,1)S(1)}, u32[]{:S(2)}, u32[]{:S(2)}) collective-permute-start(bf16[32,3072]{1,0:T(8,128)(2,1)S(1)} %add_convert_fusion.refs_0_), channel_id=1, source_target_pairs={{0,2},{1,3},{2,0},{3,1},{4,6},{5,7},{6,4},{7,5},{8,10},{9,11},{10,... | collective-permute-start | bytes 589832 | tf_op jit(solution)/shard_map/ppermute | solution.py:37
  72.6 4.0 %collective-permute-start.13 = (bf16[32,3072]{1,0:T(8,128)(2,1)S(1)}, bf16[32,3072]{1,0:T(8,128)(2,1)S(1)}, u32[]{:S(2)}, u32[]{:S(2)}) collective-permute-start(bf16[32,3072]{1,0:T(8,128)(2,1)S(1)} %fusion.15.refs_0_), channel_id=1, source_target_pairs={{0,1},{1,0},{2,3},{3,2},{4,5},{5,4},{6,7},{7,6},{8,9},{9,8},{10,11... | collective-permute-start | bytes 589832 | tf_op jit(solution)/shard_map/ppermute | solution.py:37
  79.5 6.5 %collective-permute-start.14 = (bf16[8,3072]{1,0:T(8,128)(2,1)S(1)}, bf16[8,3072]{1,0:T(8,128)(2,1)S(1)}, u32[]{:S(2)}, u32[]{:S(2)}) collective-permute-start(bf16[8,3072]{1,0:T(8,128)(2,1)S(1)} %get-tuple-element.137), channel_id=1, source_target_pairs={{0,12},{4,8},{8,4},{12,0},{1,13},{5,9},{9,5},{13,1},{2,14},{6,10},... | collective-permute-start | bytes 147464 | tf_op jit(solution)/shard_map/ppermute | solution.py:37
  80.6 6.0 %collective-permute-start.16 = (bf16[8,3072]{1,0:T(8,128)(2,1)S(1)}, bf16[8,3072]{1,0:T(8,128)(2,1)S(1)}, u32[]{:S(2)}, u32[]{:S(2)}) collective-permute-start(bf16[8,3072]{1,0:T(8,128)(2,1)S(1)} %get-tuple-element.138), channel_id=1, source_target_pairs={{0,4},{4,0},{8,12},{12,8},{1,5},{5,1},{9,13},{13,9},{2,6},{6,2},{1... | collective-permute-start | bytes 147464 | tf_op jit(solution)/shard_map/ppermute | solution.py:37
  80.7 7.0 %collective-permute-start.15 = (bf16[8,3072]{1,0:T(8,128)(2,1)S(1)}, bf16[8,3072]{1,0:T(8,128)(2,1)S(1)}, u32[]{:S(2)}, u32[]{:S(2)}) collective-permute-start(bf16[8,3072]{1,0:T(8,128)(2,1)S(1)} %get-tuple-element.139), channel_id=1, source_target_pairs={{0,8},{4,12},{8,0},{12,4},{1,9},{5,13},{9,1},{13,5},{2,10},{6,14},... | collective-permute-start | bytes 147464 | tf_op jit(solution)/shard_map/ppermute | solution.py:37
